TPU v7x, 32 devices: a whole 2x2x4 slice. The times are simulated.
32 devices in a mesh: groups: 2 (over y), ctx: 4 (over z), exp: 4 (over x, core).
Axes of the slice: x: 2, y: 2, z: 4, core: 2. Of those that a mesh axis runs over, the one named last changes fastest.
Arguments:
- resid: bfloat16 [1024, 2048], P(('groups', 'ctx', 'exp')), parts along dimension 0, may hold values from -36 to 36
- query: bfloat16 [1024, 4096], P(('groups', 'ctx'), 'exp'), parts along dimension 0, may hold values from -144 to 144
- key: bfloat16 [1024, 512], P(('groups', 'ctx'), 'exp'), parts along dimension 0, may hold values from -6 to 6
- value: bfloat16 [1024, 512], P(('groups', 'ctx'), 'exp'), parts along dimension 0, may hold values from -6 to 6
- out_proj: bfloat16 [4096, 2048], P('exp', 'ctx'), may hold values from -0.5 to 0.5
- norm_gain: float32 [2048], replicated, may hold values from 0.25 to 1.75
- w_gate: bfloat16 [16, 2048, 384], P(('ctx', 'exp')), may hold values from -0.125 to 0.125
- w_up: bfloat16 [16, 2048, 384], P(('ctx', 'exp')), may hold values from -0.125 to 0.125
- w_down: bfloat16 [16, 384, 2048], P(('ctx', 'exp')), may hold values from -0.3125 to 0.3125
- routes: int32 [1024, 8], P(('groups', 'ctx', 'exp')), parts along dimension 0, may hold values from 0 to 15, all different within a row; in each aligned block of 32 rows (0 to 31, 32 to 63, ...) at most 32 rows name the same one
- gate_weights: float32 [1024, 8], P(('groups', 'ctx', 'exp')), parts along dimension 0, may hold values from 0.05 to 0.25
- grad_out: bfloat16 [1024, 2048], P(('groups', 'ctx', 'exp')), parts along dimension 0, may hold values from -6 to 6
Outputs:
- layer_out: bfloat16 [1024, 2048], P(('groups', 'ctx', 'exp')), parts along dimension 0
- grad_resid: bfloat16 [1024, 2048], P(('groups', 'ctx', 'exp')), parts along dimension 0
- grad_query: bfloat16 [1024, 4096], P(('groups', 'ctx'), 'exp'), parts along dimension 0
- key_gradient: bfloat16 [1024, 512], P(('groups', 'ctx'), 'exp'), parts along dimension 0
- value_gradient: bfloat16 [1024, 512], P(('groups', 'ctx'), 'exp'), parts along dimension 0
- grad_out_proj: bfloat16 [8192, 2048], P(('groups', 'exp'), 'ctx'), parts along dimension 0
- grad_gain: float32 [4096], P('groups'), parts along dimension 0
- grad_w_gate: bfloat16 [32, 2048, 384], P(('groups', 'ctx', 'exp')), parts along dimension 0
- grad_w_up: bfloat16 [32, 2048, 384], P(('groups', 'ctx', 'exp')), parts along dimension 0
- grad_w_down: bfloat16 [32, 384, 2048], P(('groups', 'ctx', 'exp')), parts along dimension 0
There are 2 independent parts, one for each index of `groups`. A program takes and returns all parts, laid end to end along the dimension named above; an argument that names none is the same for every part. Nothing has to cross between parts.
Inputs may be any that keep to these rules, and one draw needn't show every extreme that they name: `routes`: each token names 8 different experts. Among the 32 tokens of one device no expert is named more than 32 times, a bound that some block reaches.
All inputs are finite; a program needn't handle non-finite values.
Results may differ from a plain program's by a relative error of at most 0.018.
Values may be sent and summed in bfloat16 or wider, within the bound.
No kernel may reach another device: no remote copies, remote signals or barrier semaphores. Data moves between devices by JAX's collectives and lax.ppermute only.
A program may use at most 128 MiB of HBM per device.

v0:
```python
import jax
import jax.numpy as jnp
from jax import lax
from jax.sharding import PartitionSpec as P

HEAD_SIZE = 128


EPS = 1e-06
NEG = -1e30


def attend_block(soft_state, queries, key_rows, val_rows, row_begin, query_pos, score_scale):
    peak_run, total_run, accum_rows = soft_state
    scores = (
        jnp.einsum("bngd,knd->bngk", queries, key_rows, preferred_element_type=jnp.float32)
        * score_scale
    )
    key_pos = row_begin + jnp.arange(key_rows.shape[0], dtype=jnp.int32)
    visible = key_pos[None, :] <= query_pos[:, None]
    scores = jnp.where(visible[:, None, None, :], scores, NEG)
    peak_new = jnp.maximum(peak_run, jnp.max(scores, -1))
    rescale = jnp.exp(peak_run - peak_new)
    weights = jnp.exp(scores - peak_new[..., None])
    total_new = total_run * rescale + jnp.sum(weights, -1)
    mixed_rows = jnp.einsum(
        "bngk,knd->bngd", weights.astype(jnp.bfloat16), val_rows, preferred_element_type=jnp.float32
    )
    return (peak_new, total_new, accum_rows * rescale[..., None] + mixed_rows)


def expert_trade(buffer):
    return lax.all_to_all(buffer, ("ctx", "exp"), split_axis=0, concat_axis=0, tiled=True)


def local(
    resid,
    query,
    key,
    value,
    out_proj,
    norm_gain,
    w_gate,
    w_up,
    w_down,
    routes,
    gate_weights,
    grad_out,
):
    ctx_count = lax.axis_size("ctx")
    exp_count = lax.axis_size("exp")
    ctx_index = lax.axis_index("ctx")
    seq_rows = query.shape[0]
    kv_heads = key.shape[1] // HEAD_SIZE
    group_width = query.shape[1] // HEAD_SIZE // kv_heads
    seq_total = seq_rows * ctx_count
    score_scale = HEAD_SIZE ** (-0.5)
    query_start = ctx_index * seq_rows
    query_pos = query_start + jnp.arange(seq_rows, dtype=jnp.int32)
    queries = query.reshape(seq_rows, kv_heads, group_width, HEAD_SIZE)
    state_shape = (seq_rows, kv_heads, group_width)
    start_state = (
        jnp.full(state_shape, NEG, jnp.float32),
        jnp.zeros(state_shape, jnp.float32),
        jnp.zeros(state_shape + (HEAD_SIZE,), jnp.float32),
    )
    block_len = min(512, seq_total)
    keys_flat, values_flat = (
        lax.all_gather(key, "ctx", axis=0, tiled=True),
        lax.all_gather(value, "ctx", axis=0, tiled=True),
    )
    keys_all = keys_flat.reshape(seq_total, kv_heads, HEAD_SIZE)
    values_all = values_flat.reshape(seq_total, kv_heads, HEAD_SIZE)
    block_count = (query_start + seq_rows + block_len - 1) // block_len

    def forward_turn(loop_turn, soft_state):
        row_begin = loop_turn * block_len
        key_rows = lax.dynamic_slice_in_dim(keys_all, row_begin, block_len, 0)
        val_rows = lax.dynamic_slice_in_dim(values_all, row_begin, block_len, 0)
        return attend_block(
            soft_state, queries, key_rows, val_rows, row_begin, query_pos, score_scale
        )

    soft_state = lax.fori_loop(0, block_count, forward_turn, start_state)
    peak_val, total_val, accum_rows = soft_state
    attention_quad = (accum_rows / total_val[..., None]).astype(jnp.bfloat16)
    attn_mix = attention_quad.reshape(seq_rows, kv_heads * group_width * HEAD_SIZE)
    log_sum_total = peak_val + jnp.log(total_val)
    proj_full = lax.all_gather(out_proj, "ctx", axis=1, tiled=True)
    tok_rows = resid.shape[0]
    proj_sum = lax.psum_scatter(
        jnp.dot(attn_mix, proj_full, preferred_element_type=jnp.float32).astype(jnp.bfloat16),
        "exp",
        scatter_dimension=0,
        tiled=True,
    ).astype(jnp.float32)
    hidden = (resid.astype(jnp.float32) + proj_sum).astype(jnp.bfloat16)
    hidden_f = hidden.astype(jnp.float32)
    inv_rms = lax.rsqrt(jnp.mean(hidden_f * hidden_f, -1, keepdims=True) + EPS)
    unit_rows = hidden_f * inv_rms
    normed = (unit_rows * norm_gain).astype(jnp.bfloat16)
    top_count = routes.shape[1]
    model_width = normed.shape[1]
    experts_local = w_gate.shape[0]
    device_count = ctx_count * exp_count
    expert_total = experts_local * device_count
    capacity = 2 * tok_rows * top_count // expert_total
    flat_routes = routes.reshape(-1)
    member = (flat_routes[:, None] == jnp.arange(expert_total, dtype=jnp.int32)[None, :]).astype(
        jnp.int32
    )
    slot_pos = jnp.sum(jnp.cumsum(member, 0) * member, 1) - 1
    dest_row = flat_routes * capacity + slot_pos
    pair_weights = gate_weights.reshape(-1)

    def place_rows(rows_out):
        return (
            jnp.zeros((expert_total * capacity, model_width), jnp.bfloat16)
            .at[dest_row]
            .set(rows_out)
        )

    def to_experts(buffer):
        return (
            buffer.reshape(device_count, experts_local, capacity, model_width)
            .transpose(1, 0, 2, 3)
            .reshape(experts_local, device_count * capacity, model_width)
        )

    def from_experts(rows_back):
        return (
            rows_back.reshape(experts_local, device_count, capacity, model_width)
            .transpose(1, 0, 2, 3)
            .reshape(device_count * experts_local * capacity, model_width)
        )

    rows_in = to_experts(expert_trade(place_rows(jnp.repeat(normed, top_count, 0))))
    pre_gate = jnp.einsum("erd,edf->erf", rows_in, w_gate, preferred_element_type=jnp.float32)
    pre_up = jnp.einsum("erd,edf->erf", rows_in, w_up, preferred_element_type=jnp.float32)
    sig_gate = jax.nn.sigmoid(pre_gate)
    act_rows = (pre_gate * sig_gate * pre_up).astype(jnp.bfloat16)
    out_rows = jnp.einsum(
        "erf,efd->erd", act_rows, w_down, preferred_element_type=jnp.float32
    ).astype(jnp.bfloat16)
    back_rows = expert_trade(from_experts(out_rows))
    returned = back_rows[dest_row].astype(jnp.float32)
    moe_sum = jnp.sum(
        (returned * pair_weights[:, None]).reshape(tok_rows, top_count, model_width), 1
    )
    layer_out = (hidden_f + moe_sum).astype(jnp.bfloat16)
    grad_f = grad_out.astype(jnp.float32)
    pair_grad = (jnp.repeat(grad_f, top_count, 0) * pair_weights[:, None]).astype(jnp.bfloat16)
    grad_in = to_experts(expert_trade(place_rows(pair_grad)))
    act_grad = jnp.einsum("erd,efd->erf", grad_in, w_down, preferred_element_type=jnp.float32)
    grad_w_down = jnp.einsum(
        "erf,erd->efd", act_rows, grad_in, preferred_element_type=jnp.float32
    ).astype(jnp.bfloat16)
    up_grad = (act_grad * pre_gate * sig_gate).astype(jnp.bfloat16)
    gate_grad = (act_grad * pre_up * sig_gate * (1.0 + pre_gate * (1.0 - sig_gate))).astype(
        jnp.bfloat16
    )
    grad_w_gate = jnp.einsum(
        "erd,erf->edf", rows_in, gate_grad, preferred_element_type=jnp.float32
    ).astype(jnp.bfloat16)
    grad_w_up = jnp.einsum(
        "erd,erf->edf", rows_in, up_grad, preferred_element_type=jnp.float32
    ).astype(jnp.bfloat16)
    row_grad = (
        jnp.einsum("erf,edf->erd", gate_grad, w_gate, preferred_element_type=jnp.float32)
        + jnp.einsum("erf,edf->erd", up_grad, w_up, preferred_element_type=jnp.float32)
    ).astype(jnp.bfloat16)
    back_grad = expert_trade(from_experts(row_grad))
    normed_grad = jnp.sum(
        back_grad[dest_row].astype(jnp.float32).reshape(tok_rows, top_count, model_width), 1
    )
    gain_part = jnp.sum(normed_grad * unit_rows, 0)
    grad_gain = lax.psum(gain_part, ("ctx", "exp"))
    scaled_grad = norm_gain * normed_grad
    hidden_grad = inv_rms * (
        scaled_grad - unit_rows * jnp.mean(scaled_grad * unit_rows, -1, keepdims=True)
    )
    grad_resid = (grad_f + hidden_grad).astype(jnp.bfloat16)
    block_grad = lax.all_gather(grad_resid, "exp", axis=0, tiled=True)
    mixture_gradient = jnp.einsum(
        "td,hd->th", block_grad, proj_full, preferred_element_type=jnp.float32
    ).astype(jnp.bfloat16)
    proj_part = jnp.einsum("th,td->hd", attn_mix, block_grad, preferred_element_type=jnp.float32)
    grad_out_proj = lax.psum_scatter(
        proj_part.astype(jnp.bfloat16), "ctx", scatter_dimension=1, tiled=True
    )
    mixture_quad = mixture_gradient.reshape(seq_rows, kv_heads, group_width, HEAD_SIZE)
    delta_sum = jnp.sum(mixture_quad.astype(jnp.float32) * attention_quad.astype(jnp.float32), -1)
    back_count = (query_start + seq_rows + block_len - 1) // block_len

    def backward_turn(loop_turn, loop_carry):
        query_grad, pair_store = loop_carry
        row_begin = loop_turn * block_len
        key_rows = lax.dynamic_slice_in_dim(keys_all, row_begin, block_len, 0)
        val_rows = lax.dynamic_slice_in_dim(values_all, row_begin, block_len, 0)
        scores = (
            jnp.einsum("bngd,knd->bngk", queries, key_rows, preferred_element_type=jnp.float32)
            * score_scale
        )
        key_pos = row_begin + jnp.arange(block_len, dtype=jnp.int32)
        visible = key_pos[None, :] <= query_pos[:, None]
        prob_full = jnp.where(
            visible[:, None, None, :], jnp.exp(scores - log_sum_total[..., None]), 0.0
        )
        prob_grad = jnp.einsum(
            "bngd,knd->bngk", mixture_quad, val_rows, preferred_element_type=jnp.float32
        )
        score_grad = prob_full * (prob_grad - delta_sum[..., None])
        prob_half = prob_full.astype(jnp.bfloat16)
        score_half = score_grad.astype(jnp.bfloat16)
        query_grad = (
            query_grad
            + jnp.einsum("bngk,knd->bngd", score_half, key_rows, preferred_element_type=jnp.float32)
            * score_scale
        )
        key_grad = (
            jnp.einsum("bngk,bngd->knd", score_half, queries, preferred_element_type=jnp.float32)
            * score_scale
        )
        value_grad = jnp.einsum(
            "bngk,bngd->knd", prob_half, mixture_quad, preferred_element_type=jnp.float32
        )
        pair_store = lax.dynamic_update_slice_in_dim(
            pair_store, jnp.stack([key_grad, value_grad], 2), row_begin, 0
        )
        return (query_grad, pair_store)

    start_back = (
        jnp.zeros(state_shape + (HEAD_SIZE,), jnp.float32),
        jnp.zeros((seq_total, kv_heads, 2, HEAD_SIZE), jnp.float32),
    )
    query_grad, pair_store = lax.fori_loop(0, back_count, backward_turn, start_back)
    grad_query = query_grad.reshape(seq_rows, kv_heads * group_width * HEAD_SIZE).astype(
        jnp.bfloat16
    )
    pair_sum = lax.psum_scatter(
        pair_store.reshape(seq_total, kv_heads * 2 * HEAD_SIZE).astype(jnp.bfloat16),
        "ctx",
        scatter_dimension=0,
        tiled=True,
    ).astype(jnp.float32)
    pair_sum = pair_sum.reshape(seq_rows, kv_heads, 2, HEAD_SIZE)
    key_gradient = pair_sum[:, :, 0].reshape(seq_rows, kv_heads * HEAD_SIZE).astype(jnp.bfloat16)
    value_gradient = pair_sum[:, :, 1].reshape(seq_rows, kv_heads * HEAD_SIZE).astype(jnp.bfloat16)
    return (
        layer_out,
        grad_resid,
        grad_query,
        key_gradient,
        value_gradient,
        grad_out_proj,
        grad_gain,
        grad_w_gate,
        grad_w_up,
        grad_w_down,
    )


def solution(mesh):
    in_specs = (
        P(("groups", "ctx", "exp"), None),
        P(("groups", "ctx"), "exp"),
        P(("groups", "ctx"), "exp"),
        P(("groups", "ctx"), "exp"),
        P("exp", "ctx"),
        P(),
        P(("ctx", "exp"), None, None),
        P(("ctx", "exp"), None, None),
        P(("ctx", "exp"), None, None),
        P(("groups", "ctx", "exp"), None),
        P(("groups", "ctx", "exp"), None),
        P(("groups", "ctx", "exp"), None),
    )
    out_specs = (
        P(("groups", "ctx", "exp"), None),
        P(("groups", "ctx", "exp"), None),
        P(("groups", "ctx"), "exp"),
        P(("groups", "ctx"), "exp"),
        P(("groups", "ctx"), "exp"),
        P(("groups", "exp"), "ctx"),
        P("groups"),
        P(("groups", "ctx", "exp"), None, None),
        P(("groups", "ctx", "exp"), None, None),
        P(("groups", "ctx", "exp"), None, None),
    )
    return jax.shard_map(local, mesh=mesh, in_specs=in_specs, out_specs=out_specs, check_vma=False)
```

profile of v0, /device:TPU:0, one launch (start us, length us, event | category | flops | bytes accessed | tf_op | source)
XLA Modules:
  0.0 475.7 jit_solution(8733258914140163050)
XLA Ops:
  10.3 15.2 %all_gather.12 = bf16[512,128]{1,0:T(8,128)(2,1)S(1)} all-gather(bf16[128,128]{1,0:T(8,128)(2,1)S(1)} %copy-done.19), channel_id=1, replica_groups=mesh['groups'=2,'ctx'=4,'exp'=4] {'ctx'}, dimensions={0}, use_global_device_ids=true | all-gather | bytes 163840 | tf_op jit(solution)/shard_map/all_gather | solution.py:69
  25.5 16.2 %all_gather.13 = bf16[512,128]{1,0:T(8,128)(2,1)S(1)} all-gather(bf16[128,128]{1,0:T(8,128)(2,1)S(1)} %copy-done.20), channel_id=1, replica_groups=mesh['groups'=2,'ctx'=4,'exp'=4] {'ctx'}, dimensions={0}, use_global_device_ids=true | all-gather | bytes 163840 | tf_op jit(solution)/shard_map/all_gather | solution.py:70
  43.8 51.7 %all-gather.2.cloned.1.call-done = bf16[1024,2048]{1,0:T(8,128)(2,1)} async-done(((bf16[1024,512]{1,0:T(8,128)(2,1)}), bf16[1024,2048]{1,0:T(8,128)(2,1)}) %all-gather.2.cloned.1.call-update) | async-done | bytes 4194320 | tf_op jit(solution)/shard_map/all_gather | solution.py:89
  95.4 3.8 convolution_convert_fusion.5
  100.4 19.2 %reduce-scatter.6.cloned.1.call-done = bf16[32,2048]{1,0:T(8,128)(2,1)} async-done(((bf16[128,2048]{1,0:T(8,128)(2,1)}), bf16[32,2048]{1,0:T(8,128)(2,1)}) %reduce-scatter.6.cloned.1.call-update) | async-done | bytes 131088 | tf_op jit(solution)/shard_map/reduce_scatter | solution.py:91
  124.5 4.9 %all-to-all-start = ((bf16[16,32,2048]{2,1,0:T(8,128)(2,1)}), bf16[16,32,2048]{2,1,0:T(8,128)(2,1)}, u32[]{:S(2)}, u32[]{:S(2)}) async-start(bf16[16,32,2048]{2,1,0:T(8,128)(2,1)} %bitcast.284), calls=%async_computation.1 | async-start | bytes 4194304 | tf_op jit(solution)/shard_map/all_to_all | solution.py:33
  129.6 3.8 scatter_custom_fusion.1
  133.4 37.1 %all-to-all-done = bf16[16,32,2048]{2,1,0:T(8,128)(2,1)} async-done(((bf16[16,32,2048]{2,1,0:T(8,128)(2,1)}), bf16[16,32,2048]{2,1,0:T(8,128)(2,1)}, u32[]{:S(2)}, u32[]{:S(2)}) %all-to-all-start) | async-done | bytes 2097184 | tf_op jit(solution)/shard_map/all_to_all | solution.py:33
  170.5 11.3 %all-to-all-start.2 = ((bf16[16,32,2048]{2,1,0:T(8,128)(2,1)}), bf16[16,32,2048]{2,1,0:T(8,128)(2,1)}, u32[]{:S(2)}, u32[]{:S(2)}) async-start(bf16[16,32,2048]{2,1,0:T(8,128)(2,1)} %bitcast.283), calls=%async_computation.3 | async-start | bytes 4194304 | tf_op jit(solution)/shard_map/all_to_all | solution.py:33
  181.8 4.3 fusion.39
  189.8 33.1 %all-to-all-done.2 = bf16[16,32,2048]{2,1,0:T(8,128)(2,1)} async-done(((bf16[16,32,2048]{2,1,0:T(8,128)(2,1)}), bf16[16,32,2048]{2,1,0:T(8,128)(2,1)}, u32[]{:S(2)}, u32[]{:S(2)}) %all-to-all-start.2) | async-done | bytes 2097184 | tf_op jit(solution)/shard_map/all_to_all | solution.py:33
  231.1 11.3 %all-to-all-start.3 = ((bf16[16,32,2048]{2,1,0:T(8,128)(2,1)}), bf16[16,32,2048]{2,1,0:T(8,128)(2,1)}, u32[]{:S(2)}, u32[]{:S(2)}) async-start(bf16[16,32,2048]{2,1,0:T(8,128)(2,1)} %bitcast.285), calls=%async_computation.4 | async-start | bytes 4194304 | tf_op jit(solution)/shard_map/all_to_all | solution.py:33
  244.9 38.6 %all-to-all-done.3 = bf16[16,32,2048]{2,1,0:T(8,128)(2,1)} async-done(((bf16[16,32,2048]{2,1,0:T(8,128)(2,1)}), bf16[16,32,2048]{2,1,0:T(8,128)(2,1)}, u32[]{:S(2)}, u32[]{:S(2)}) %all-to-all-start.3) | async-done | bytes 2097184 | tf_op jit(solution)/shard_map/all_to_all | solution.py:33
  283.5 11.3 %all-to-all-start.1 = ((bf16[16,32,2048]{2,1,0:T(8,128)(2,1)}), bf16[16,32,2048]{2,1,0:T(8,128)(2,1)}, u32[]{:S(2)}, u32[]{:S(2)}) async-start(bf16[16,32,2048]{2,1,0:T(8,128)(2,1)} %bitcast.292), calls=%async_computation.2 | async-start | bytes 4194304 | tf_op jit(solution)/shard_map/all_to_all | solution.py:33
  295.7 4.2 gather_fusion.1
  299.9 36.0 %all-to-all-done.1 = bf16[16,32,2048]{2,1,0:T(8,128)(2,1)} async-done(((bf16[16,32,2048]{2,1,0:T(8,128)(2,1)}), bf16[16,32,2048]{2,1,0:T(8,128)(2,1)}, u32[]{:S(2)}, u32[]{:S(2)}) %all-to-all-start.1) | async-done | bytes 2097184 | tf_op jit(solution)/shard_map/all_to_all | solution.py:33
  335.9 5.2 %gather_fusion = bf16[256,2048]{1,0:T(8,128)(2,1)} fusion(bf16[512,2048]{1,0:T(8,128)(2,1)} %bitcast.15, s32[1024]{0:T(1024)S(1)} %pad_clamp_fusion), kind=kCustom, calls=%fused_computation | custom fusion | bytes 2098176 | tf_op jit(solution)/shard_map/gather | solution.py:146
  346.2 9.3 %all_gather.15 = bf16[128,2048]{1,0:T(8,128)(2,1)S(1)} all-gather(bf16[32,2048]{1,0:T(8,128)(2,1)S(1)} %get-tuple-element.292), channel_id=1, replica_groups=mesh['groups'=2,'ctx'=4,'exp'=4] {'exp'}, dimensions={0}, use_global_device_ids=true | all-gather | bytes 655360 | tf_op jit(solution)/shard_map/all_gather | solution.py:183
  367.2 4.1 convolution_convert_fusion
  372.3 3.8 fusion.32
  376.1 4.1 fusion.30
  380.2 4.1 fusion.31
  385.3 39.6 %psum.7 = f32[2048]{0:T(1024)} all-reduce(f32[2048]{0:T(1024)S(1)} %copy-done.21), channel_id=1, replica_groups=mesh['groups'=2,'ctx'=4,'exp'=4] {'ctx','exp'}, use_global_device_ids=true, to_apply=%region_20.21 | all-reduce | flops 2048 | bytes 16384 | tf_op jit(solution)/shard_map/psum | solution.py:177
  427.2 41.9 %reduce-scatter.8.cloned.1.call-done = bf16[1024,512]{1,0:T(8,128)(2,1)} async-done(((bf16[1024,2048]{1,0:T(8,128)(2,1)}), bf16[1024,512]{1,0:T(8,128)(2,1)}) %reduce-scatter.8.cloned.1.call-update) | async-done | bytes 1048592 | tf_op jit(solution)/shard_map/reduce_scatter | solution.py:188
  (136 shorter events, 52.3 us)
Async XLA Ops:
  7.2 215.8 %copy-start = (bf16[1,384,2048]{2,1,0:T(8,128)(2,1)S(1)}, bf16[1,384,2048]{2,1,0:T(8,128)(2,1)}, u32[]{:S(2)}) copy-start(bf16[1,384,2048]{2,1,0:T(8,128)(2,1)} %param.24) | copy-start | bytes 4718596
  7.2 18.3 %copy-start.20 = (bf16[128,128]{1,0:T(8,128)(2,1)S(1)}, bf16[128,128]{1,0:T(8,128)(2,1)}, u32[]{:S(2)}) copy-start(bf16[128,128]{1,0:T(8,128)(2,1)} %param.19) | copy-start | bytes 98308
  7.2 88.2 %all-gather.2.cloned.1.call-start = ((), (), s32[]{:S(2)}) async-start(), calls=%async_computation.7 | async-start | bytes 5242880 | tf_op jit(solution)/shard_map/all_gather | solution.py:89
  7.9 111.6 %reduce-scatter.6.cloned.1.call-start = ((), (), s32[]{:S(2)}) async-start(), calls=%async_computation.8 | async-start | bytes 655360 | tf_op jit(solution)/shard_map/reduce_scatter | solution.py:91
  43.7 55.5 %copy-start.2 = (f32[128,1,8,128]{0,3,2,1:T(8,128)}, f32[128,1,8,128]{0,3,2,1:T(8,128)S(1)}, u32[]{:S(2)}) copy-start(f32[128,1,8,128]{0,3,2,1:T(8,128)S(1)} %copy.50) | copy-start | bytes 1572868
  43.8 55.4 %copy-start.4 = (bf16[128,1,8,128]{0,3,2,1:T(8,128)(2,1)}, bf16[128,1,8,128]{0,3,2,1:T(8,128)(2,1)S(1)}, u32[]{:S(2)}) copy-start(bf16[128,1,8,128]{0,3,2,1:T(8,128)(2,1)S(1)} %divide_convert_fusion) | copy-start | bytes 786436
  95.4 4.6 copy-start.22
  95.4 24.1 %copy-start.17 = (bf16[32,2048]{1,0:T(8,128)(2,1)S(1)}, bf16[32,2048]{1,0:T(8,128)(2,1)}, u32[]{:S(2)}) copy-start(bf16[32,2048]{1,0:T(8,128)(2,1)} %param.16) | copy-start | bytes 393220
  95.4 25.2 %copy-start.18 = (f32[2048]{0:T(1024)S(1)}, f32[2048]{0:T(1024)}, u32[]{:S(2)}) copy-start(f32[2048]{0:T(1024)} %param.21) | copy-start | bytes 24580
  120.6 223.5 %copy-start.23 = (f32[32]{0:T(128)}, f32[32]{0:T(128)S(1)}, u32[]{:S(2)}) copy-start(f32[32]{0:T(128)S(1)} %add_rsqrt_fusion) | copy-start | bytes 388
  124.5 4.9 %copy-start.24 = (f32[32,8]{0,1:T(8,128)S(1)}, f32[32,8]{0,1:T(8,128)}, u32[]{:S(2)}) copy-start(f32[32,8]{0,1:T(8,128)} %param.26) | copy-start | bytes 3076
  124.5 5.1 %copy-start.11 = (bf16[32,2048]{1,0:T(8,128)(2,1)S(1)}, bf16[32,2048]{1,0:T(8,128)(2,1)}, u32[]{:S(2)}) copy-start(bf16[32,2048]{1,0:T(8,128)(2,1)} %param.27) | copy-start | bytes 393220
  124.5 46.1 %all-to-all-start = ((bf16[16,32,2048]{2,1,0:T(8,128)(2,1)}), bf16[16,32,2048]{2,1,0:T(8,128)(2,1)}, u32[]{:S(2)}, u32[]{:S(2)}) async-start(bf16[16,32,2048]{2,1,0:T(8,128)(2,1)} %bitcast.284), calls=%async_computation.1 | async-start | bytes 4194304 | tf_op jit(solution)/shard_map/all_to_all | solution.py:33
  170.5 52.4 %all-to-all-start.2 = ((bf16[16,32,2048]{2,1,0:T(8,128)(2,1)}), bf16[16,32,2048]{2,1,0:T(8,128)(2,1)}, u32[]{:S(2)}, u32[]{:S(2)}) async-start(bf16[16,32,2048]{2,1,0:T(8,128)(2,1)} %bitcast.283), calls=%async_computation.3 | async-start | bytes 4194304 | tf_op jit(solution)/shard_map/all_to_all | solution.py:33
  181.8 4.3 copy-start.6
  226.6 15.7 %copy-start.15 = (bf16[512,384]{1,0:T(8,128)(2,1)}, bf16[512,384]{1,0:T(8,128)(2,1)S(1)}, u32[]{:S(2)}) copy-start(bf16[512,384]{1,0:T(8,128)(2,1)S(1)} %get-tuple-element.291) | copy-start | bytes 1179652
  231.1 52.4 %all-to-all-start.3 = ((bf16[16,32,2048]{2,1,0:T(8,128)(2,1)}), bf16[16,32,2048]{2,1,0:T(8,128)(2,1)}, u32[]{:S(2)}, u32[]{:S(2)}) async-start(bf16[16,32,2048]{2,1,0:T(8,128)(2,1)} %bitcast.285), calls=%async_computation.4 | async-start | bytes 4194304 | tf_op jit(solution)/shard_map/all_to_all | solution.py:33
  283.5 52.4 %all-to-all-start.1 = ((bf16[16,32,2048]{2,1,0:T(8,128)(2,1)}), bf16[16,32,2048]{2,1,0:T(8,128)(2,1)}, u32[]{:S(2)}, u32[]{:S(2)}) async-start(bf16[16,32,2048]{2,1,0:T(8,128)(2,1)} %bitcast.292), calls=%async_computation.2 | async-start | bytes 4194304 | tf_op jit(solution)/shard_map/all_to_all | solution.py:33
  294.8 130.0 %reduce-scatter.10.cloned.1.call-start = ((), (), s32[]{:S(2)}) async-start(), calls=%async_computation.10 | async-start | bytes 327680
  341.1 14.4 %copy-start.1 = (bf16[1024,2048]{1,0:T(8,128)(2,1)S(1)}, bf16[1024,2048]{1,0:T(8,128)(2,1)}, u32[]{:S(2)}) copy-start(bf16[1024,2048]{1,0:T(8,128)(2,1)} %all-gather.2.cloned.1.call-done) | copy-start | bytes 12582916
  346.2 10.9 %copy-start.12 = (bf16[32,2048]{1,0:T(8,128)(2,1)}, bf16[32,2048]{1,0:T(8,128)(2,1)S(1)}, u32[]{:S(2)}) copy-start(bf16[32,2048]{1,0:T(8,128)(2,1)S(1)} %get-tuple-element.292) | copy-start | bytes 393220
  357.1 4.5 copy-start.25
  366.9 102.3 %reduce-scatter.8.cloned.1.call-start = ((), (), s32[]{:S(2)}) async-start(), calls=%async_computation.9 | async-start | bytes 5242880 | tf_op jit(solution)/shard_map/reduce_scatter | solution.py:188
  380.2 5.0 %copy-start.21 = (f32[2048]{0:T(1024)S(1)}, f32[2048]{0:T(1024)}, u32[]{:S(2)}) copy-start(f32[2048]{0:T(1024)} %get-tuple-element.241) | copy-start | bytes 24580
  (10 other events, 25.0 us)
Sparse Core Ops, SparseCore 0:
  9.6 85.7 all-gather.1
  99.4 20.1 reduce-scatter.5
  367.0 23.9 reduce-scatter.9
  393.7 75.4 reduce-scatter.7
where the time goes:
time: 477 us; the launch traced here: 476 us
  waiting for transfers between devices  258 us (54%)
  blocking collectives  80.4 us (17%)
  matrix products  43 us (9%)
  starting transfers between devices  39.3 us (8%)
  local copies, waits for them, and re-layouts  26.4 us (6%)
  between operations  14.2 us (3%)
  other arithmetic  13.9 us (3%)
    all_to_all x4, waiting for transfers between devices, expert_trade(): lax.all_to_all(buffer, ('ctx', 'exp'), split_axis=0, concat_axis=0, tiled...  145 us
    all_gather x1, waiting for transfers between devices, local(): proj_full = lax.all_gather(out_proj, 'ctx', axis=1, tiled=True)  51.7 us
    reduce_scatter x1, waiting for transfers between devices, local(): lax.psum_scatter(proj_part.astype(jnp.bfloat16), 'ctx', scatter_dimension...  41.9 us
    psum x1, blocking collectives, local(): grad_gain = lax.psum(gain_part, ('ctx', 'exp'))  39.6 us
    all_to_all x4, starting transfers between devices, expert_trade(): lax.all_to_all(buffer, ('ctx', 'exp'), split_axis=0, concat_axis=0, tiled...  38.7 us
    reduce_scatter x1, waiting for transfers between devices, local(): lax.psum_scatter(jnp.dot(attn_mix, proj_full, preferred_element_type=jnp....  19.2 us
    all_gather x1, blocking collectives, local(): lax.all_gather(value, 'ctx', axis=0, tiled=True)  16.2 us
    all_gather x1, blocking collectives, local(): lax.all_gather(key, 'ctx', axis=0, tiled=True)  15.2 us
  transfers between devices with their start and end apart: 8, of which 7 were waited for; matrix products, arithmetic and copies ran while one was open for 9% of the time, Pallas kernels for 0%

commit v1 on v0

--- a/solution.py
+++ b/solution.py
@@ -1,6 +1,8 @@
 import jax
 import jax.numpy as jnp
 from jax import lax
+from jax.experimental import pallas as pl
+from jax.experimental.pallas import tpu as pltpu
 from jax.sharding import PartitionSpec as P
 
 HEAD_SIZE = 128
@@ -33,7 +35,7 @@
     return lax.all_to_all(buffer, ("ctx", "exp"), split_axis=0, concat_axis=0, tiled=True)
 
 
-def local(
+def local_routed(
     resid,
     query,
     key,
@@ -259,6 +261,285 @@
         grad_w_down,
     )
 
+F32 = jnp.float32
+BF16 = jnp.bfloat16
+
+
+def shifted(x, shift, count):
+    return lax.ppermute(x, "ctx", [(i, (i + shift) % count) for i in range(count)])
+
+
+def swapped(x, bit, count):
+    return lax.ppermute(x, "exp", [(i, i ^ bit) for i in range(count)])
+
+
+def exp_bits(exp_count):
+    return [1 << b for b in reversed(range(exp_count.bit_length() - 1))]
+
+
+def pick(x, index, axis):
+    return lax.dynamic_index_in_dim(x, index, axis, keepdims=False)
+
+
+def ctx_order(blocks, ctx_index):
+    count = len(blocks)
+    return jnp.stack(blocks)[(ctx_index - jnp.arange(count, dtype=jnp.int32)) % count]
+
+
+def exp_order(blocks, exp_index):
+    count = len(blocks)
+    return jnp.stack(blocks)[exp_index ^ jnp.arange(count, dtype=jnp.int32)]
+
+
+def gather_ctx(x, count):
+    return [x] + [shifted(x, d, count) for d in range(1, count)]
+
+
+def gather_exp(x, count):
+    parts = {0: x}
+    for bit in exp_bits(count):
+        for r in list(parts):
+            parts[r ^ bit] = swapped(parts[r], bit, count)
+    return [parts[r] for r in range(count)]
+
+
+def scatter_exp(x, exp_index, count):
+    for bit in reversed(exp_bits(count)):
+        halves = x.reshape((x.shape[0] // 2, 2) + x.shape[1:])
+        mine = (exp_index // bit) % 2
+        got = swapped(pick(halves, 1 - mine, 1), bit, count)
+        x = (pick(halves, mine, 1).astype(F32) + got.astype(F32)).astype(BF16)
+    return x[0]
+
+
+def scatter_ctx(x, ctx_index, count):
+    total = pick(x, ctx_index, 0).astype(F32)
+    for d in range(1, count):
+        total = total + shifted(pick(x, (ctx_index + d) % count, 0), d, count).astype(F32)
+    return total
+
+
+def nt(a, b):
+    return lax.dot_general(a, b, (((1,), (1,)), ((), ())), preferred_element_type=F32)
+
+
+def tn(a, b):
+    return lax.dot_general(a, b, (((0,), (0,)), ((), ())), preferred_element_type=F32)
+
+
+def nn(a, b):
+    return lax.dot_general(a, b, (((1,), (0,)), ((), ())), preferred_element_type=F32)
+
+
+def soft_rows(query, keys, block):
+    rows = query.shape[0]
+    scores = nt(query, keys) * HEAD_SIZE ** (-0.5)
+    query_pos = block * rows + lax.broadcasted_iota(jnp.int32, scores.shape, 0)
+    key_pos = lax.broadcasted_iota(jnp.int32, scores.shape, 1)
+    scores = jnp.where(key_pos <= query_pos, scores, NEG)
+    weights = jnp.exp(scores - jnp.max(scores, -1, keepdims=True))
+    return weights, jnp.sum(weights, -1, keepdims=True)
+
+
+def forward_kernel(query_ref, key_ref, value_ref, mix_ref):
+    block = pl.program_id(0)
+    for head in range(query_ref.shape[1] // HEAD_SIZE):
+        cols = slice(head * HEAD_SIZE, (head + 1) * HEAD_SIZE)
+        weights, total = soft_rows(query_ref[:, cols], key_ref[...], block)
+        mixed = nn(weights.astype(BF16), value_ref[...])
+        mix_ref[:, cols] = (mixed / total).astype(BF16)
+
+
+def attention_forward(query_all, key_all, value_all, rows):
+    total, width = query_all.shape
+    return pl.pallas_call(
+        forward_kernel,
+        grid=(total // rows,),
+        in_specs=[
+            pl.BlockSpec((rows, width), lambda i: (i, 0)),
+            pl.BlockSpec(key_all.shape, lambda i: (0, 0)),
+            pl.BlockSpec(value_all.shape, lambda i: (0, 0)),
+        ],
+        out_specs=pl.BlockSpec((rows, width), lambda i: (i, 0)),
+        out_shape=jax.ShapeDtypeStruct((total, width), BF16),
+        compiler_params=pltpu.CompilerParams(vmem_limit_bytes=32 << 20),
+        name="attention_forward",
+    )(query_all, key_all, value_all)
+
+
+def backward_kernel(block_ref, query_ref, key_ref, value_ref, mix_ref, grad_ref, dq_ref, pair_ref):
+    block = block_ref[0]
+    keys, values = key_ref[...], value_ref[...]
+    scale = HEAD_SIZE ** (-0.5)
+    key_sum = value_sum = 0.0
+    for head in range(query_ref.shape[1] // HEAD_SIZE):
+        cols = slice(head * HEAD_SIZE, (head + 1) * HEAD_SIZE)
+        query, mix, grad = query_ref[:, cols], mix_ref[:, cols], grad_ref[:, cols]
+        weights, total = soft_rows(query, keys, block)
+        prob = weights / total
+        delta = jnp.sum(grad.astype(F32) * mix.astype(F32), -1, keepdims=True)
+        score_half = (prob * (nt(grad, values) - delta)).astype(BF16)
+        dq_ref[:, cols] = (nn(score_half, keys) * scale).astype(BF16)
+        key_sum = key_sum + tn(score_half, query)
+        value_sum = value_sum + tn(prob.astype(BF16), grad)
+    pair_ref[:, :HEAD_SIZE] = (key_sum * scale).astype(BF16)
+    pair_ref[:, HEAD_SIZE:] = value_sum.astype(BF16)
+
+
+def attention_backward(block, query, key_all, value_all, mix, grad):
+    vmem = pl.BlockSpec(memory_space=pltpu.VMEM)
+    return pl.pallas_call(
+        backward_kernel,
+        in_specs=[pl.BlockSpec(memory_space=pltpu.SMEM)] + [vmem] * 5,
+        out_specs=[vmem, vmem],
+        out_shape=[
+            jax.ShapeDtypeStruct(query.shape, BF16),
+            jax.ShapeDtypeStruct((key_all.shape[0], 2 * HEAD_SIZE), BF16),
+        ],
+        compiler_params=pltpu.CompilerParams(vmem_limit_bytes=32 << 20),
+        name="attention_backward",
+    )(block.reshape(1), query, key_all, value_all, mix, grad)
+
+
+def local_dense(
+    resid,
+    query,
+    key,
+    value,
+    out_proj,
+    norm_gain,
+    w_gate,
+    w_up,
+    w_down,
+    routes,
+    gate_weights,
+    grad_out,
+):
+    n, m = lax.axis_size("ctx"), lax.axis_size("exp")
+    c, e = lax.axis_index("ctx"), lax.axis_index("exp")
+    rows, head_cols = query.shape
+    tok, width = resid.shape
+    cols = out_proj.shape[1]
+    expert_total = n * m
+    total = n * m * tok
+
+    pair = jnp.concatenate([key, value], 1)
+    pair_all = ctx_order(gather_ctx(pair, n), c).reshape(n * rows, 2 * HEAD_SIZE)
+    key_all, value_all = pair_all[:, :HEAD_SIZE], pair_all[:, HEAD_SIZE:]
+    query_all = ctx_order(gather_ctx(query, n), c).reshape(n * rows, head_cols)
+    resid_cut = resid.reshape(tok, n, cols)
+    resid_all = ctx_order(
+        [pick(resid_cut, c, 1)]
+        + [shifted(pick(resid_cut, (c + d) % n, 1), d, n) for d in range(1, n)],
+        c,
+    )
+    gate_dense = jnp.sum(
+        jnp.where(
+            routes[:, :, None] == jnp.arange(expert_total, dtype=jnp.int32)[None, None, :],
+            gate_weights[:, :, None],
+            0.0,
+        ),
+        1,
+    )
+    gate_all = lax.all_gather(gate_dense, ("ctx", "exp"), axis=0, tiled=True)
+    gate_col = lax.dynamic_slice_in_dim(gate_all, c * m + e, 1, 1)
+
+    def gather_rows(x):
+        got = ctx_order(gather_ctx(x, n), c)
+        got = exp_order(gather_exp(got, m), e)
+        return got.transpose(1, 0, 2, 3).reshape(total, width)
+
+    grad_all = gather_rows(grad_out)
+    proj_full = lax.all_gather(out_proj, "ctx", axis=1, tiled=True)
+
+    mix_all = attention_forward(query_all, key_all, value_all, rows)
+    part = nn(mix_all, out_proj).astype(BF16).reshape(n, m, tok, cols)
+    block_sum = scatter_exp(part.transpose(1, 0, 2, 3), e, m)
+    hidden_block = (block_sum.astype(F32) + resid_all.astype(F32)).astype(BF16)
+
+    got = jnp.stack(exp_order(gather_exp(ctx_order(gather_ctx(hidden_block, n), c), m), e))
+    hidden_all = got.transpose(2, 0, 3, 1, 4).reshape(total, width)
+    hidden_f = hidden_all.astype(F32)
+    rms_all = lax.rsqrt(jnp.mean(hidden_f * hidden_f, -1, keepdims=True) + EPS)
+    normed_all = (hidden_f * rms_all * norm_gain).astype(BF16)
+
+    gate_in, up_in, down_in = w_gate[0], w_up[0], w_down[0]
+    routed = gate_col > 0.0
+    grad_rows = (grad_all.astype(F32) * gate_col).astype(BF16)
+    act_grad = nt(grad_rows, down_in)
+    pre_gate = nn(normed_all, gate_in)
+    pre_up = nn(normed_all, up_in)
+    sig = jax.nn.sigmoid(pre_gate)
+    act_rows = (pre_gate * sig * pre_up).astype(BF16)
+    up_grad = (act_grad * pre_gate * sig).astype(BF16)
+    gate_grad = (act_grad * pre_up * sig * (1.0 + pre_gate * (1.0 - sig))).astype(BF16)
+    row_grad = (nt(gate_grad, gate_in) + nt(up_grad, up_in)).astype(BF16)
+    out_rows = nn(act_rows, down_in).astype(BF16)
+    weighted = (out_rows.astype(F32) * gate_col).astype(BF16)
+
+    def scatter_rows(x):
+        blocks = x.reshape(n, m, tok, width).transpose(1, 0, 2, 3)
+        return scatter_ctx(scatter_exp(blocks, e, m), c, n)
+
+    normed_grad = scatter_rows(row_grad)
+    moe_sum = scatter_rows(weighted)
+    grad_w_down = tn(act_rows, grad_rows).astype(BF16)[None]
+    grad_w_gate = tn(normed_all, gate_grad).astype(BF16)[None]
+    grad_w_up = tn(normed_all, up_grad).astype(BF16)[None]
+
+    start = (c * m + e) * tok
+    hidden = lax.dynamic_slice_in_dim(hidden_all, start, tok, 0).astype(F32)
+    inv_rms = lax.dynamic_slice_in_dim(rms_all, start, tok, 0)
+    layer_out = (hidden + moe_sum).astype(BF16)
+    unit_rows = hidden * inv_rms
+    scaled = norm_gain * normed_grad
+    hidden_grad = inv_rms * (scaled - unit_rows * jnp.mean(scaled * unit_rows, -1, keepdims=True))
+    grad_resid = (grad_out.astype(F32) + hidden_grad).astype(BF16)
+    grad_gain = jnp.sum(normed_grad * unit_rows, 0).reshape(-1, 128)
+    for bit in exp_bits(m):
+        grad_gain = grad_gain + swapped(grad_gain, bit, m)
+    grad_gain = sum(gather_ctx(grad_gain, n)[1:], grad_gain).reshape(width)
+
+    block_grad = exp_order(gather_exp(grad_resid, m), e).reshape(rows, width)
+    mix_grad = nt(block_grad, proj_full).astype(BF16)
+    mix = lax.dynamic_slice_in_dim(mix_all, c * rows, rows, 0)
+    grad_query, pair_part = attention_backward(c, query, key_all, value_all, mix, mix_grad)
+    pair_sum = scatter_ctx(pair_part.reshape(n, rows, 2 * HEAD_SIZE), c, n).astype(BF16)
+
+    grad_cut = grad_resid.reshape(tok, n, cols)
+    cut = ctx_order(
+        [pick(grad_cut, c, 1)]
+        + [shifted(pick(grad_cut, (c + d) % n, 1), d, n) for d in range(1, n)],
+        c,
+    )
+    cut = exp_order(gather_exp(cut, m), e).transpose(1, 0, 2, 3).reshape(total, cols)
+    grad_out_proj = tn(mix_all, cut).astype(BF16)
+    return (
+        layer_out,
+        grad_resid,
+        grad_query,
+        pair_sum[:, :HEAD_SIZE],
+        pair_sum[:, HEAD_SIZE:],
+        grad_out_proj,
+        grad_gain,
+        grad_w_gate,
+        grad_w_up,
+        grad_w_down,
+    )
+
+
+def local(*args):
+    resid, key, w_gate, routes = args[0], args[2], args[6], args[9]
+    ctx_count, exp_count = lax.axis_size("ctx"), lax.axis_size("exp")
+    expert_total = w_gate.shape[0] * ctx_count * exp_count
+    dense = (
+        2 * routes.shape[1] >= expert_total
+        and w_gate.shape[0] == 1
+        and key.shape[1] == HEAD_SIZE
+        and exp_count & (exp_count - 1) == 0
+    )
+    return (local_dense if dense else local_routed)(*args)
+
 
 def solution(mesh):
     in_specs = (

time: 477 us -> 314 us (0.66)
  waiting for transfers between devices: 258 us -> 58.9 us
  blocking collectives: 80.4 us -> 24.3 us
  starting transfers between devices: 39.3 us -> 92.7 us
  local copies, waits for them, and re-layouts: 26.4 us -> 56.2 us
  matrix products: 43 us -> 21.8 us
  other arithmetic: 13.9 us -> 29.9 us
  Pallas kernels: 0 us -> 13.6 us
    all_to_all x4 -> x0, waiting for transfers between devices: 145 us -> none  [expert_trade(): lax.all_to_all(buffer, ('ctx', 'exp'), split_axis=0, concat_axis=0, tiled...]
    ppermute x0 -> x50, starting transfers between devices: none -> 92.7 us  [the longest x30 82.1 us: shifted(): lax.ppermute(x, 'ctx', [(i, (i + shift) % count) for i in range(count)])]
    reduce_scatter x2 -> x0, waiting for transfers between devices: 61.1 us -> none  [the longest x1 41.9 us: local(): lax.psum_scatter(proj_part.astype(jnp.bfloat16), 'ctx', scatter_dimension...]
    ppermute x0 -> x50, waiting for transfers between devices: none -> 58.9 us  [the longest x20 29.9 us: swapped(): return lax.ppermute(x, 'exp', [(i, i ^ bit) for i in range(count)])]
    all_gather x1, waiting for transfers between devices: 51.7 us -> 0.01 us  [local_dense(): proj_full = lax.all_gather(out_proj, 'ctx', axis=1, tiled=True)]
    psum x1 -> x0, blocking collectives: 39.6 us -> none  [local(): grad_gain = lax.psum(gain_part, ('ctx', 'exp'))]
    all_to_all x4 -> x0, starting transfers between devices: 38.7 us -> none  [expert_trade(): lax.all_to_all(buffer, ('ctx', 'exp'), split_axis=0, concat_axis=0, tiled...]
    dot_general x19 -> x12, matrix products: 43 us -> 21.8 us  [the longest x4 9.06 us: tn(): lax.dot_general(a, b, (((0,), (0,)), ((), ())), preferred_element_type=F32)]
  transfers between devices with their start and end apart: 8 -> 51, of which waited for: 7 -> 14; matrix products, arithmetic and copies ran while one was open for 9% -> 32% of each run, Pallas kernels for 0% -> 3%
where the time goes in v1:
time: 314 us; the launch traced here: 312 us
  starting transfers between devices  92.7 us (30%)
  waiting for transfers between devices  58.9 us (19%)
  local copies, waits for them, and re-layouts  56.2 us (18%)
  other arithmetic  29.9 us (10%)
  blocking collectives  24.3 us (8%)
  matrix products  21.8 us (7%)
  between operations  14.8 us (5%)
  Pallas kernels  13.6 us (4%)
    ppermute x30, starting transfers between devices, shifted(): lax.ppermute(x, 'ctx', [(i, (i + shift) % count) for i in range(count)])  82.1 us
    ppermute x20, waiting for transfers between devices, swapped(): return lax.ppermute(x, 'exp', [(i, i ^ bit) for i in range(count)])  29.9 us
    ppermute x30, waiting for transfers between devices, shifted(): lax.ppermute(x, 'ctx', [(i, (i + shift) % count) for i in range(count)])  29 us
    all_gather x1, blocking collectives, local_dense(): gate_all = lax.all_gather(gate_dense, ('ctx', 'exp'), axis=0, tiled=True)  24.3 us
    gather x4, local copies, waits for them, and re-layouts, exp_order(): return jnp.stack(blocks)[exp_index ^ jnp.arange(count, dtype=jnp.int32)]  12.7 us
    unnamed x60, local copies, waits for them, and re-layouts  12.6 us
    ppermute x20, starting transfers between devices, swapped(): return lax.ppermute(x, 'exp', [(i, i ^ bit) for i in range(count)])  10.6 us
    another operation x4, other arithmetic, exp_order(): return jnp.stack(blocks)[exp_index ^ jnp.arange(count, dtype=jnp.int32)]  9.67 us
  transfers between devices with their start and end apart: 51, of which 14 were waited for; matrix products, arithmetic and copies ran while one was open for 32% of the time, Pallas kernels for 3%

profile of v1, /device:TPU:0, one launch (start us, length us, event | category | flops | bytes accessed | tf_op | source)
XLA Modules:
  0.0 312.2 jit_solution(2678046812977673300)
XLA Ops:
  7.3 5.1 %collective-permute-start.2 = (bf16[128,1024]{1,0:T(8,128)(2,1)}, bf16[128,1024]{1,0:T(8,128)(2,1)S(1)}, u32[]{:S(2)}, u32[]{:S(2)}) collective-permute-start(bf16[128,1024]{1,0:T(8,128)(2,1)} %query_ref.1), channel_id=1, source_target_pairs={{0,12},{4,0},{8,4},{12,8},{1,13},{5,1},{9,5},{13,9},{2,14},{6,2},{... | collective-permute-start | bytes 786440 | tf_op jit(solution)/shard_map/ppermute | solution.py:269
  21.6 24.3 %all-gather = f32[16,32,16]{1,2,0:T(8,128)S(1)} all-gather(f32[1,32,16]{1,2,0:T(8,128)S(1)} %bitcast.266), channel_id=1, replica_groups=mesh['groups'=2,'ctx'=4,'exp'=4] {'ctx','exp'}, dimensions={0}, use_global_device_ids=true | all-gather | bytes 34816 | tf_op jit(solution)/shard_map/all_gather | solution.py:444
  47.3 22.7 %collective-permute-start = (bf16[128,1024]{1,0:T(8,128)(2,1)S(1)}, bf16[128,1024]{1,0:T(8,128)(2,1)S(1)}, u32[]{:S(2)}, u32[]{:S(2)}) collective-permute-start(bf16[128,1024]{1,0:T(8,128)(2,1)S(1)} %copy-done.3), channel_id=1, source_target_pairs={{0,4},{4,8},{8,12},{12,0},{1,5},{5,9},{9,13},{13,1},{2,6},{6,10},{... | collective-permute-start | bytes 786440 | tf_op jit(solution)/shard_map/ppermute | solution.py:269
  71.6 3.8 %collective-permute-start.23 = (bf16[32,2048]{1,0:T(8,128)(2,1)S(1)}, bf16[32,2048]{1,0:T(8,128)(2,1)}, u32[]{:S(2)}, u32[]{:S(2)}) collective-permute-start(bf16[32,2048]{1,0:T(8,128)(2,1)S(1)} %copy-done.15), channel_id=1, source_target_pairs={{0,8},{4,12},{8,0},{12,4},{1,9},{5,13},{9,1},{13,5},{2,10},{6,14},... | collective-permute-start | bytes 393224 | tf_op jit(solution)/shard_map/ppermute | solution.py:269
  76.2 3.8 %collective-permute-start.10 = (bf16[32,512]{1,0:T(8,128)(2,1)}, bf16[32,512]{1,0:T(8,128)(2,1)}, u32[]{:S(2)}, u32[]{:S(2)}) collective-permute-start(bf16[32,512]{1,0:T(8,128)(2,1)} %bitcast.211), channel_id=1, source_target_pairs={{0,12},{4,0},{8,4},{12,8},{1,13},{5,1},{9,5},{13,9},{2,14},{6,2},{... | collective-permute-start | bytes 98312 | tf_op jit(solution)/shard_map/ppermute | solution.py:269
  80.0 4.3 %collective-permute-done = bf16[128,1024]{1,0:T(8,128)(2,1)S(1)} collective-permute-done((bf16[128,1024]{1,0:T(8,128)(2,1)S(1)}, bf16[128,1024]{1,0:T(8,128)(2,1)S(1)}, u32[]{:S(2)}, u32[]{:S(2)}) %collective-permute-start) | collective-permute-done | bytes 262176 | tf_op jit(solution)/shard_map/ppermute | solution.py:269
  87.2 9.1 %attention_forward.1 = bf16[512,1024]{1,0:T(8,128)(2,1)S(1)} custom-call(bf16[512,1024]{1,0:T(8,128)(2,1)S(1)} %bitcast.215, bf16[512,128]{1,0:T(8,128)(2,1)S(1)} %get-tuple-element.34.key_ref, bf16[512,128]{1,0:T(8,128)(2,1)S(1)} %get-tuple-element.33.value_ref), custom_call_target="tpu_custom_call" | custom-call | tf_op jit(solution)/shard_map/attention_forward/pallas_call | solution.py:355
  108.2 15.1 %collective-permute-start.9 = (bf16[32,512]{1,0:T(8,128)(2,1)}, bf16[32,512]{1,0:T(8,128)(2,1)}, u32[]{:S(2)}, u32[]{:S(2)}) collective-permute-start(bf16[32,512]{1,0:T(8,128)(2,1)} %bitcast.262), channel_id=1, source_target_pairs={{0,8},{4,12},{8,0},{12,4},{1,9},{5,13},{9,1},{13,5},{2,10},{6,14},... | collective-permute-start | bytes 98312 | tf_op jit(solution)/shard_map/ppermute | solution.py:269
  127.8 2.6 collective-permute-start.26
  134.6 8.9 %collective-permute-done.26 = bf16[4,32,2048]{2,1,0:T(8,128)(2,1)} collective-permute-done((bf16[4,32,2048]{2,1,0:T(8,128)(2,1)}, bf16[4,32,2048]{2,1,0:T(8,128)(2,1)}, u32[]{:S(2)}, u32[]{:S(2)}) %collective-permute-start.26) | collective-permute-done | bytes 524320 | tf_op jit(solution)/shard_map/ppermute | solution.py:273
  146.9 3.6 %collective-permute-start.13 = (bf16[4,32,512]{2,1,0:T(8,128)(2,1)S(1)}, bf16[4,32,512]{2,1,0:T(8,128)(2,1)S(1)}, u32[]{:S(2)}, u32[]{:S(2)}) collective-permute-start(bf16[4,32,512]{2,1,0:T(8,128)(2,1)S(1)} %fusion.31), channel_id=1, source_target_pairs={{0,12},{4,0},{8,4},{12,8},{1,13},{5,1},{9,5},{13,9},{2,14},{6,2},{... | collective-permute-start | bytes 393224 | tf_op jit(solution)/shard_map/ppermute | solution.py:269
  154.4 6.6 %collective-permute-done.12 = bf16[4,32,512]{2,1,0:T(8,128)(2,1)S(1)} collective-permute-done((bf16[4,32,512]{2,1,0:T(8,128)(2,1)S(1)}, bf16[4,32,512]{2,1,0:T(8,128)(2,1)S(1)}, u32[]{:S(2)}, u32[]{:S(2)}) %collective-permute-start.12) | collective-permute-done | bytes 131104 | tf_op jit(solution)/shard_map/ppermute | solution.py:269
  165.7 3.1 %pad_maximum_fusion.1 = bf16[4,4,32,2048]{3,2,1,0:T(8,128)(2,1)} fusion(bf16[1,4,32,2048]{3,2,1,0:T(8,128)(2,1)} %bitcast.55, bf16[1,4,32,2048]{3,2,1,0:T(8,128)(2,1)} %bitcast.54, bf16[1,4,32,2048]{3,2,1,0:T(8,128)(2,1)} %bitcast.53, bf16[1,4,32,2048]{3,2,1,0:T(8,128)(2,1)} %bitcast.239), kind=kLoop, calls=%fused_computation.30 | loop fusion | flops 3145728 | bytes 4194304 | tf_op jit(solution)/shard_map/stack | solution.py:291
  168.8 3.8 %gather_fusion.6 = bf16[4,4,32,2048]{3,2,1,0:T(8,128)(2,1)} fusion(bf16[4,4,32,2048]{3,2,1,0:T(8,128)(2,1)} %pad_maximum_fusion.1, s32[1024]{0:T(1024)} %pad_clamp_fusion), kind=kCustom, calls=%fused_computation.6 | custom fusion | bytes 4194320 | tf_op jit(solution)/shard_map/gather | solution.py:291
  180.4 2.8 pad_maximum_fusion
  183.1 3.8 %gather_fusion.4 = bf16[4,4,4,32,512]{4,3,2,1,0:T(8,128)(2,1)} fusion(bf16[4,4,4,32,512]{4,3,2,1,0:T(8,128)(2,1)} %pad_maximum_fusion, s32[1024]{0:T(1024)} %pad_clamp_fusion), kind=kCustom, calls=%fused_computation.4 | custom fusion | bytes 4194320 | tf_op jit(solution)/shard_map/gather | solution.py:291
  189.2 3.4 %copy.94 = bf16[4,4,32,4,512]{4,3,2,1,0:T(4,128)(2,1)S(1)} copy(bf16[4,4,32,4,512]{4,2,0,3,1:T(8,128)(2,1)} %bitcast.219) | data formatting | bytes 4194304 | tf_op jit(solution)/shard_map/transpose | solution.py:461
  218.6 12.2 %collective-permute-done.29 = bf16[1,4,32,2048]{3,2,1,0:T(8,128)(2,1)S(1)} collective-permute-done((bf16[1,4,32,2048]{3,2,1,0:T(8,128)(2,1)S(1)}, bf16[1,4,32,2048]{3,2,1,0:T(8,128)(2,1)S(1)}, u32[]{:S(2)}, u32[]{:S(2)}) %collective-permute-start.29) | collective-permute-done | bytes 524320 | tf_op jit(solution)/shard_map/ppermute | solution.py:273
  236.0 5.5 %collective-permute-done.18 = bf16[1,4,32,2048]{3,2,1,0:T(8,128)(2,1)S(1)} collective-permute-done((bf16[1,4,32,2048]{3,2,1,0:T(8,128)(2,1)S(1)}, bf16[1,4,32,2048]{3,2,1,0:T(8,128)(2,1)S(1)}, u32[]{:S(2)}, u32[]{:S(2)}) %collective-permute-start.18) | collective-permute-done | bytes 524320 | tf_op jit(solution)/shard_map/ppermute | solution.py:273
  248.5 7.8 %collective-permute-done.20 = bf16[32,2048]{1,0:T(8,128)(2,1)S(1)} collective-permute-done((bf16[32,2048]{1,0:T(8,128)(2,1)S(1)}, bf16[32,2048]{1,0:T(8,128)(2,1)S(1)}, u32[]{:S(2)}, u32[]{:S(2)}) %collective-permute-start.20) | collective-permute-done | bytes 131104 | tf_op jit(solution)/shard_map/ppermute | solution.py:269
  286.4 3.9 %convolution_convert_fusion.6.grad_ref = bf16[128,1024]{1,0:T(8,128)(2,1)S(1)} fusion(bf16[128,2048]{1,0:T(8,128)(2,1)} %bitcast.232, bf16[1024,2048]{1,0:T(8,128)(2,1)} %all-gather.3.cloned.1.call-done), kind=kOutput, calls=%fused_computation.47 | convolution fusion | flops 537001984 | bytes 4980736 | tf_op jit(solution)/shard_map/dot_general | solution.py:323
  290.3 4.5 %attention_backward.1 = (bf16[128,1024]{1,0:T(8,128)(2,1)}, bf16[512,256]{1,0:T(8,128)(2,1)S(1)}) custom-call(s32[1]{0:T(128)} %bitcast.69.block_ref, bf16[128,1024]{1,0:T(8,128)(2,1)S(1)} %copy-done.3, bf16[512,128]{1,0:T(8,128)(2,1)S(1)} %get-tuple-element.34.key_ref, bf16[512,128]{1,0:T(8,128)(2,1)S(1)} %get-tuple-element.33.value_ref, ...), custom_call_target="tpu_custom_call" | custom-call | tf_op jit(solution)/shard_map/attention_backward/pallas_call | solution.py:391
  294.8 2.8 collective-permute-start.38
  300.3 4.4 %collective-permute-done.37 = bf16[128,256]{1,0:T(8,128)(2,1)S(1)} collective-permute-done((bf16[128,256]{1,0:T(8,128)(2,1)S(1)}, bf16[128,256]{1,0:T(8,128)(2,1)S(1)}, u32[]{:S(2)}, u32[]{:S(2)}) %collective-permute-start.37) | collective-permute-done | bytes 65568 | tf_op jit(solution)/shard_map/ppermute | solution.py:269
  (235 shorter events, 129.4 us)
Async XLA Ops:
  7.2 279.1 %all-gather.3.cloned.1.call-start = ((), (), s32[]{:S(2)}) async-start(), calls=%async_computation | async-start | bytes 5242880 | tf_op jit(solution)/shard_map/all_gather | solution.py:453
  7.3 68.8 %collective-permute-start.2 = (bf16[128,1024]{1,0:T(8,128)(2,1)}, bf16[128,1024]{1,0:T(8,128)(2,1)S(1)}, u32[]{:S(2)}, u32[]{:S(2)}) collective-permute-start(bf16[128,1024]{1,0:T(8,128)(2,1)} %query_ref.1), channel_id=1, source_target_pairs={{0,12},{4,0},{8,4},{12,8},{1,13},{5,1},{9,5},{13,9},{2,14},{6,2},{... | collective-permute-start | bytes 786440 | tf_op jit(solution)/shard_map/ppermute | solution.py:269
  12.4 63.8 %collective-permute-start.1 = (bf16[128,1024]{1,0:T(8,128)(2,1)}, bf16[128,1024]{1,0:T(8,128)(2,1)S(1)}, u32[]{:S(2)}, u32[]{:S(2)}) collective-permute-start(bf16[128,1024]{1,0:T(8,128)(2,1)} %query_ref.1), channel_id=1, source_target_pairs={{0,8},{4,12},{8,0},{12,4},{1,9},{5,13},{9,1},{13,5},{2,10},{6,14},... | collective-permute-start | bytes 786440 | tf_op jit(solution)/shard_map/ppermute | solution.py:269
  13.9 33.4 %collective-permute-start.5 = (bf16[128,256]{1,0:T(8,128)(2,1)S(1)}, bf16[128,256]{1,0:T(8,128)(2,1)S(1)}, u32[]{:S(2)}, u32[]{:S(2)}) collective-permute-start(bf16[128,256]{1,0:T(8,128)(2,1)S(1)} %constant_dynamic-update-slice_fusion), channel_id=1, source_target_pairs={{0,12},{4,0},{8,4},{12,8},{1,13},{5,1},{9,5},{13,9},{2,14},{6,2},{... | collective-permute-start | bytes 196616 | tf_op jit(solution)/shard_map/ppermute | solution.py:269
  14.5 55.6 %collective-permute-start.4 = (bf16[128,256]{1,0:T(8,128)(2,1)S(1)}, bf16[128,256]{1,0:T(8,128)(2,1)S(1)}, u32[]{:S(2)}, u32[]{:S(2)}) collective-permute-start(bf16[128,256]{1,0:T(8,128)(2,1)S(1)} %constant_dynamic-update-slice_fusion), channel_id=1, source_target_pairs={{0,8},{4,12},{8,0},{12,4},{1,9},{5,13},{9,1},{13,5},{2,10},{6,14},... | collective-permute-start | bytes 196616 | tf_op jit(solution)/shard_map/ppermute | solution.py:269
  17.0 54.7 %collective-permute-start.3 = (bf16[128,256]{1,0:T(8,128)(2,1)S(1)}, bf16[128,256]{1,0:T(8,128)(2,1)S(1)}, u32[]{:S(2)}, u32[]{:S(2)}) collective-permute-start(bf16[128,256]{1,0:T(8,128)(2,1)S(1)} %constant_dynamic-update-slice_fusion), channel_id=1, source_target_pairs={{0,4},{4,8},{8,12},{12,0},{1,5},{5,9},{9,13},{13,1},{2,6},{6,10},{... | collective-permute-start | bytes 196616 | tf_op jit(solution)/shard_map/ppermute | solution.py:269
  47.3 37.0 %collective-permute-start = (bf16[128,1024]{1,0:T(8,128)(2,1)S(1)}, bf16[128,1024]{1,0:T(8,128)(2,1)S(1)}, u32[]{:S(2)}, u32[]{:S(2)}) collective-permute-start(bf16[128,1024]{1,0:T(8,128)(2,1)S(1)} %copy-done.3), channel_id=1, source_target_pairs={{0,4},{4,8},{8,12},{12,0},{1,5},{5,9},{9,13},{13,1},{2,6},{6,10},{... | collective-permute-start | bytes 786440 | tf_op jit(solution)/shard_map/ppermute | solution.py:269
  70.0 38.2 %collective-permute-start.24 = (bf16[32,2048]{1,0:T(8,128)(2,1)S(1)}, bf16[32,2048]{1,0:T(8,128)(2,1)}, u32[]{:S(2)}, u32[]{:S(2)}) collective-permute-start(bf16[32,2048]{1,0:T(8,128)(2,1)S(1)} %copy-done.15), channel_id=1, source_target_pairs={{0,12},{4,0},{8,4},{12,8},{1,13},{5,1},{9,5},{13,9},{2,14},{6,2},{... | collective-permute-start | bytes 393224 | tf_op jit(solution)/shard_map/ppermute | solution.py:269
  71.6 51.7 %collective-permute-start.23 = (bf16[32,2048]{1,0:T(8,128)(2,1)S(1)}, bf16[32,2048]{1,0:T(8,128)(2,1)}, u32[]{:S(2)}, u32[]{:S(2)}) collective-permute-start(bf16[32,2048]{1,0:T(8,128)(2,1)S(1)} %copy-done.15), channel_id=1, source_target_pairs={{0,8},{4,12},{8,0},{12,4},{1,9},{5,13},{9,1},{13,5},{2,10},{6,14},... | collective-permute-start | bytes 393224 | tf_op jit(solution)/shard_map/ppermute | solution.py:269
  76.1 47.3 %collective-permute-start.22 = (bf16[32,2048]{1,0:T(8,128)(2,1)S(1)}, bf16[32,2048]{1,0:T(8,128)(2,1)}, u32[]{:S(2)}, u32[]{:S(2)}) collective-permute-start(bf16[32,2048]{1,0:T(8,128)(2,1)S(1)} %copy-done.15), channel_id=1, source_target_pairs={{0,4},{4,8},{8,12},{12,0},{1,5},{5,9},{9,13},{13,1},{2,6},{6,10},{... | collective-permute-start | bytes 393224 | tf_op jit(solution)/shard_map/ppermute | solution.py:269
  76.2 56.7 %collective-permute-start.10 = (bf16[32,512]{1,0:T(8,128)(2,1)}, bf16[32,512]{1,0:T(8,128)(2,1)}, u32[]{:S(2)}, u32[]{:S(2)}) collective-permute-start(bf16[32,512]{1,0:T(8,128)(2,1)} %bitcast.211), channel_id=1, source_target_pairs={{0,12},{4,0},{8,4},{12,8},{1,13},{5,1},{9,5},{13,9},{2,14},{6,2},{... | collective-permute-start | bytes 98312 | tf_op jit(solution)/shard_map/ppermute | solution.py:269
  98.1 32.3 %collective-permute-start.6 = (bf16[2,4,32,512]{3,2,1,0:T(8,128)(2,1)S(1)}, bf16[2,4,32,512]{3,2,1,0:T(8,128)(2,1)}, u32[]{:S(2)}, u32[]{:S(2)}) collective-permute-start(bf16[2,4,32,512]{3,2,1,0:T(8,128)(2,1)S(1)} %dynamic-slice_bitcast_fusion.2), channel_id=1, source_target_pairs={{0,1},{1,0},{2,3},{3,2},{4,5},{5,4},{6,7},{7,6},{8,9},{9,8},{10,11... | collective-permute-start | bytes 786440 | tf_op jit(solution)/shard_map/ppermute | solution.py:273
  108.2 24.7 %collective-permute-start.9 = (bf16[32,512]{1,0:T(8,128)(2,1)}, bf16[32,512]{1,0:T(8,128)(2,1)}, u32[]{:S(2)}, u32[]{:S(2)}) collective-permute-start(bf16[32,512]{1,0:T(8,128)(2,1)} %bitcast.262), channel_id=1, source_target_pairs={{0,8},{4,12},{8,0},{12,4},{1,9},{5,13},{9,1},{13,5},{2,10},{6,14},... | collective-permute-start | bytes 98312 | tf_op jit(solution)/shard_map/ppermute | solution.py:269
  127.8 15.7 %collective-permute-start.26 = (bf16[4,32,2048]{2,1,0:T(8,128)(2,1)}, bf16[4,32,2048]{2,1,0:T(8,128)(2,1)}, u32[]{:S(2)}, u32[]{:S(2)}) collective-permute-start(bf16[4,32,2048]{2,1,0:T(8,128)(2,1)} %gather_fusion.5), channel_id=1, source_target_pairs={{0,2},{1,3},{2,0},{3,1},{4,6},{5,7},{6,4},{7,5},{8,10},{9,11},{10,... | collective-permute-start | bytes 1572872 | tf_op jit(solution)/shard_map/ppermute | solution.py:273
  134.4 31.3 %collective-permute-start.25 = (bf16[4,32,2048]{2,1,0:T(8,128)(2,1)}, bf16[4,32,2048]{2,1,0:T(8,128)(2,1)}, u32[]{:S(2)}, u32[]{:S(2)}) collective-permute-start(bf16[4,32,2048]{2,1,0:T(8,128)(2,1)} %gather_fusion.5), channel_id=1, source_target_pairs={{0,1},{1,0},{2,3},{3,2},{4,5},{5,4},{6,7},{7,6},{8,9},{9,8},{10,11... | collective-permute-start | bytes 1572872 | tf_op jit(solution)/shard_map/ppermute | solution.py:273
  143.4 22.3 %collective-permute-start.27 = (bf16[4,32,2048]{2,1,0:T(8,128)(2,1)}, bf16[4,32,2048]{2,1,0:T(8,128)(2,1)}, u32[]{:S(2)}, u32[]{:S(2)}) collective-permute-start(bf16[4,32,2048]{2,1,0:T(8,128)(2,1)} %collective-permute-done.26), channel_id=1, source_target_pairs={{0,1},{1,0},{2,3},{3,2},{4,5},{5,4},{6,7},{7,6},{8,9},{9,8},{10,11... | collective-permute-start | bytes 1572872 | tf_op jit(solution)/shard_map/ppermute | solution.py:273
  164.5 13.6 %collective-permute-start.15 = (bf16[4,4,32,512]{3,2,1,0:T(8,128)(2,1)}, bf16[4,4,32,512]{3,2,1,0:T(8,128)(2,1)}, u32[]{:S(2)}, u32[]{:S(2)}) collective-permute-start(bf16[4,4,32,512]{3,2,1,0:T(8,128)(2,1)} %gather_fusion.3), channel_id=1, source_target_pairs={{0,2},{1,3},{2,0},{3,1},{4,6},{5,7},{6,4},{7,5},{8,10},{9,11},{10,... | collective-permute-start | bytes 1572872 | tf_op jit(solution)/shard_map/ppermute | solution.py:273
  165.7 14.6 %collective-permute-start.14 = (bf16[4,4,32,512]{3,2,1,0:T(8,128)(2,1)}, bf16[4,4,32,512]{3,2,1,0:T(8,128)(2,1)}, u32[]{:S(2)}, u32[]{:S(2)}) collective-permute-start(bf16[4,4,32,512]{3,2,1,0:T(8,128)(2,1)} %gather_fusion.3), channel_id=1, source_target_pairs={{0,1},{1,0},{2,3},{3,2},{4,5},{5,4},{6,7},{7,6},{8,9},{9,8},{10,11... | collective-permute-start | bytes 1572872 | tf_op jit(solution)/shard_map/ppermute | solution.py:273
  216.0 14.8 %collective-permute-start.29 = (bf16[1,4,32,2048]{3,2,1,0:T(8,128)(2,1)S(1)}, bf16[1,4,32,2048]{3,2,1,0:T(8,128)(2,1)S(1)}, u32[]{:S(2)}, u32[]{:S(2)}) collective-permute-start(bf16[1,4,32,2048]{3,2,1,0:T(8,128)(2,1)S(1)} %constant_dynamic-slice_fusion.5), channel_id=1, source_target_pairs={{0,2},{1,3},{2,0},{3,1},{4,6},{5,7},{6,4},{7,5},{8,10},{9,11},{10,... | collective-permute-start | bytes 1572872 | tf_op jit(solution)/shard_map/ppermute | solution.py:273
  217.3 24.2 %collective-permute-start.18 = (bf16[1,4,32,2048]{3,2,1,0:T(8,128)(2,1)S(1)}, bf16[1,4,32,2048]{3,2,1,0:T(8,128)(2,1)S(1)}, u32[]{:S(2)}, u32[]{:S(2)}) collective-permute-start(bf16[1,4,32,2048]{3,2,1,0:T(8,128)(2,1)S(1)} %constant_dynamic-slice_fusion.8), channel_id=1, source_target_pairs={{0,2},{1,3},{2,0},{3,1},{4,6},{5,7},{6,4},{7,5},{8,10},{9,11},{10,... | collective-permute-start | bytes 1572872 | tf_op jit(solution)/shard_map/ppermute | solution.py:273
  231.0 13.7 %collective-permute-start.32 = (bf16[32,2048]{1,0:T(8,128)(2,1)S(1)}, bf16[32,2048]{1,0:T(8,128)(2,1)S(1)}, u32[]{:S(2)}, u32[]{:S(2)}) collective-permute-start(bf16[32,2048]{1,0:T(8,128)(2,1)S(1)} %get-tuple-element.25), channel_id=1, source_target_pairs={{0,12},{4,0},{8,4},{12,8},{1,13},{5,1},{9,5},{13,9},{2,14},{6,2},{... | collective-permute-start | bytes 393224 | tf_op jit(solution)/shard_map/ppermute | solution.py:269
  233.0 13.6 %collective-permute-start.31 = (bf16[32,2048]{1,0:T(8,128)(2,1)S(1)}, bf16[32,2048]{1,0:T(8,128)(2,1)S(1)}, u32[]{:S(2)}, u32[]{:S(2)}) collective-permute-start(bf16[32,2048]{1,0:T(8,128)(2,1)S(1)} %get-tuple-element.26), channel_id=1, source_target_pairs={{0,8},{4,12},{8,0},{12,4},{1,9},{5,13},{9,1},{13,5},{2,10},{6,14},... | collective-permute-start | bytes 393224 | tf_op jit(solution)/shard_map/ppermute | solution.py:269
  257.2 14.5 %collective-permute-start.34 = (bf16[32,2048]{1,0:T(8,128)(2,1)}, bf16[32,2048]{1,0:T(8,128)(2,1)}, u32[]{:S(2)}, u32[]{:S(2)}) collective-permute-start(bf16[32,2048]{1,0:T(8,128)(2,1)} %get-tuple-element.19), channel_id=1, source_target_pairs={{0,2},{1,3},{2,0},{3,1},{4,6},{5,7},{6,4},{7,5},{8,10},{9,11},{10,... | collective-permute-start | bytes 393224 | tf_op jit(solution)/shard_map/ppermute | solution.py:273
  257.8 17.8 %collective-permute-start.33 = (bf16[32,2048]{1,0:T(8,128)(2,1)}, bf16[32,2048]{1,0:T(8,128)(2,1)}, u32[]{:S(2)}, u32[]{:S(2)}) collective-permute-start(bf16[32,2048]{1,0:T(8,128)(2,1)} %get-tuple-element.19), channel_id=1, source_target_pairs={{0,1},{1,0},{2,3},{3,2},{4,5},{5,4},{6,7},{7,6},{8,9},{9,8},{10,11... | collective-permute-start | bytes 393224 | tf_op jit(solution)/shard_map/ppermute | solution.py:273
  (51 other events, 712.7 us)
Sparse Core Ops, SparseCore 0:
  19.1 101.7 all-gather.2

commit v2 on v0

--- a/solution.py
+++ b/solution.py
@@ -1,6 +1,8 @@
 import jax
 import jax.numpy as jnp
 from jax import lax
+from jax.experimental import pallas as pl
+from jax.experimental.pallas import tpu as pltpu
 from jax.sharding import PartitionSpec as P
 
 HEAD_SIZE = 128
@@ -33,7 +35,7 @@
     return lax.all_to_all(buffer, ("ctx", "exp"), split_axis=0, concat_axis=0, tiled=True)
 
 
-def local(
+def local_routed(
     resid,
     query,
     key,
@@ -260,6 +262,513 @@
     )
 
 
+F32 = jnp.float32
+BF16 = jnp.bfloat16
+LOG2E = 1.4426950408889634
+SETS = (0, 2, 1, 3)
+
+
+def shifted(x, shift, count):
+    return lax.ppermute(x, "ctx", [(i, (i + shift) % count) for i in range(count)])
+
+
+def swapped(x, bit):
+    return lax.ppermute(x, "exp", [(i, i ^ bit) for i in range(4)])
+
+
+def pick(x, index, axis):
+    return lax.dynamic_index_in_dim(x, index, axis, keepdims=False)
+
+
+def nt(a, b):
+    return lax.dot_general(a, b, (((1,), (1,)), ((), ())), preferred_element_type=F32)
+
+
+def tn(a, b):
+    return lax.dot_general(a, b, (((0,), (0,)), ((), ())), preferred_element_type=F32)
+
+
+def nn(a, b):
+    return lax.dot_general(a, b, (((1,), (0,)), ((), ())), preferred_element_type=F32)
+
+
+def wrap(value, count):
+    return lax.rem(value + count, count)
+
+
+def run_kernel(body, name, place, args, outs, scratch=(), flops=0, limit=40):
+    vmem = pl.BlockSpec(memory_space=pltpu.VMEM)
+    shapes = [jax.ShapeDtypeStruct(shape, dtype) for shape, dtype in outs]
+    moved = sum(x.size * x.dtype.itemsize for x in list(args) + shapes)
+    return pl.pallas_call(
+        body,
+        in_specs=[pl.BlockSpec(memory_space=pltpu.SMEM)] + [vmem] * len(args),
+        out_specs=[vmem] * len(outs),
+        out_shape=shapes,
+        scratch_shapes=[pltpu.VMEM(shape, dtype) for shape, dtype in scratch],
+        compiler_params=pltpu.CompilerParams(vmem_limit_bytes=limit << 20),
+        cost_estimate=pl.CostEstimate(flops=flops, bytes_accessed=moved, transcendentals=0),
+        name=name,
+    )(place, *args)
+
+
+def attend(place, query_parts, pair_parts, out_proj):
+    n = len(query_parts)
+    rows, width = query_parts[0].shape
+    tok = rows // 4
+    cols = out_proj.shape[1]
+    heads = width // HEAD_SIZE
+    factor = HEAD_SIZE ** (-0.5) * LOG2E
+
+    def body(place_ref, *refs):
+        q_refs, p_refs, proj_ref = refs[:n], refs[n : 2 * n], refs[2 * n]
+        mix_ref, own_ref, keep_ref, send_ref, qs, ks, vs, ps = refs[2 * n + 1 :]
+        c, e = place_ref[0], place_ref[1]
+        for d in range(n):
+            at = pl.multiple_of(wrap(c - d, n) * rows, rows)
+            qs[pl.ds(at, rows), :] = q_refs[d][...]
+            ks[pl.ds(at, rows), :] = p_refs[d][:, :HEAD_SIZE]
+            vs[pl.ds(at, rows), :] = p_refs[d][:, HEAD_SIZE:]
+        below = lax.broadcasted_iota(jnp.int32, (rows, rows), 1) <= lax.broadcasted_iota(
+            jnp.int32, (rows, rows), 0
+        )
+        core, line = lax.rem(e, 2), lax.div(e, 2)
+        for b in range(n):
+            lo, hi = b * rows, (b + 1) * rows
+            for head in range(heads):
+                at = slice(head * HEAD_SIZE, (head + 1) * HEAD_SIZE)
+                scores = nt(qs[lo:hi, at], ks[:hi, :])
+                last = jnp.where(below, scores[:, lo:], NEG)
+                scores = jnp.concatenate([scores[:, :lo], last], 1) if b else last
+                peak = jnp.max(scores, -1, keepdims=True)
+                weights = jnp.exp2((scores - peak) * factor)
+                total = jnp.sum(weights, -1, keepdims=True)
+                mix_ref[lo:hi, at] = (nn(weights.astype(BF16), vs[:hi, :]) / total).astype(BF16)
+            ps[...] = nn(mix_ref[lo:hi, :], proj_ref[...]).astype(BF16)
+            d = wrap(c - b, n)
+            for turn in range(2):
+                base = (line + turn - 2 * turn * line) * 2
+                keep_ref[turn, d] = ps[pl.ds(pl.multiple_of((base + core) * tok, tok), tok), :]
+                send_ref[turn, d] = ps[pl.ds(pl.multiple_of((base + 1 - core) * tok, tok), tok), :]
+        own_ref[...] = mix_ref[pl.ds(pl.multiple_of(c * rows, rows), rows), :]
+
+    return run_kernel(
+        body,
+        "attend",
+        place,
+        [*query_parts, *pair_parts, out_proj],
+        [
+            ((n * rows, width), BF16),
+            ((rows, width), BF16),
+            ((2, n, tok, cols), BF16),
+            ((2, n, tok, cols), BF16),
+        ],
+        [
+            ((n * rows, width), BF16),
+            ((n * rows, HEAD_SIZE), BF16),
+            ((n * rows, HEAD_SIZE), BF16),
+            ((rows, cols), BF16),
+        ],
+        flops=4 * n * rows * n * rows * width,
+    )
+
+
+def hidden_rows(place, keep, received, crossed, resid_parts):
+    n = len(resid_parts)
+
+    def body(place_ref, keep_ref, received_ref, crossed_ref, *refs):
+        for d in range(n):
+            total = keep_ref[0, d].astype(F32) + received_ref[0, d].astype(F32)
+            total = total + crossed_ref[d].astype(F32) + refs[d][...].astype(F32)
+            refs[n][d] = total.astype(BF16)
+
+    return run_kernel(
+        body, "hidden_rows", place, [keep, received, crossed, *resid_parts], [(crossed.shape, BF16)]
+    )[0]
+
+
+def grad_rows_of(place, grad_sets, w_down, width):
+    n, tok = grad_sets[0].shape[:2]
+    total = 4 * n * tok
+    experts = 4 * n
+
+    def body(place_ref, *refs):
+        down_ref, rows_ref, gate_ref, act_ref = refs[4:]
+        expert = place_ref[0] * 4 + place_ref[1]
+        lane = lax.broadcasted_iota(jnp.int32, (tok, 128), 1)
+        wanted = (lane == expert) | (lane == expert + experts)
+        for s in range(4):
+            for d in range(n):
+                at = s * n * tok + (-d) % n * tok
+                gate = jnp.where(wanted, refs[s][d, :, width:].astype(F32), 0.0)
+                gate = jnp.sum(gate, -1, keepdims=True)
+                gate_ref[at : at + tok, :] = gate
+                rows_ref[at : at + tok, :] = (refs[s][d, :, :width].astype(F32) * gate).astype(BF16)
+        act_ref[...] = nt(rows_ref[...], down_ref[...])
+
+    return run_kernel(
+        body,
+        "grad_rows",
+        place,
+        [*grad_sets, w_down],
+        [((total, width), BF16), ((total, 1), F32), ((total, w_down.shape[0]), F32)],
+        flops=2 * total * width * w_down.shape[0],
+    )
+
+
+def expert_rows(place, hidden_sets, act_grad, norm_gain, w_gate, w_up):
+    n, tok, cols = hidden_sets[0][0].shape
+    width, hidden_units = w_gate.shape
+    group = n * tok
+    total = 4 * group
+
+    def body(place_ref, *refs):
+        pieces = refs[: 4 * n]
+        act_grad_ref, gain_ref, gate_ref, up_ref = refs[4 * n : 4 * n + 4]
+        normed_ref, act_ref, gate_grad_ref, up_grad_ref, own_ref = refs[4 * n + 4 : 4 * n + 9]
+        grads, hid = refs[4 * n + 9 : 4 * n + 13], refs[4 * n + 13]
+        c = place_ref[0]
+        for s in range(4):
+            for d in range(n):
+                at = pl.multiple_of(wrap(c - d, n) * cols, cols)
+                for t in range(n):
+                    row = s * group + (-(d + t)) % n * tok
+                    hid[row : row + tok, pl.ds(at, cols)] = pieces[s * n + d][t]
+            rows = slice(s * group, (s + 1) * group)
+            value = hid[rows, :].astype(F32)
+            inv_rms = lax.rsqrt(jnp.mean(value * value, -1, keepdims=True) + EPS)
+            normed_ref[rows, :] = (value * inv_rms * gain_ref[...]).astype(BF16)
+        own_ref[...] = hid[:tok, :]
+        pre_gate = nn(normed_ref[...], gate_ref[...])
+        pre_up = nn(normed_ref[...], up_ref[...])
+        sig = jax.nn.sigmoid(pre_gate)
+        act_ref[...] = (pre_gate * sig * pre_up).astype(BF16)
+        act_grad_value = act_grad_ref[...]
+        up_grad_ref[...] = (act_grad_value * pre_gate * sig).astype(BF16)
+        gate_grad_ref[...] = (
+            act_grad_value * pre_up * sig * (1.0 + pre_gate * (1.0 - sig))
+        ).astype(BF16)
+        for j in range(n):
+            at = slice(j * cols, (j + 1) * cols)
+            part = nt(gate_grad_ref[...], gate_ref[at, :]) + nt(up_grad_ref[...], up_ref[at, :])
+            for s in range(4):
+                block = part[s * group : (s + 1) * group].astype(BF16)
+                grads[s][:, :, at] = block.reshape(n, tok, cols)
+
+    units = ((total, hidden_units), BF16)
+    return run_kernel(
+        body,
+        "expert_rows",
+        place,
+        [*sum(hidden_sets, []), act_grad, norm_gain.reshape(1, width), w_gate, w_up],
+        [((total, width), BF16), units, units, units, ((tok, width), BF16)]
+        + [((n, tok, width), BF16)] * 4,
+        [((total, width), BF16)],
+        flops=8 * total * width * hidden_units,
+    )
+
+
+def weighted_rows(place, act_rows, gate, w_down, n):
+    total = act_rows.shape[0]
+    width = w_down.shape[1]
+    group, cols = total // 4, width // n
+
+    def body(place_ref, act_ref, gate_ref, down_ref, *outs):
+        for j in range(n):
+            at = slice(j * cols, (j + 1) * cols)
+            part = nn(act_ref[...], down_ref[:, at]).astype(BF16).astype(F32) * gate_ref[...]
+            for s in range(4):
+                block = part[s * group : (s + 1) * group].astype(BF16)
+                outs[s][:, :, at] = block.reshape(n, group // n, cols)
+
+    return run_kernel(
+        body,
+        "weighted_rows",
+        place,
+        [act_rows, gate, w_down],
+        [((n, group // n, width), BF16)] * 4,
+        flops=2 * total * width * w_down.shape[0],
+    )
+
+
+def sum_back(parts):
+    n = parts[0].shape[0]
+    order = sorted(range(n), key=lambda j: -min(j, n - j))
+    far, near = swapped(parts[3], 1), swapped(parts[2], 1)
+
+    def add(*xs):
+        return sum([x.astype(F32) for x in xs[1:]], xs[0].astype(F32)).astype(BF16)
+
+    crossed = {j: swapped(add(parts[1][j], far[j]), 2) for j in order}
+    sums = {j: add(parts[0][j], near[j], crossed[j]) for j in order}
+    received = {j: shifted(sums[j], j, n) for j in order if j}
+    return [sums[0]] + [received[j] for j in range(1, n)]
+
+
+def norm_backward(place, summed, hidden, grad_out, norm_gain, cols):
+    n = len(summed)
+    tok, width = hidden.shape
+
+    def body(place_ref, *refs):
+        hidden_ref, grad_ref, gain_ref = refs[n : n + 3]
+        out_ref, part_ref, cuts = refs[n + 3], refs[n + 4], refs[n + 5 :]
+        c = place_ref[0]
+        normed_grad = sum([r[...].astype(F32) for r in refs[1:n]], refs[0][...].astype(F32))
+        value = hidden_ref[...].astype(F32)
+        inv_rms = lax.rsqrt(jnp.mean(value * value, -1, keepdims=True) + EPS)
+        unit_rows = value * inv_rms
+        part_ref[...] = jnp.sum(normed_grad * unit_rows, 0, keepdims=True)
+        scaled = gain_ref[...] * normed_grad
+        mean = jnp.mean(scaled * unit_rows, -1, keepdims=True)
+        grad = grad_ref[...].astype(F32) + inv_rms * (scaled - unit_rows * mean)
+        out_ref[...] = grad.astype(BF16)
+        for d in range(n):
+            cuts[d][...] = out_ref[:, pl.ds(pl.multiple_of(wrap(c + d, n) * cols, cols), cols)]
+
+    return run_kernel(
+        body,
+        "norm_backward",
+        place,
+        [*summed, hidden, grad_out, norm_gain.reshape(1, width)],
+        [((tok, width), BF16), ((1, width), F32)] + [((tok, cols), BF16)] * n,
+    )
+
+
+def layer_rows(place, summed, hidden):
+    def body(place_ref, *refs):
+        total = refs[-2][...].astype(F32)
+        for r in refs[:-2]:
+            total = total + r[...].astype(F32)
+        refs[-1][...] = total.astype(BF16)
+
+    return run_kernel(body, "layer_rows", place, [*summed, hidden], [(hidden.shape, BF16)])[0]
+
+
+def attend_backward(place, grad_parts, out_proj, proj_near, proj_far, query, pair_parts, mix):
+    n = len(pair_parts)
+    rows, width = query.shape
+    tok = rows // 4
+    cols = out_proj.shape[1]
+    heads = width // HEAD_SIZE
+    half = width // 2
+    scale = HEAD_SIZE ** (-0.5)
+
+    def body(place_ref, *refs):
+        g_refs, proj_ref = refs[:4], refs[4]
+        near, far = refs[5 : 4 + n], refs[4 + n : 3 + 2 * n]
+        query_ref = refs[3 + 2 * n]
+        p_refs = refs[4 + 2 * n : 4 + 3 * n]
+        mix_ref, dq_ref = refs[4 + 3 * n : 6 + 3 * n]
+        outs = refs[6 + 3 * n : 6 + 4 * n]
+        gs, acc, qs, ms, ks, vs, score_half, prob_half = refs[6 + 4 * n :]
+        c, e, g = place_ref[0], place_ref[1], place_ref[2]
+        core, line = lax.rem(e, 2), lax.div(e, 2)
+        for r in range(4):
+            low, high = r % 2, r // 2
+            other = (line + high - 2 * high * line) * 2 + core + low - 2 * low * core
+            gs[pl.ds(pl.multiple_of(other * tok, tok), tok), :] = g_refs[r][...]
+
+        def columns(d):
+            return gs[:, pl.ds(pl.multiple_of(wrap(c - d, n) * cols, cols), cols)]
+
+        acc[...] = nt(columns(0), proj_ref[...])
+        here = pl.ds(pl.multiple_of(g * half, half), half)
+        there = pl.ds(pl.multiple_of((1 - g) * half, half), half)
+        acc[:, here] += sum([nt(columns(d), near[d - 1][...]) for d in range(1, n)])
+        acc[:, there] += sum([nt(columns(d), far[d - 1][...]) for d in range(1, n)])
+        key_pos = lax.broadcasted_iota(jnp.int32, (rows, n * rows), 1)
+        visible = (key_pos <= lax.broadcasted_iota(jnp.int32, (rows, n * rows), 0)) | (
+            (key_pos >= rows) & (key_pos < (c + 1) * rows)
+        )
+        for d in range(n):
+            ks[d * rows : (d + 1) * rows, :] = p_refs[d][:, :HEAD_SIZE]
+            vs[d * rows : (d + 1) * rows, :] = p_refs[d][:, HEAD_SIZE:]
+        for head in range(heads):
+            at = slice(head * HEAD_SIZE, (head + 1) * HEAD_SIZE)
+            rs = slice(head * rows, (head + 1) * rows)
+            grad = acc[:, at].astype(BF16)
+            qs[rs, :] = query_ref[:, at]
+            ms[rs, :] = grad
+            scores = jnp.where(visible, nt(query_ref[:, at], ks[...]), NEG)
+            peak = jnp.max(scores, -1, keepdims=True)
+            weights = jnp.exp2((scores - peak) * (scale * LOG2E))
+            prob = weights * (1.0 / jnp.sum(weights, -1, keepdims=True))
+            delta = jnp.sum(grad.astype(F32) * mix_ref[:, at].astype(F32), -1, keepdims=True)
+            score_half[rs, :] = (prob * (nt(grad, vs[...]) - delta)).astype(BF16)
+            prob_half[rs, :] = prob.astype(BF16)
+            dq_ref[:, at] = (nn(score_half[rs, :], ks[...]) * scale).astype(BF16)
+        key_sum = (tn(score_half[...], qs[...]) * scale).astype(BF16)
+        value_sum = tn(prob_half[...], ms[...]).astype(BF16)
+        for j in range(n):
+            rs = slice((-j) % n * rows, ((-j) % n + 1) * rows)
+            outs[j][:, :HEAD_SIZE] = key_sum[rs]
+            outs[j][:, HEAD_SIZE:] = value_sum[rs]
+
+    stacked = ((heads * rows, HEAD_SIZE), BF16)
+    keys = ((n * rows, HEAD_SIZE), BF16)
+    halves = ((heads * rows, n * rows), BF16)
+    return run_kernel(
+        body,
+        "attend_backward",
+        place,
+        [*grad_parts, out_proj, *proj_near, *proj_far, query, *pair_parts, mix],
+        [((rows, width), BF16)] + [((rows, 2 * HEAD_SIZE), BF16)] * n,
+        [((rows, n * cols), BF16), ((rows, width), F32), stacked, stacked, keys, keys, halves, halves],
+        flops=2 * rows * width * (n * cols + 5 * n * rows),
+    )
+
+
+def proj_grad(place, mix_all, cut_sets):
+    n, tok, cols = cut_sets[0].shape
+    width = mix_all.shape[1]
+
+    def body(place_ref, mix_ref, *refs):
+        out_ref, rows_ref = refs[4], refs[5]
+        c, e = place_ref[0], place_ref[1]
+        core, line = lax.rem(e, 2), lax.div(e, 2)
+        for r in range(4):
+            low, high = r % 2, r // 2
+            other = (line + high - 2 * high * line) * 2 + core + low - 2 * low * core
+            for d in range(n):
+                at = pl.multiple_of((wrap(c - d, n) * 4 + other) * tok, tok)
+                rows_ref[pl.ds(at, tok), :] = refs[r][d]
+        out_ref[...] = tn(mix_ref[...], rows_ref[...]).astype(BF16)
+
+    return run_kernel(
+        body,
+        "proj_grad",
+        place,
+        [mix_all, *cut_sets],
+        [((width, cols), BF16)],
+        [((4 * n * tok, cols), BF16)],
+        flops=8 * n * tok * cols * width,
+    )[0]
+
+
+def local_dense(
+    resid,
+    query,
+    key,
+    value,
+    out_proj,
+    norm_gain,
+    w_gate,
+    w_up,
+    w_down,
+    routes,
+    gate_weights,
+    grad_out,
+):
+    n = lax.axis_size("ctx")
+    c, e, g = lax.axis_index("ctx"), lax.axis_index("exp"), lax.axis_index("groups")
+    place = jnp.stack([c, e, g]).astype(jnp.int32)
+    tok, width = resid.shape
+    cols = out_proj.shape[1]
+    experts = 4 * n
+
+    def to_all(x):
+        return [x] + [shifted(x, d, n) for d in range(1, n)]
+
+    pair_parts = to_all(jnp.concatenate([key, value], 1))
+    query_parts = to_all(query)
+    resid_cut = resid.reshape(tok, n, cols)
+    resid_parts = [pick(resid_cut, c, 1)] + [
+        shifted(pick(resid_cut, wrap(c + d, n), 1), d, n) for d in range(1, n)
+    ]
+
+    gates = jnp.sum(
+        jnp.where(
+            routes[:, :, None] == jnp.arange(experts, dtype=jnp.int32), gate_weights[:, :, None], 0.0
+        ),
+        1,
+    )
+    gate_high = lax.reduce_precision(gates, 8, 7)
+    payload = jnp.concatenate(
+        [
+            grad_out,
+            gate_high.astype(BF16),
+            (gates - gate_high).astype(BF16),
+            jnp.zeros((tok, 128 - 2 * experts), BF16),
+        ],
+        1,
+    )
+    payload, proj_half, *_ = lax.optimization_barrier(
+        (payload, lax.dynamic_slice_in_dim(out_proj, g * (out_proj.shape[0] // 2), out_proj.shape[0] // 2, 0))
+        + tuple(query_parts[1:])
+    )
+    grad_own = jnp.stack(to_all(payload))
+    grad_line = swapped(grad_own, 2)
+    grad_sets = [grad_own, grad_line, swapped(grad_own, 1), swapped(grad_line, 1)]
+
+    proj_near = to_all(proj_half)[1:]
+    proj_far = [lax.ppermute(x, "groups", [(0, 1), (1, 0)]) for x in proj_near]
+
+    mix_all, mix, keep, send = attend(place, query_parts, pair_parts, out_proj)
+    received = swapped(send, 1)
+    crossed = swapped((keep[1].astype(F32) + received[1].astype(F32)).astype(BF16), 2)
+    hidden_own = to_all(hidden_rows(place, keep, received, crossed, resid_parts))
+    hidden_line = [swapped(x, 2) for x in hidden_own]
+    hidden_sets = [hidden_own, hidden_line] + [
+        [swapped(x, 1) for x in xs] for xs in (hidden_own, hidden_line)
+    ]
+
+    grad_rows, gate, act_grad = grad_rows_of(place, grad_sets, w_down[0], width)
+    normed, act_rows, gate_grad, up_grad, hidden, *row_grads = expert_rows(
+        place, hidden_sets, act_grad, norm_gain, w_gate[0], w_up[0]
+    )
+    summed = sum_back(row_grads)
+    grad_resid, gain_part, *cuts = norm_backward(place, summed, hidden, grad_out, norm_gain, cols)
+
+    near = swapped(grad_resid, 2)
+    grad_parts = [grad_resid, swapped(grad_resid, 1), near, swapped(near, 1)]
+    grad_query, *pairs = attend_backward(
+        place, grad_parts, out_proj, proj_near, proj_far, query, pair_parts, mix
+    )
+    pair_sum = sum(
+        [shifted(pairs[j], j, n).astype(F32) for j in range(1, n)], pairs[0].astype(F32)
+    ).astype(BF16)
+
+    cut_own = jnp.stack([cuts[0]] + [shifted(cuts[d], d, n) for d in range(1, n)])
+    cut_line = swapped(cut_own, 2)
+    cut_sets = [cut_own, swapped(cut_own, 1), cut_line, swapped(cut_line, 1)]
+    grad_out_proj = proj_grad(place, mix_all, cut_sets)
+
+    grad_gain = gain_part.reshape(-1, 128)
+    for bit in (1, 2):
+        grad_gain = grad_gain + swapped(grad_gain, bit)
+    grad_gain = sum([shifted(grad_gain, d, n) for d in range(1, n)], grad_gain).reshape(width)
+
+    layer_out = layer_rows(
+        place, sum_back(weighted_rows(place, act_rows, gate, w_down[0], n)), hidden
+    )
+    return (
+        layer_out,
+        grad_resid,
+        grad_query,
+        pair_sum[:, :HEAD_SIZE],
+        pair_sum[:, HEAD_SIZE:],
+        grad_out_proj,
+        grad_gain,
+        tn(normed, gate_grad).astype(BF16)[None],
+        tn(normed, up_grad).astype(BF16)[None],
+        tn(act_rows, grad_rows).astype(BF16)[None],
+    )
+
+
+def local(*args):
+    key, w_gate, routes = args[2], args[6], args[9]
+    ctx_count, exp_count = lax.axis_size("ctx"), lax.axis_size("exp")
+    expert_total = w_gate.shape[0] * ctx_count * exp_count
+    dense = (
+        2 * routes.shape[1] >= expert_total
+        and w_gate.shape[0] == 1
+        and key.shape[1] == HEAD_SIZE
+        and exp_count == 4
+        and lax.axis_size("groups") == 2
+    )
+    return (local_dense if dense else local_routed)(*args)
+
+
 def solution(mesh):
     in_specs = (
         P(("groups", "ctx", "exp"), None),

time: 477 us -> 227 us (0.48)
  waiting for transfers between devices: 258 us -> 87.2 us
  blocking collectives: 80.4 us -> 0 us
  starting transfers between devices: 39.3 us -> 84 us
  matrix products: 43 us -> 7.03 us
  Pallas kernels: 0 us -> 31.2 us
  local copies, waits for them, and re-layouts: 26.4 us -> 11.4 us
  between operations: 14.2 us -> 1.08 us
  other arithmetic: 13.9 us -> 4.26 us
    all_to_all x4 -> x0, waiting for transfers between devices: 145 us -> none  [expert_trade(): lax.all_to_all(buffer, ('ctx', 'exp'), split_axis=0, concat_axis=0, tiled...]
    ppermute x0 -> x73, waiting for transfers between devices: none -> 87.2 us  [the longest x33 56.7 us: shifted(): lax.ppermute(x, 'ctx', [(i, (i + shift) % count) for i in range(count)])]
    ppermute x0 -> x73, starting transfers between devices: none -> 84 us  [the longest x33 60.1 us: shifted(): lax.ppermute(x, 'ctx', [(i, (i + shift) % count) for i in range(count)])]
    reduce_scatter x2 -> x0, waiting for transfers between devices: 61.1 us -> none  [the longest x1 41.9 us: local(): lax.psum_scatter(proj_part.astype(jnp.bfloat16), 'ctx', scatter_dimension...]
    all_gather x1 -> x0, waiting for transfers between devices: 51.7 us -> none  [local(): proj_full = lax.all_gather(out_proj, 'ctx', axis=1, tiled=True)]
    all_gather x3 -> x0, blocking collectives: 40.8 us -> none  [the longest x1 16.2 us: local(): lax.all_gather(value, 'ctx', axis=0, tiled=True)]
    psum x1 -> x0, blocking collectives: 39.6 us -> none  [local(): grad_gain = lax.psum(gain_part, ('ctx', 'exp'))]
    all_to_all x4 -> x0, starting transfers between devices: 38.7 us -> none  [expert_trade(): lax.all_to_all(buffer, ('ctx', 'exp'), split_axis=0, concat_axis=0, tiled...]
  transfers between devices with their start and end apart: 8 -> 73, of which waited for: 7 -> 21; matrix products, arithmetic and copies ran while one was open for 9% -> 8% of each run, Pallas kernels for 0% -> 11%
where the time goes in v2:
time: 227 us; the launch traced here: 226 us
  waiting for transfers between devices  87.2 us (38%)
  starting transfers between devices  84 us (37%)
  Pallas kernels  31.2 us (14%)
  local copies, waits for them, and re-layouts  11.4 us (5%)
  matrix products  7.03 us (3%)
  other arithmetic  4.26 us (2%)
    ppermute x33, starting transfers between devices, shifted(): lax.ppermute(x, 'ctx', [(i, (i + shift) % count) for i in range(count)])  60.1 us
    ppermute x33, waiting for transfers between devices, shifted(): lax.ppermute(x, 'ctx', [(i, (i + shift) % count) for i in range(count)])  56.7 us
    pallas_call x9, Pallas kernels, run_kernel(): pl.pallas_call(body, in_specs=[pl.BlockSpec(memory_space=pltpu.SMEM)] + [...  31.2 us
    ppermute x37, waiting for transfers between devices, swapped(): return lax.ppermute(x, 'exp', [(i, i ^ bit) for i in range(4)])  24.5 us
    ppermute x37, starting transfers between devices, swapped(): return lax.ppermute(x, 'exp', [(i, i ^ bit) for i in range(4)])  19.4 us
    dot_general x3, matrix products, tn(): lax.dot_general(a, b, (((0,), (0,)), ((), ())), preferred_element_type=F32)  7.03 us
    ppermute x3, waiting for transfers between devices, local_dense(): proj_far = [lax.ppermute(x, 'groups', [(0, 1), (1, 0)]) for x in proj_near]  6.06 us
    ppermute x3, starting transfers between devices, local_dense(): proj_far = [lax.ppermute(x, 'groups', [(0, 1), (1, 0)]) for x in proj_near]  4.58 us
  transfers between devices with their start and end apart: 73, of which 21 were waited for; matrix products, arithmetic and copies ran while one was open for 8% of the time, Pallas kernels for 11%

profile of v2, /device:TPU:0, one launch (start us, length us, event | category | flops | bytes accessed | tf_op | source)
XLA Modules:
  0.0 226.2 jit_solution(12850238056816140727)
XLA Ops:
  0.6 3.1 %collective-permute-start = (bf16[128,1024]{1,0:T(8,128)(2,1)}, bf16[128,1024]{1,0:T(8,128)(2,1)S(1)}, u32[]{:S(2)}, u32[]{:S(2)}) collective-permute-start(bf16[128,1024]{1,0:T(8,128)(2,1)} %refs_11_.1), channel_id=1, source_target_pairs={{0,4},{4,8},{8,12},{12,0},{1,5},{5,9},{9,13},{13,1},{2,6},{6,10},{... | collective-permute-start | bytes 786440 | tf_op jit(solution)/shard_map/ppermute | solution.py:272
  14.1 2.8 %collective-permute-start.5 = (bf16[128,256]{1,0:T(8,128)(2,1)S(1)}, bf16[128,256]{1,0:T(8,128)(2,1)S(1)}, u32[]{:S(2)}, u32[]{:S(2)}) collective-permute-start(bf16[128,256]{1,0:T(8,128)(2,1)S(1)} %constant_dynamic-update-slice_fusion.refs_4_.refs_12_), channel_id=1, source_target_pairs={{0,12},{4,0},{8,4},{12,8},{1,13},{5,1},{9,5},{13,9},{2,14},{6,2},{... | collective-permute-start | bytes 196616 | tf_op jit(solution)/shard_map/ppermute | solution.py:272
  16.9 7.6 %collective-permute-done.1.refs_2_ = bf16[128,1024]{1,0:T(8,128)(2,1)S(1)} collective-permute-done((bf16[128,1024]{1,0:T(8,128)(2,1)}, bf16[128,1024]{1,0:T(8,128)(2,1)S(1)}, u32[]{:S(2)}, u32[]{:S(2)}) %collective-permute-start.1) | collective-permute-done | bytes 262176 | tf_op jit(solution)/shard_map/ppermute | solution.py:272
  24.5 7.2 %collective-permute-start.27 = (bf16[32,2176]{1,0:T(8,128)(2,1)S(1)}, bf16[32,2176]{1,0:T(8,128)(2,1)S(1)}, u32[]{:S(2)}, u32[]{:S(2)}) collective-permute-start(bf16[32,2176]{1,0:T(8,128)(2,1)S(1)} %concatenate.7), channel_id=1, source_target_pairs={{0,8},{4,12},{8,0},{12,4},{1,9},{5,13},{9,1},{13,5},{2,10},{6,14},... | collective-permute-start | bytes 417800 | tf_op jit(solution)/shard_map/ppermute | solution.py:272
  31.8 3.3 %collective-permute-start.28 = (bf16[32,2176]{1,0:T(8,128)(2,1)S(1)}, bf16[32,2176]{1,0:T(8,128)(2,1)S(1)}, u32[]{:S(2)}, u32[]{:S(2)}) collective-permute-start(bf16[32,2176]{1,0:T(8,128)(2,1)S(1)} %concatenate.7), channel_id=1, source_target_pairs={{0,12},{4,0},{8,4},{12,8},{1,13},{5,1},{9,5},{13,9},{2,14},{6,2},{... | collective-permute-start | bytes 417800 | tf_op jit(solution)/shard_map/ppermute | solution.py:272
  37.6 8.8 %attend.1 = (bf16[512,1024]{1,0:T(8,128)(2,1)S(1)}, bf16[128,1024]{1,0:T(8,128)(2,1)S(1)}, bf16[2,4,32,512]{3,2,1,0:T(8,128)(2,1)S(1)}, bf16[2,4,32,512]{3,2,1,0:T(8,128)(2,1)}) custom-call(s32[3]{0:T(128)S(1)} %pad_add_fusion.place_ref, bf16[128,1024]{1,0:T(8,128)(2,1)S(1)} %copy-done.4, bf16[128,1024]{1,0:T(8,128)(2,1)S(1)} %collective-permute-done.refs_1_, ...), custom_call_target="tpu_custom_call" | custom-call | flops 1073741824 | bytes 4194304 | tf_op jit(solution)/shard_map/attend/pallas_call | solution.py:303
  54.5 6.6 %collective-permute-start.10 = (bf16[32,512]{1,0:T(8,128)(2,1)S(1)}, bf16[32,512]{1,0:T(8,128)(2,1)S(1)}, u32[]{:S(2)}, u32[]{:S(2)}) collective-permute-start(bf16[32,512]{1,0:T(8,128)(2,1)S(1)} %bitcast.108), channel_id=1, source_target_pairs={{0,12},{4,0},{8,4},{12,8},{1,13},{5,1},{9,5},{13,9},{2,14},{6,2},{... | collective-permute-start | bytes 98312 | tf_op jit(solution)/shard_map/ppermute | solution.py:272
  63.9 3.0 %collective-permute-done.8.refs_1_ = bf16[32,512]{1,0:T(8,128)(2,1)S(1)} collective-permute-done((bf16[32,512]{1,0:T(8,128)(2,1)S(1)}, bf16[32,512]{1,0:T(8,128)(2,1)S(1)}, u32[]{:S(2)}, u32[]{:S(2)}) %collective-permute-start.8) | collective-permute-done | bytes 32800 | tf_op jit(solution)/shard_map/ppermute | solution.py:272
  70.2 4.0 %collective-permute-start.12 = (bf16[4,32,512]{2,1,0:T(8,128)(2,1)S(1)}, bf16[4,32,512]{2,1,0:T(8,128)(2,1)S(1)}, u32[]{:S(2)}, u32[]{:S(2)}) collective-permute-start(bf16[4,32,512]{2,1,0:T(8,128)(2,1)S(1)} %hidden_rows.1.refs_0_), channel_id=1, source_target_pairs={{0,8},{4,12},{8,0},{12,4},{1,9},{5,13},{9,1},{13,5},{2,10},{6,14},... | collective-permute-start | bytes 393224 | tf_op jit(solution)/shard_map/ppermute | solution.py:272
  74.2 3.9 %collective-permute-done.11.refs_1_ = bf16[4,32,512]{2,1,0:T(8,128)(2,1)S(1)} collective-permute-done((bf16[4,32,512]{2,1,0:T(8,128)(2,1)S(1)}, bf16[4,32,512]{2,1,0:T(8,128)(2,1)S(1)}, u32[]{:S(2)}, u32[]{:S(2)}) %collective-permute-start.11) | collective-permute-done | bytes 131104 | tf_op jit(solution)/shard_map/ppermute | solution.py:272
  79.6 3.0 %collective-permute-done.12.refs_2_ = bf16[4,32,512]{2,1,0:T(8,128)(2,1)S(1)} collective-permute-done((bf16[4,32,512]{2,1,0:T(8,128)(2,1)S(1)}, bf16[4,32,512]{2,1,0:T(8,128)(2,1)S(1)}, u32[]{:S(2)}, u32[]{:S(2)}) %collective-permute-start.12) | collective-permute-done | bytes 131104 | tf_op jit(solution)/shard_map/ppermute | solution.py:272
  86.1 2.8 %collective-permute-done.15.refs_5_ = bf16[4,32,512]{2,1,0:T(8,128)(2,1)S(1)} collective-permute-done((bf16[4,32,512]{2,1,0:T(8,128)(2,1)S(1)}, bf16[4,32,512]{2,1,0:T(8,128)(2,1)S(1)}, u32[]{:S(2)}, u32[]{:S(2)}) %collective-permute-start.15) | collective-permute-done | bytes 131104 | tf_op jit(solution)/shard_map/ppermute | solution.py:276
  88.9 2.8 %collective-permute-done.16.refs_6_ = bf16[4,32,512]{2,1,0:T(8,128)(2,1)S(1)} collective-permute-done((bf16[4,32,512]{2,1,0:T(8,128)(2,1)S(1)}, bf16[4,32,512]{2,1,0:T(8,128)(2,1)S(1)}, u32[]{:S(2)}, u32[]{:S(2)}) %collective-permute-start.16) | collective-permute-done | bytes 131104 | tf_op jit(solution)/shard_map/ppermute | solution.py:276
  97.8 6.1 %expert_rows.1 = (bf16[512,2048]{1,0:T(8,128)(2,1)S(1)}, bf16[512,384]{1,0:T(8,128)(2,1)S(1)}, bf16[512,384]{1,0:T(8,128)(2,1)S(1)}, bf16[512,384]{1,0:T(8,128)(...) custom-call(s32[3]{0:T(128)S(1)} %pad_add_fusion.place_ref, ...), custom_call_target="tpu_custom_call" | custom-call | flops 3221225472 | bytes 11542528 | tf_op jit(solution)/shard_map/expert_rows/pallas_call | solution.py:303
  108.5 2.8 %collective-permute-start.53 = (bf16[512,512]{1,0:T(8,128)(2,1)S(1)}, bf16[512,512]{1,0:T(8,128)(2,1)S(1)}, u32[]{:S(2)}, u32[]{:S(2)}) collective-permute-start(bf16[512,512]{1,0:T(8,128)(2,1)S(1)} %copy-done.19), channel_id=1, source_target_pairs={{0,4},{4,8},{8,12},{12,0},{1,5},{5,9},{9,13},{13,1},{2,6},{6,10},{... | collective-permute-start | bytes 1572872 | tf_op jit(solution)/shard_map/ppermute | solution.py:272
  114.1 3.5 %collective-permute-done.44 = bf16[32,2048]{1,0:T(8,128)(2,1)S(1)} collective-permute-done((bf16[32,2048]{1,0:T(8,128)(2,1)S(1)}, bf16[32,2048]{1,0:T(8,128)(2,1)S(1)}, u32[]{:S(2)}, u32[]{:S(2)}) %collective-permute-start.44) | collective-permute-done | bytes 131104 | tf_op jit(solution)/shard_map/ppermute | solution.py:276
  134.5 2.8 %collective-permute-start.49 = (bf16[32,2048]{1,0:T(8,128)(2,1)S(1)}, bf16[32,2048]{1,0:T(8,128)(2,1)S(1)}, u32[]{:S(2)}, u32[]{:S(2)}) collective-permute-start(bf16[32,2048]{1,0:T(8,128)(2,1)S(1)} %get-tuple-element.76), channel_id=1, source_target_pairs={{0,12},{4,0},{8,4},{12,8},{1,13},{5,1},{9,5},{13,9},{2,14},{6,2},{... | collective-permute-start | bytes 393224 | tf_op jit(solution)/shard_map/ppermute | solution.py:272
  137.5 33.4 %collective-permute-done.47.refs_2_ = bf16[32,2048]{1,0:T(8,128)(2,1)S(1)} collective-permute-done((bf16[32,2048]{1,0:T(8,128)(2,1)S(1)}, bf16[32,2048]{1,0:T(8,128)(2,1)S(1)}, u32[]{:S(2)}, u32[]{:S(2)}) %collective-permute-start.47) | collective-permute-done | bytes 131104 | tf_op jit(solution)/shard_map/ppermute | solution.py:272
  171.3 3.4 %collective-permute-start.38 = (bf16[32,2048]{1,0:T(8,128)(2,1)S(1)}, bf16[32,2048]{1,0:T(8,128)(2,1)S(1)}, u32[]{:S(2)}, u32[]{:S(2)}) collective-permute-start(bf16[32,2048]{1,0:T(8,128)(2,1)S(1)} %get-tuple-element.85), channel_id=1, source_target_pairs={{0,8},{4,12},{8,0},{12,4},{1,9},{5,13},{9,1},{13,5},{2,10},{6,14},... | collective-permute-start | bytes 393224 | tf_op jit(solution)/shard_map/ppermute | solution.py:272
  192.2 2.9 %collective-permute-done.69 = f32[16,128]{1,0:T(8,128)S(1)} collective-permute-done((f32[16,128]{1,0:T(8,128)S(1)}, f32[16,128]{1,0:T(8,128)S(1)}, u32[]{:S(2)}, u32[]{:S(2)}) %collective-permute-start.69) | collective-permute-done | bytes 8224 | tf_op jit(solution)/shard_map/ppermute | solution.py:276
  200.1 6.1 %collective-permute-done.58.refs_10_ = bf16[512,512]{1,0:T(8,128)(2,1)S(1)} collective-permute-done((bf16[512,512]{1,0:T(8,128)(2,1)S(1)}, bf16[512,512]{1,0:T(8,128)(2,1)S(1)}, u32[]{:S(2)}, u32[]{:S(2)}) %collective-permute-start.58) | collective-permute-done | bytes 524320 | tf_op jit(solution)/shard_map/ppermute | solution.py:704
  207.2 3.1 %collective-permute-start.72 = (f32[16,128]{1,0:T(8,128)S(1)}, f32[16,128]{1,0:T(8,128)S(1)}, u32[]{:S(2)}, u32[]{:S(2)}) collective-permute-start(f32[16,128]{1,0:T(8,128)S(1)} %add.211), channel_id=1, source_target_pairs={{0,12},{4,0},{8,4},{12,8},{1,13},{5,1},{9,5},{13,9},{2,14},{6,2},{... | collective-permute-start | bytes 24584 | tf_op jit(solution)/shard_map/ppermute | solution.py:272
  210.9 6.1 %attend_backward.1 = (bf16[128,1024]{1,0:T(8,128)(2,1)}, bf16[128,256]{1,0:T(8,128)(2,1)S(1)}, bf16[128,256]{1,0:T(8,128)(2,1)S(1)}, bf16[128,256]{1,0:T(8,128)(2,1)S(1)}, bf16[128,256]{1,0:T(8,128)(2,1)S(1)}) custom-call(s32[3]{0:T(128)S(1)} %pad_add_fusion.place_ref, bf16[32,2048]{1,0:T(8,128)(2,1)S(1)} %copy-done.8, ...), custom_call_target="tpu_custom_call" | custom-call | flops 1207959552 | bytes 6029312 | tf_op jit(solution)/shard_map/attend_backward/pallas_call | solution.py:303
  217.7 3.2 %collective-permute-start.61 = (bf16[128,256]{1,0:T(8,128)(2,1)S(1)}, bf16[128,256]{1,0:T(8,128)(2,1)S(1)}, u32[]{:S(2)}, u32[]{:S(2)}) collective-permute-start(bf16[128,256]{1,0:T(8,128)(2,1)S(1)} %get-tuple-element.65), channel_id=1, source_target_pairs={{0,12},{4,0},{8,4},{12,8},{1,13},{5,1},{9,5},{13,9},{2,14},{6,2},{... | collective-permute-start | bytes 196616 | tf_op jit(solution)/shard_map/ppermute | solution.py:272
  (203 shorter events, 93.1 us)
Async XLA Ops:
  3.7 20.8 %collective-permute-start.1 = (bf16[128,1024]{1,0:T(8,128)(2,1)}, bf16[128,1024]{1,0:T(8,128)(2,1)S(1)}, u32[]{:S(2)}, u32[]{:S(2)}) collective-permute-start(bf16[128,1024]{1,0:T(8,128)(2,1)} %refs_11_.1), channel_id=1, source_target_pairs={{0,8},{4,12},{8,0},{12,4},{1,9},{5,13},{9,1},{13,5},{2,10},{6,14},... | collective-permute-start | bytes 786440 | tf_op jit(solution)/shard_map/ppermute | solution.py:272
  6.3 18.2 %collective-permute-start.2 = (bf16[128,1024]{1,0:T(8,128)(2,1)}, bf16[128,1024]{1,0:T(8,128)(2,1)S(1)}, u32[]{:S(2)}, u32[]{:S(2)}) collective-permute-start(bf16[128,1024]{1,0:T(8,128)(2,1)} %refs_11_.1), channel_id=1, source_target_pairs={{0,12},{4,0},{8,4},{12,8},{1,13},{5,1},{9,5},{13,9},{2,14},{6,2},{... | collective-permute-start | bytes 786440 | tf_op jit(solution)/shard_map/ppermute | solution.py:272
  9.2 25.8 %collective-permute-start.3 = (bf16[128,256]{1,0:T(8,128)(2,1)S(1)}, bf16[128,256]{1,0:T(8,128)(2,1)S(1)}, u32[]{:S(2)}, u32[]{:S(2)}) collective-permute-start(bf16[128,256]{1,0:T(8,128)(2,1)S(1)} %constant_dynamic-update-slice_fusion.refs_4_.refs_12_), channel_id=1, source_target_pairs={{0,4},{4,8},{8,12},{12,0},{1,5},{5,9},{9,13},{13,1},{2,6},{6,10},{... | collective-permute-start | bytes 196616 | tf_op jit(solution)/shard_map/ppermute | solution.py:272
  9.9 25.5 %collective-permute-start.4 = (bf16[128,256]{1,0:T(8,128)(2,1)S(1)}, bf16[128,256]{1,0:T(8,128)(2,1)S(1)}, u32[]{:S(2)}, u32[]{:S(2)}) collective-permute-start(bf16[128,256]{1,0:T(8,128)(2,1)S(1)} %constant_dynamic-update-slice_fusion.refs_4_.refs_12_), channel_id=1, source_target_pairs={{0,8},{4,12},{8,0},{12,4},{1,9},{5,13},{9,1},{13,5},{2,10},{6,14},... | collective-permute-start | bytes 196616 | tf_op jit(solution)/shard_map/ppermute | solution.py:272
  14.1 21.3 %collective-permute-start.5 = (bf16[128,256]{1,0:T(8,128)(2,1)S(1)}, bf16[128,256]{1,0:T(8,128)(2,1)S(1)}, u32[]{:S(2)}, u32[]{:S(2)}) collective-permute-start(bf16[128,256]{1,0:T(8,128)(2,1)S(1)} %constant_dynamic-update-slice_fusion.refs_4_.refs_12_), channel_id=1, source_target_pairs={{0,12},{4,0},{8,4},{12,8},{1,13},{5,1},{9,5},{13,9},{2,14},{6,2},{... | collective-permute-start | bytes 196616 | tf_op jit(solution)/shard_map/ppermute | solution.py:272
  24.5 22.6 %collective-permute-start.27 = (bf16[32,2176]{1,0:T(8,128)(2,1)S(1)}, bf16[32,2176]{1,0:T(8,128)(2,1)S(1)}, u32[]{:S(2)}, u32[]{:S(2)}) collective-permute-start(bf16[32,2176]{1,0:T(8,128)(2,1)S(1)} %concatenate.7), channel_id=1, source_target_pairs={{0,8},{4,12},{8,0},{12,4},{1,9},{5,13},{9,1},{13,5},{2,10},{6,14},... | collective-permute-start | bytes 417800 | tf_op jit(solution)/shard_map/ppermute | solution.py:272
  31.8 15.3 %collective-permute-start.28 = (bf16[32,2176]{1,0:T(8,128)(2,1)S(1)}, bf16[32,2176]{1,0:T(8,128)(2,1)S(1)}, u32[]{:S(2)}, u32[]{:S(2)}) collective-permute-start(bf16[32,2176]{1,0:T(8,128)(2,1)S(1)} %concatenate.7), channel_id=1, source_target_pairs={{0,12},{4,0},{8,4},{12,8},{1,13},{5,1},{9,5},{13,9},{2,14},{6,2},{... | collective-permute-start | bytes 417800 | tf_op jit(solution)/shard_map/ppermute | solution.py:272
  48.2 15.6 %collective-permute-start.29 = (bf16[4,32,2176]{2,1,0:T(8,128)(2,1)S(1)}, bf16[4,32,2176]{2,1,0:T(8,128)(2,1)}, u32[]{:S(2)}, u32[]{:S(2)}) collective-permute-start(bf16[4,32,2176]{2,1,0:T(8,128)(2,1)S(1)} %pad_maximum_fusion.refs_0_), channel_id=1, source_target_pairs={{0,2},{1,3},{2,0},{3,1},{4,6},{5,7},{6,4},{7,5},{8,10},{9,11},{10,... | collective-permute-start | bytes 1671176 | tf_op jit(solution)/shard_map/ppermute | solution.py:276
  52.4 14.5 %collective-permute-start.7 = (bf16[4,32,512]{2,1,0:T(8,128)(2,1)S(1)}, bf16[4,32,512]{2,1,0:T(8,128)(2,1)S(1)}, u32[]{:S(2)}, u32[]{:S(2)}) collective-permute-start(bf16[4,32,512]{2,1,0:T(8,128)(2,1)S(1)} %fusion.11), channel_id=1, source_target_pairs={{0,2},{1,3},{2,0},{3,1},{4,6},{5,7},{6,4},{7,5},{8,10},{9,11},{10,... | collective-permute-start | bytes 393224 | tf_op jit(solution)/shard_map/ppermute | solution.py:276
  62.7 32.0 %collective-permute-start.30 = (bf16[4,32,2176]{2,1,0:T(8,128)(2,1)S(1)}, bf16[4,32,2176]{2,1,0:T(8,128)(2,1)S(1)}, u32[]{:S(2)}, u32[]{:S(2)}) collective-permute-start(bf16[4,32,2176]{2,1,0:T(8,128)(2,1)S(1)} %pad_maximum_fusion.refs_0_), channel_id=1, source_target_pairs={{0,1},{1,0},{2,3},{3,2},{4,5},{5,4},{6,7},{7,6},{8,9},{9,8},{10,11... | collective-permute-start | bytes 1671176 | tf_op jit(solution)/shard_map/ppermute | solution.py:276
  63.9 31.3 %collective-permute-start.31 = (bf16[4,32,2176]{2,1,0:T(8,128)(2,1)}, bf16[4,32,2176]{2,1,0:T(8,128)(2,1)S(1)}, u32[]{:S(2)}, u32[]{:S(2)}) collective-permute-start(bf16[4,32,2176]{2,1,0:T(8,128)(2,1)} %collective-permute-done.29.refs_1_), channel_id=1, source_target_pairs={{0,1},{1,0},{2,3},{3,2},{4,5},{5,4},{6,7},{7,6},{8,9},{9,8},{10,11... | collective-permute-start | bytes 1671176 | tf_op jit(solution)/shard_map/ppermute | solution.py:276
  108.5 15.5 %collective-permute-start.53 = (bf16[512,512]{1,0:T(8,128)(2,1)S(1)}, bf16[512,512]{1,0:T(8,128)(2,1)S(1)}, u32[]{:S(2)}, u32[]{:S(2)}) collective-permute-start(bf16[512,512]{1,0:T(8,128)(2,1)S(1)} %copy-done.19), channel_id=1, source_target_pairs={{0,4},{4,8},{8,12},{12,0},{1,5},{5,9},{9,13},{13,1},{2,6},{6,10},{... | collective-permute-start | bytes 1572872 | tf_op jit(solution)/shard_map/ppermute | solution.py:272
  111.3 14.3 %collective-permute-start.32 = (bf16[4,32,2048]{2,1,0:T(8,128)(2,1)S(1)}, bf16[4,32,2048]{2,1,0:T(8,128)(2,1)S(1)}, u32[]{:S(2)}, u32[]{:S(2)}) collective-permute-start(bf16[4,32,2048]{2,1,0:T(8,128)(2,1)S(1)} %get-tuple-element.50), channel_id=1, source_target_pairs={{0,1},{1,0},{2,3},{3,2},{4,5},{5,4},{6,7},{7,6},{8,9},{9,8},{10,11... | collective-permute-start | bytes 1572872 | tf_op jit(solution)/shard_map/ppermute | solution.py:276
  126.9 49.3 %collective-permute-start.54 = (bf16[512,512]{1,0:T(8,128)(2,1)S(1)}, bf16[512,512]{1,0:T(8,128)(2,1)S(1)}, u32[]{:S(2)}, u32[]{:S(2)}) collective-permute-start(bf16[512,512]{1,0:T(8,128)(2,1)S(1)} %copy-done.19), channel_id=1, source_target_pairs={{0,8},{4,12},{8,0},{12,4},{1,9},{5,13},{9,1},{13,5},{2,10},{6,14},... | collective-permute-start | bytes 1572872 | tf_op jit(solution)/shard_map/ppermute | solution.py:272
  128.8 47.4 %collective-permute-start.55 = (bf16[512,512]{1,0:T(8,128)(2,1)S(1)}, bf16[512,512]{1,0:T(8,128)(2,1)S(1)}, u32[]{:S(2)}, u32[]{:S(2)}) collective-permute-start(bf16[512,512]{1,0:T(8,128)(2,1)S(1)} %copy-done.19), channel_id=1, source_target_pairs={{0,12},{4,0},{8,4},{12,8},{1,13},{5,1},{9,5},{13,9},{2,14},{6,2},{... | collective-permute-start | bytes 1572872 | tf_op jit(solution)/shard_map/ppermute | solution.py:272
  131.6 45.3 %collective-permute-start.56 = (bf16[512,512]{1,0:T(8,128)(2,1)S(1)}, bf16[512,512]{1,0:T(8,128)(2,1)S(1)}, u32[]{:S(2)}, u32[]{:S(2)}) collective-permute-start(bf16[512,512]{1,0:T(8,128)(2,1)S(1)} %collective-permute-done.53.refs_5_), channel_id=1, source_target_pairs={{0,16},{16,0},{1,17},{17,1},{2,18},{18,2},{3,19},{19,3},{4,20},{20... | collective-permute-start | bytes 1572872 | tf_op jit(solution)/shard_map/ppermute | solution.py:704
  134.0 36.9 %collective-permute-start.47 = (bf16[32,2048]{1,0:T(8,128)(2,1)S(1)}, bf16[32,2048]{1,0:T(8,128)(2,1)S(1)}, u32[]{:S(2)}, u32[]{:S(2)}) collective-permute-start(bf16[32,2048]{1,0:T(8,128)(2,1)S(1)} %get-tuple-element.77), channel_id=1, source_target_pairs={{0,8},{4,12},{8,0},{12,4},{1,9},{5,13},{9,1},{13,5},{2,10},{6,14},... | collective-permute-start | bytes 393224 | tf_op jit(solution)/shard_map/ppermute | solution.py:272
  134.5 36.8 %collective-permute-start.49 = (bf16[32,2048]{1,0:T(8,128)(2,1)S(1)}, bf16[32,2048]{1,0:T(8,128)(2,1)S(1)}, u32[]{:S(2)}, u32[]{:S(2)}) collective-permute-start(bf16[32,2048]{1,0:T(8,128)(2,1)S(1)} %get-tuple-element.76), channel_id=1, source_target_pairs={{0,12},{4,0},{8,4},{12,8},{1,13},{5,1},{9,5},{13,9},{2,14},{6,2},{... | collective-permute-start | bytes 393224 | tf_op jit(solution)/shard_map/ppermute | solution.py:272
  181.2 18.1 %collective-permute-start.57 = (bf16[512,512]{1,0:T(8,128)(2,1)S(1)}, bf16[512,512]{1,0:T(8,128)(2,1)S(1)}, u32[]{:S(2)}, u32[]{:S(2)}) collective-permute-start(bf16[512,512]{1,0:T(8,128)(2,1)S(1)} %collective-permute-done.54.refs_6_), channel_id=1, source_target_pairs={{0,16},{16,0},{1,17},{17,1},{2,18},{18,2},{3,19},{19,3},{4,20},{20... | collective-permute-start | bytes 1572872 | tf_op jit(solution)/shard_map/ppermute | solution.py:704
  184.6 21.5 %collective-permute-start.58 = (bf16[512,512]{1,0:T(8,128)(2,1)S(1)}, bf16[512,512]{1,0:T(8,128)(2,1)S(1)}, u32[]{:S(2)}, u32[]{:S(2)}) collective-permute-start(bf16[512,512]{1,0:T(8,128)(2,1)S(1)} %collective-permute-done.55.refs_7_), channel_id=1, source_target_pairs={{0,16},{16,0},{1,17},{17,1},{2,18},{18,2},{3,19},{19,3},{4,20},{20... | collective-permute-start | bytes 1572872 | tf_op jit(solution)/shard_map/ppermute | solution.py:704
  192.1 15.1 %collective-permute-start.50 = (bf16[32,2048]{1,0:T(8,128)(2,1)S(1)}, bf16[32,2048]{1,0:T(8,128)(2,1)S(1)}, u32[]{:S(2)}, u32[]{:S(2)}) collective-permute-start(bf16[32,2048]{1,0:T(8,128)(2,1)S(1)} %copy-done.8), channel_id=1, source_target_pairs={{0,1},{1,0},{2,3},{3,2},{4,5},{5,4},{6,7},{7,6},{8,9},{9,8},{10,11... | collective-permute-start | bytes 393224 | tf_op jit(solution)/shard_map/ppermute | solution.py:276
  195.1 15.3 %collective-permute-start.66 = (bf16[4,32,512]{2,1,0:T(8,128)(2,1)S(1)}, bf16[4,32,512]{2,1,0:T(8,128)(2,1)S(1)}, u32[]{:S(2)}, u32[]{:S(2)}) collective-permute-start(bf16[4,32,512]{2,1,0:T(8,128)(2,1)S(1)} %pad_maximum_fusion.1.refs_0_), channel_id=1, source_target_pairs={{0,2},{1,3},{2,0},{3,1},{4,6},{5,7},{6,4},{7,5},{8,10},{9,11},{10,... | collective-permute-start | bytes 393224 | tf_op jit(solution)/shard_map/ppermute | solution.py:276
  195.8 14.6 %collective-permute-start.52 = (bf16[32,2048]{1,0:T(8,128)(2,1)S(1)}, bf16[32,2048]{1,0:T(8,128)(2,1)S(1)}, u32[]{:S(2)}, u32[]{:S(2)}) collective-permute-start(bf16[32,2048]{1,0:T(8,128)(2,1)S(1)} %collective-permute-done.51.refs_2_), channel_id=1, source_target_pairs={{0,1},{1,0},{2,3},{3,2},{4,5},{5,4},{6,7},{7,6},{8,9},{9,8},{10,11... | collective-permute-start | bytes 393224 | tf_op jit(solution)/shard_map/ppermute | solution.py:276
  199.3 17.7 %collective-permute-start.70 = (f32[16,128]{1,0:T(8,128)S(1)}, f32[16,128]{1,0:T(8,128)S(1)}, u32[]{:S(2)}, u32[]{:S(2)}) collective-permute-start(f32[16,128]{1,0:T(8,128)S(1)} %add.211), channel_id=1, source_target_pairs={{0,4},{4,8},{8,12},{12,0},{1,5},{5,9},{9,13},{13,1},{2,6},{6,10},{... | collective-permute-start | bytes 24584 | tf_op jit(solution)/shard_map/ppermute | solution.py:272
  (69 other events, 734.9 us)

commit v3 on v2

--- a/solution.py
+++ b/solution.py
@@ -268,12 +268,21 @@
 SETS = (0, 2, 1, 3)
 
 
-def shifted(x, shift, count):
-    return lax.ppermute(x, "ctx", [(i, (i + shift) % count) for i in range(count)])
-
-
-def swapped(x, bit):
-    return lax.ppermute(x, "exp", [(i, i ^ bit) for i in range(4)])
+def crossed(x, bits):
+    return lax.ppermute(x, "ctx", [(i, i ^ bits) for i in range(4)])
+
+
+def swapped(x, bits):
+    return lax.ppermute(x, "exp", [(i, i ^ bits) for i in range(4)])
+
+
+def after(x, *others):
+    return lax.optimization_barrier((x, *others))[0]
+
+
+def from_all(x):
+    far, near = crossed(x, 2), crossed(x, 1)
+    return [x, near, far, crossed(far, 1)]
 
 
 def pick(x, index, axis):
@@ -290,10 +299,6 @@
 
 def nn(a, b):
     return lax.dot_general(a, b, (((1,), (0,)), ((), ())), preferred_element_type=F32)
-
-
-def wrap(value, count):
-    return lax.rem(value + count, count)
 
 
 def run_kernel(body, name, place, args, outs, scratch=(), flops=0, limit=40):
@@ -312,105 +317,96 @@
     )(place, *args)
 
 
-def attend(place, query_parts, pair_parts, out_proj):
-    n = len(query_parts)
-    rows, width = query_parts[0].shape
+def visible_keys(rows, count, query_block, base):
+    shape = (rows, count * rows)
+    key_pos = lax.broadcasted_iota(jnp.int32, shape, 1)
+    turn = sum([(key_pos >= i * rows).astype(jnp.int32) for i in range(1, count)])
+    offset = key_pos - turn * rows
+    diagonal = offset <= lax.broadcasted_iota(jnp.int32, shape, 0)
+    block = turn ^ base
+    return (block < query_block) | ((block == query_block) & diagonal)
+
+
+def attend(place, turn, query, pairs, out_proj):
+    n = len(pairs)
+    rows, width = query.shape
     tok = rows // 4
     cols = out_proj.shape[1]
     heads = width // HEAD_SIZE
     factor = HEAD_SIZE ** (-0.5) * LOG2E
 
-    def body(place_ref, *refs):
-        q_refs, p_refs, proj_ref = refs[:n], refs[n : 2 * n], refs[2 * n]
-        mix_ref, own_ref, keep_ref, send_ref, qs, ks, vs, ps = refs[2 * n + 1 :]
+    def body(place_ref, query_ref, *refs):
+        proj_ref, mix_ref, keep_ref, send_ref, ks, vs, ps = refs[n:]
         c, e = place_ref[0], place_ref[1]
-        for d in range(n):
-            at = pl.multiple_of(wrap(c - d, n) * rows, rows)
-            qs[pl.ds(at, rows), :] = q_refs[d][...]
-            ks[pl.ds(at, rows), :] = p_refs[d][:, :HEAD_SIZE]
-            vs[pl.ds(at, rows), :] = p_refs[d][:, HEAD_SIZE:]
-        below = lax.broadcasted_iota(jnp.int32, (rows, rows), 1) <= lax.broadcasted_iota(
-            jnp.int32, (rows, rows), 0
-        )
-        core, line = lax.rem(e, 2), lax.div(e, 2)
-        for b in range(n):
-            lo, hi = b * rows, (b + 1) * rows
-            for head in range(heads):
-                at = slice(head * HEAD_SIZE, (head + 1) * HEAD_SIZE)
-                scores = nt(qs[lo:hi, at], ks[:hi, :])
-                last = jnp.where(below, scores[:, lo:], NEG)
-                scores = jnp.concatenate([scores[:, :lo], last], 1) if b else last
-                peak = jnp.max(scores, -1, keepdims=True)
-                weights = jnp.exp2((scores - peak) * factor)
-                total = jnp.sum(weights, -1, keepdims=True)
-                mix_ref[lo:hi, at] = (nn(weights.astype(BF16), vs[:hi, :]) / total).astype(BF16)
-            ps[...] = nn(mix_ref[lo:hi, :], proj_ref[...]).astype(BF16)
-            d = wrap(c - b, n)
-            for turn in range(2):
-                base = (line + turn - 2 * turn * line) * 2
-                keep_ref[turn, d] = ps[pl.ds(pl.multiple_of((base + core) * tok, tok), tok), :]
-                send_ref[turn, d] = ps[pl.ds(pl.multiple_of((base + 1 - core) * tok, tok), tok), :]
-        own_ref[...] = mix_ref[pl.ds(pl.multiple_of(c * rows, rows), rows), :]
+        for r in range(n):
+            ks[r * rows : (r + 1) * rows, :] = refs[r][:, :HEAD_SIZE]
+            vs[r * rows : (r + 1) * rows, :] = refs[r][:, HEAD_SIZE:]
+        visible = visible_keys(rows, n, c ^ turn, c)
+        for head in range(heads):
+            at = slice(head * HEAD_SIZE, (head + 1) * HEAD_SIZE)
+            scores = jnp.where(visible, nt(query_ref[:, at], ks[...]), NEG)
+            peak = jnp.max(scores, -1, keepdims=True)
+            weights = jnp.exp2((scores - peak) * factor)
+            total = jnp.sum(weights, -1, keepdims=True)
+            mix_ref[:, at] = (nn(weights.astype(BF16), vs[...]) / total).astype(BF16)
+        ps[...] = nn(mix_ref[...], proj_ref[...]).astype(BF16)
+        for x in range(2):
+            same, other = e ^ (2 * x), e ^ (2 * x + 1)
+            keep_ref[x] = ps[pl.ds(pl.multiple_of(same * tok, tok), tok), :]
+            send_ref[x] = ps[pl.ds(pl.multiple_of(other * tok, tok), tok), :]
 
     return run_kernel(
         body,
         "attend",
         place,
-        [*query_parts, *pair_parts, out_proj],
-        [
-            ((n * rows, width), BF16),
-            ((rows, width), BF16),
-            ((2, n, tok, cols), BF16),
-            ((2, n, tok, cols), BF16),
-        ],
-        [
-            ((n * rows, width), BF16),
-            ((n * rows, HEAD_SIZE), BF16),
-            ((n * rows, HEAD_SIZE), BF16),
-            ((rows, cols), BF16),
-        ],
-        flops=4 * n * rows * n * rows * width,
-    )
-
-
-def hidden_rows(place, keep, received, crossed, resid_parts):
+        [query, *pairs, out_proj],
+        [((rows, width), BF16), ((2, tok, cols), BF16), ((2, tok, cols), BF16)],
+        [((n * rows, HEAD_SIZE), BF16), ((n * rows, HEAD_SIZE), BF16), ((rows, cols), BF16)],
+        flops=4 * rows * n * rows * width,
+    )
+
+
+def hidden_rows(place, keep, received, line, resid_parts):
     n = len(resid_parts)
 
-    def body(place_ref, keep_ref, received_ref, crossed_ref, *refs):
+    def body(place_ref, *refs):
         for d in range(n):
-            total = keep_ref[0, d].astype(F32) + received_ref[0, d].astype(F32)
-            total = total + crossed_ref[d].astype(F32) + refs[d][...].astype(F32)
-            refs[n][d] = total.astype(BF16)
+            total = refs[d][0].astype(F32) + refs[n + d][0].astype(F32)
+            total = total + refs[2 * n + d][...].astype(F32) + refs[3 * n + d][...].astype(F32)
+            refs[4 * n][d] = total.astype(BF16)
 
     return run_kernel(
-        body, "hidden_rows", place, [keep, received, crossed, *resid_parts], [(crossed.shape, BF16)]
+        body,
+        "hidden_rows",
+        place,
+        [*keep, *received, *line, *resid_parts],
+        [((n, *line[0].shape), BF16)],
     )[0]
 
 
 def grad_rows_of(place, grad_sets, w_down, width):
-    n, tok = grad_sets[0].shape[:2]
+    n, tok = len(grad_sets[0]), grad_sets[0][0].shape[0]
     total = 4 * n * tok
     experts = 4 * n
 
     def body(place_ref, *refs):
-        down_ref, rows_ref, gate_ref, act_ref = refs[4:]
+        down_ref, rows_ref, gate_ref, act_ref = refs[4 * n :]
         expert = place_ref[0] * 4 + place_ref[1]
         lane = lax.broadcasted_iota(jnp.int32, (tok, 128), 1)
         wanted = (lane == expert) | (lane == expert + experts)
-        for s in range(4):
-            for d in range(n):
-                at = s * n * tok + (-d) % n * tok
-                gate = jnp.where(wanted, refs[s][d, :, width:].astype(F32), 0.0)
-                gate = jnp.sum(gate, -1, keepdims=True)
-                gate_ref[at : at + tok, :] = gate
-                rows_ref[at : at + tok, :] = (refs[s][d, :, :width].astype(F32) * gate).astype(BF16)
+        for s in range(4 * n):
+            at = slice(s * tok, (s + 1) * tok)
+            gate = jnp.where(wanted, refs[s][:, width:].astype(F32), 0.0)
+            gate = jnp.sum(gate, -1, keepdims=True)
+            gate_ref[at, :] = gate
+            rows_ref[at, :] = (refs[s][:, :width].astype(F32) * gate).astype(BF16)
         act_ref[...] = nt(rows_ref[...], down_ref[...])
 
     return run_kernel(
         body,
         "grad_rows",
         place,
-        [*grad_sets, w_down],
+        [*sum(grad_sets, []), w_down],
         [((total, width), BF16), ((total, 1), F32), ((total, w_down.shape[0]), F32)],
         flops=2 * total * width * w_down.shape[0],
     )
@@ -430,9 +426,9 @@
         c = place_ref[0]
         for s in range(4):
             for d in range(n):
-                at = pl.multiple_of(wrap(c - d, n) * cols, cols)
+                at = pl.multiple_of((c ^ d) * cols, cols)
                 for t in range(n):
-                    row = s * group + (-(d + t)) % n * tok
+                    row = s * group + (d ^ t) * tok
                     hid[row : row + tok, pl.ds(at, cols)] = pieces[s * n + d][t]
             rows = slice(s * group, (s + 1) * group)
             value = hid[rows, :].astype(F32)
@@ -491,23 +487,31 @@
     )
 
 
-def sum_back(parts):
-    n = parts[0].shape[0]
-    order = sorted(range(n), key=lambda j: -min(j, n - j))
-    far, near = swapped(parts[3], 1), swapped(parts[2], 1)
-
+def sum_back(parts, before_exp=(), before_ctx=(), beside=()):
     def add(*xs):
         return sum([x.astype(F32) for x in xs[1:]], xs[0].astype(F32)).astype(BF16)
 
-    crossed = {j: swapped(add(parts[1][j], far[j]), 2) for j in order}
-    sums = {j: add(parts[0][j], near[j], crossed[j]) for j in order}
-    received = {j: shifted(sums[j], j, n) for j in order if j}
-    return [sums[0]] + [received[j] for j in range(1, n)]
+    if before_exp:
+        parts = [after(x, *before_exp) for x in parts]
+    far, near = swapped(parts[3], 1), swapped(parts[2], 1)
+    line = {}
+    for j in (3, 2, 1, 0):
+        part = add(parts[1][j], far[j])
+        if j == 1:
+            part = after(part, line[3], *beside)
+        elif j == 0:
+            part = after(part, line[2])
+        line[j] = swapped(part, 2)
+    sums = [add(parts[0][j], near[j], line[j]) for j in range(4)]
+    if before_ctx:
+        sums = [after(x, *before_ctx) for x in sums]
+    return [sums[0]] + [crossed(sums[j], j) for j in (1, 2, 3)]
 
 
 def norm_backward(place, summed, hidden, grad_out, norm_gain, cols):
     n = len(summed)
     tok, width = hidden.shape
+    blocks = width // cols
 
     def body(place_ref, *refs):
         hidden_ref, grad_ref, gain_ref = refs[n : n + 3]
@@ -522,15 +526,15 @@
         mean = jnp.mean(scaled * unit_rows, -1, keepdims=True)
         grad = grad_ref[...].astype(F32) + inv_rms * (scaled - unit_rows * mean)
         out_ref[...] = grad.astype(BF16)
-        for d in range(n):
-            cuts[d][...] = out_ref[:, pl.ds(pl.multiple_of(wrap(c + d, n) * cols, cols), cols)]
+        for d in range(blocks):
+            cuts[d][...] = out_ref[:, pl.ds(pl.multiple_of((c ^ d) * cols, cols), cols)]
 
     return run_kernel(
         body,
         "norm_backward",
         place,
         [*summed, hidden, grad_out, norm_gain.reshape(1, width)],
-        [((tok, width), BF16), ((1, width), F32)] + [((tok, cols), BF16)] * n,
+        [((tok, width), BF16), ((1, width), F32)] + [((tok, cols), BF16)] * blocks,
     )
 
 
@@ -544,49 +548,56 @@
     return run_kernel(body, "layer_rows", place, [*summed, hidden], [(hidden.shape, BF16)])[0]
 
 
-def attend_backward(place, grad_parts, out_proj, proj_near, proj_far, query, pair_parts, mix):
-    n = len(pair_parts)
-    rows, width = query.shape
-    tok = rows // 4
-    cols = out_proj.shape[1]
+def mix_grad_parts(place, cut_sets, out_proj):
+    n, tok, cols = cut_sets[0].shape
+    rows, width = 4 * tok, out_proj.shape[0]
+
+    def body(place_ref, *refs):
+        proj_ref, outs, grads = refs[4], refs[5 : 5 + n], refs[5 + n]
+        e = place_ref[1]
+        for d in range(n):
+            for r in range(4):
+                at = pl.multiple_of(d * rows + (e ^ r) * tok, tok)
+                grads[pl.ds(at, tok), :] = refs[r][d]
+        for half in range(2):
+            at = slice(half * width // 2, (half + 1) * width // 2)
+            part = nt(grads[...], proj_ref[at, :]).astype(BF16)
+            for d in range(n):
+                outs[d][:, at] = part[d * rows : (d + 1) * rows]
+
+    return run_kernel(
+        body,
+        "mix_grad_parts",
+        place,
+        [*cut_sets, out_proj],
+        [((rows, width), BF16)] * n,
+        [((n * rows, cols), BF16)],
+        flops=2 * n * rows * cols * width,
+    )
+
+
+def attend_backward(place, grad_parts, query, pairs, mix):
+    n, g = len(pairs), len(grad_parts)
+    rows, width = mix.shape
     heads = width // HEAD_SIZE
-    half = width // 2
     scale = HEAD_SIZE ** (-0.5)
 
     def body(place_ref, *refs):
-        g_refs, proj_ref = refs[:4], refs[4]
-        near, far = refs[5 : 4 + n], refs[4 + n : 3 + 2 * n]
-        query_ref = refs[3 + 2 * n]
-        p_refs = refs[4 + 2 * n : 4 + 3 * n]
-        mix_ref, dq_ref = refs[4 + 3 * n : 6 + 3 * n]
-        outs = refs[6 + 3 * n : 6 + 4 * n]
-        gs, acc, qs, ms, ks, vs, score_half, prob_half = refs[6 + 4 * n :]
-        c, e, g = place_ref[0], place_ref[1], place_ref[2]
-        core, line = lax.rem(e, 2), lax.div(e, 2)
-        for r in range(4):
-            low, high = r % 2, r // 2
-            other = (line + high - 2 * high * line) * 2 + core + low - 2 * low * core
-            gs[pl.ds(pl.multiple_of(other * tok, tok), tok), :] = g_refs[r][...]
-
-        def columns(d):
-            return gs[:, pl.ds(pl.multiple_of(wrap(c - d, n) * cols, cols), cols)]
-
-        acc[...] = nt(columns(0), proj_ref[...])
-        here = pl.ds(pl.multiple_of(g * half, half), half)
-        there = pl.ds(pl.multiple_of((1 - g) * half, half), half)
-        acc[:, here] += sum([nt(columns(d), near[d - 1][...]) for d in range(1, n)])
-        acc[:, there] += sum([nt(columns(d), far[d - 1][...]) for d in range(1, n)])
-        key_pos = lax.broadcasted_iota(jnp.int32, (rows, n * rows), 1)
-        visible = (key_pos <= lax.broadcasted_iota(jnp.int32, (rows, n * rows), 0)) | (
-            (key_pos >= rows) & (key_pos < (c + 1) * rows)
-        )
+        g_refs, query_ref = refs[:g], refs[g]
+        p_refs = refs[g + 1 : g + 1 + n]
+        mix_ref, dq_ref = refs[g + 1 + n : g + 3 + n]
+        outs = refs[g + 3 + n : g + 3 + 2 * n]
+        qs, ms, ks, vs, score_half, prob_half = refs[g + 3 + 2 * n :]
+        c = place_ref[0]
+        visible = visible_keys(rows, n, c, c)
         for d in range(n):
             ks[d * rows : (d + 1) * rows, :] = p_refs[d][:, :HEAD_SIZE]
             vs[d * rows : (d + 1) * rows, :] = p_refs[d][:, HEAD_SIZE:]
         for head in range(heads):
             at = slice(head * HEAD_SIZE, (head + 1) * HEAD_SIZE)
             rs = slice(head * rows, (head + 1) * rows)
-            grad = acc[:, at].astype(BF16)
+            grad = sum([x[:, at].astype(F32) for x in g_refs[1:]], g_refs[0][:, at].astype(F32))
+            grad = grad.astype(BF16)
             qs[rs, :] = query_ref[:, at]
             ms[rs, :] = grad
             scores = jnp.where(visible, nt(query_ref[:, at], ks[...]), NEG)
@@ -600,7 +611,7 @@
         key_sum = (tn(score_half[...], qs[...]) * scale).astype(BF16)
         value_sum = tn(prob_half[...], ms[...]).astype(BF16)
         for j in range(n):
-            rs = slice((-j) % n * rows, ((-j) % n + 1) * rows)
+            rs = slice(j * rows, (j + 1) * rows)
             outs[j][:, :HEAD_SIZE] = key_sum[rs]
             outs[j][:, HEAD_SIZE:] = value_sum[rs]
 
@@ -611,36 +622,34 @@
         body,
         "attend_backward",
         place,
-        [*grad_parts, out_proj, *proj_near, *proj_far, query, *pair_parts, mix],
+        [*grad_parts, query, *pairs, mix],
         [((rows, width), BF16)] + [((rows, 2 * HEAD_SIZE), BF16)] * n,
-        [((rows, n * cols), BF16), ((rows, width), F32), stacked, stacked, keys, keys, halves, halves],
-        flops=2 * rows * width * (n * cols + 5 * n * rows),
-    )
-
-
-def proj_grad(place, mix_all, cut_sets):
+        [stacked, stacked, keys, keys, halves, halves],
+        flops=10 * rows * width * n * rows,
+    )
+
+
+def proj_grad(place, mixes, cut_sets):
     n, tok, cols = cut_sets[0].shape
-    width = mix_all.shape[1]
-
-    def body(place_ref, mix_ref, *refs):
-        out_ref, rows_ref = refs[4], refs[5]
-        c, e = place_ref[0], place_ref[1]
-        core, line = lax.rem(e, 2), lax.div(e, 2)
-        for r in range(4):
-            low, high = r % 2, r // 2
-            other = (line + high - 2 * high * line) * 2 + core + low - 2 * low * core
-            for d in range(n):
-                at = pl.multiple_of((wrap(c - d, n) * 4 + other) * tok, tok)
-                rows_ref[pl.ds(at, tok), :] = refs[r][d]
-        out_ref[...] = tn(mix_ref[...], rows_ref[...]).astype(BF16)
+    rows, width = mixes[0].shape
+
+    def body(place_ref, *refs):
+        out_ref, grads, mix = refs[n + 4 :]
+        e = place_ref[1]
+        for d in range(n):
+            mix[d * rows : (d + 1) * rows, :] = refs[d][...]
+            for r in range(4):
+                at = pl.multiple_of(d * rows + (e ^ r) * tok, tok)
+                grads[pl.ds(at, tok), :] = refs[n + r][d]
+        out_ref[...] = tn(mix[...], grads[...]).astype(BF16)
 
     return run_kernel(
         body,
         "proj_grad",
         place,
-        [mix_all, *cut_sets],
+        [*mixes, *cut_sets],
         [((width, cols), BF16)],
-        [((4 * n * tok, cols), BF16)],
+        [((n * rows, cols), BF16), ((n * rows, width), BF16)],
         flops=8 * n * tok * cols * width,
     )[0]
 
@@ -660,21 +669,20 @@
     grad_out,
 ):
     n = lax.axis_size("ctx")
-    c, e, g = lax.axis_index("ctx"), lax.axis_index("exp"), lax.axis_index("groups")
-    place = jnp.stack([c, e, g]).astype(jnp.int32)
+    c, e = lax.axis_index("ctx"), lax.axis_index("exp")
+    place = jnp.stack([c, e]).astype(jnp.int32)
     tok, width = resid.shape
     cols = out_proj.shape[1]
     experts = 4 * n
-
-    def to_all(x):
-        return [x] + [shifted(x, d, n) for d in range(1, n)]
-
-    pair_parts = to_all(jnp.concatenate([key, value], 1))
-    query_parts = to_all(query)
-    resid_cut = resid.reshape(tok, n, cols)
-    resid_parts = [pick(resid_cut, c, 1)] + [
-        shifted(pick(resid_cut, wrap(c + d, n), 1), d, n) for d in range(1, n)
-    ]
+    scope = jax.named_scope
+
+    def across(blocks):
+        return [blocks[0]] + [crossed(blocks[r], r) for r in range(1, n)]
+
+    with scope("gather_pairs"):
+        pairs = from_all(jnp.concatenate([key, value], 1))
+    with scope("gather_queries"):
+        queries = from_all(query)
 
     gates = jnp.sum(
         jnp.where(
@@ -692,55 +700,70 @@
         ],
         1,
     )
-    payload, proj_half, *_ = lax.optimization_barrier(
-        (payload, lax.dynamic_slice_in_dim(out_proj, g * (out_proj.shape[0] // 2), out_proj.shape[0] // 2, 0))
-        + tuple(query_parts[1:])
-    )
-    grad_own = jnp.stack(to_all(payload))
-    grad_line = swapped(grad_own, 2)
-    grad_sets = [grad_own, grad_line, swapped(grad_own, 1), swapped(grad_line, 1)]
-
-    proj_near = to_all(proj_half)[1:]
-    proj_far = [lax.ppermute(x, "groups", [(0, 1), (1, 0)]) for x in proj_near]
-
-    mix_all, mix, keep, send = attend(place, query_parts, pair_parts, out_proj)
-    received = swapped(send, 1)
-    crossed = swapped((keep[1].astype(F32) + received[1].astype(F32)).astype(BF16), 2)
-    hidden_own = to_all(hidden_rows(place, keep, received, crossed, resid_parts))
-    hidden_line = [swapped(x, 2) for x in hidden_own]
-    hidden_sets = [hidden_own, hidden_line] + [
-        [swapped(x, 1) for x in xs] for xs in (hidden_own, hidden_line)
-    ]
-
+    with scope("gather_resid"):
+        resid_cut = resid.reshape(tok, n, cols)
+        resid_parts = across([pick(resid_cut, c ^ r, 1) for r in range(n)])
+    with scope("gather_grads"):
+        grad_own = from_all(after(payload, *queries[1:3]))
+        grad_line = [swapped(payload, 2)] + [swapped(x, 2) for x in grad_own[1:]]
+        grad_sets = [grad_own, grad_line] + [
+            [swapped(x, 1) for x in xs] for xs in (grad_own, grad_line)
+        ]
     grad_rows, gate, act_grad = grad_rows_of(place, grad_sets, w_down[0], width)
+
+    mixes, keep, send = zip(*[attend(place, r, queries[r], pairs, out_proj) for r in range(n)])
+    with scope("sum_heads"):
+        received = [swapped(x, 1) for x in send]
+        sums = [(k[1].astype(F32) + r[1].astype(F32)).astype(BF16) for k, r in zip(keep, received)]
+        sums[3] = after(sums[3], *grad_own[1:3])
+        line = [swapped(x, 2) for x in sums]
+    hidden_block = hidden_rows(place, keep, received, line, resid_parts)
+    with scope("gather_hidden"):
+        hidden_own = from_all(after(hidden_block, grad_own[3], *grad_line[:3]))
+        hidden_line = [swapped(x, 2) for x in hidden_own]
+        hidden_line[-1], act_grad = lax.optimization_barrier((hidden_line[-1], act_grad))
+        hidden_sets = [hidden_own, hidden_line] + [
+            [swapped(x, 1) for x in xs] for xs in (hidden_own, hidden_line)
+        ]
+
     normed, act_rows, gate_grad, up_grad, hidden, *row_grads = expert_rows(
         place, hidden_sets, act_grad, norm_gain, w_gate[0], w_up[0]
     )
-    summed = sum_back(row_grads)
+    weighted = weighted_rows(place, act_rows, gate, w_down[0], n)
+    with scope("sum_row_grads"):
+        summed = sum_back(row_grads, beside=weighted[:1])
     grad_resid, gain_part, *cuts = norm_backward(place, summed, hidden, grad_out, norm_gain, cols)
 
-    near = swapped(grad_resid, 2)
-    grad_parts = [grad_resid, swapped(grad_resid, 1), near, swapped(near, 1)]
-    grad_query, *pairs = attend_backward(
-        place, grad_parts, out_proj, proj_near, proj_far, query, pair_parts, mix
-    )
-    pair_sum = sum(
-        [shifted(pairs[j], j, n).astype(F32) for j in range(1, n)], pairs[0].astype(F32)
-    ).astype(BF16)
-
-    cut_own = jnp.stack([cuts[0]] + [shifted(cuts[d], d, n) for d in range(1, n)])
-    cut_line = swapped(cut_own, 2)
-    cut_sets = [cut_own, swapped(cut_own, 1), cut_line, swapped(cut_line, 1)]
-    grad_out_proj = proj_grad(place, mix_all, cut_sets)
-
-    grad_gain = gain_part.reshape(-1, 128)
-    for bit in (1, 2):
-        grad_gain = grad_gain + swapped(grad_gain, bit)
-    grad_gain = sum([shifted(grad_gain, d, n) for d in range(1, n)], grad_gain).reshape(width)
-
-    layer_out = layer_rows(
-        place, sum_back(weighted_rows(place, act_rows, gate, w_down[0], n)), hidden
-    )
+    with scope("gather_cuts"):
+        cut_own = jnp.stack(across(cuts))
+        cut_line = swapped(cut_own, 2)
+        cut_sets = [cut_own, swapped(cut_own, 1), cut_line, swapped(cut_line, 1)]
+    mix_parts = mix_grad_parts(place, cut_sets, out_proj)
+    with scope("sum_mix_grad"):
+        second = (mix_parts[2].astype(F32) + crossed(mix_parts[3], 1).astype(F32)).astype(BF16)
+        mix_grads = [mix_parts[0], crossed(mix_parts[1], 1), crossed(second, 2)]
+
+    normed, act_rows, cut_own = lax.optimization_barrier((normed, act_rows, cut_own, mix_parts[3]))[:3]
+    cut_sets[0] = cut_own
+    grad_w_gate = tn(normed, gate_grad).astype(BF16)
+    grad_w_up = tn(normed, up_grad).astype(BF16)
+    grad_w_down = tn(act_rows, grad_rows).astype(BF16)
+    grad_out_proj = proj_grad(place, mixes, cut_sets)
+    mix_grads[0] = after(mix_grads[0], grad_w_gate, grad_w_up, grad_out_proj)
+
+    grad_query, *pair_parts = attend_backward(place, mix_grads, query, pairs, mixes[0])
+    with scope("sum_pairs"):
+        pair_parts = across(pair_parts)
+        pair_sum = sum([x.astype(F32) for x in pair_parts[1:]], pair_parts[0].astype(F32)).astype(BF16)
+
+    with scope("sum_gain"):
+        grad_gain = after(gain_part.reshape(-1, 128), mix_parts[3])
+        for bit in (1, 2):
+            grad_gain = grad_gain + swapped(grad_gain, bit)
+        grad_gain = sum(across([grad_gain] * n)[1:], grad_gain).reshape(width)
+
+    with scope("sum_outputs"):
+        layer_out = layer_rows(place, sum_back(weighted, summed[:1], summed[1:]), hidden)
     return (
         layer_out,
         grad_resid,
@@ -749,9 +772,9 @@
         pair_sum[:, HEAD_SIZE:],
         grad_out_proj,
         grad_gain,
-        tn(normed, gate_grad).astype(BF16)[None],
-        tn(normed, up_grad).astype(BF16)[None],
-        tn(act_rows, grad_rows).astype(BF16)[None],
+        grad_w_gate[None],
+        grad_w_up[None],
+        grad_w_down[None],
     )
 
 
@@ -764,6 +787,7 @@
         and w_gate.shape[0] == 1
         and key.shape[1] == HEAD_SIZE
         and exp_count == 4
+        and ctx_count == 4
         and lax.axis_size("groups") == 2
     )
     return (local_dense if dense else local_routed)(*args)

time: 227 us -> 195 us (0.86)
  waiting for transfers between devices: 87.2 us -> 67.8 us
  starting transfers between devices: 84 us -> 77.2 us
  local copies, waits for them, and re-layouts: 11.4 us -> 6.02 us
    ppermute x73 -> x82, waiting for transfers between devices: 87.2 us -> 67.8 us  [the longest x33 41 us: crossed(): return lax.ppermute(x, 'ctx', [(i, i ^ bits) for i in range(4)])]
    ppermute x73 -> x82, starting transfers between devices: 84 us -> 77.2 us  [the longest x33 46.1 us: crossed(): return lax.ppermute(x, 'ctx', [(i, i ^ bits) for i in range(4)])]
    pallas_call x9 -> x13, Pallas kernels: 31.2 us -> 33.2 us  [run_kernel(): pl.pallas_call(body, in_specs=[pl.BlockSpec(memory_space=pltpu.SMEM)] + [...]
  transfers between devices with their start and end apart: 73 -> 82, of which waited for: 21 -> 31; matrix products, arithmetic and copies ran while one was open for 8% -> 5% of each run, Pallas kernels for 11% -> 13%
where the time goes in v3:
time: 195 us
  starting transfers between devices  77.2 us (40%)
  waiting for transfers between devices  67.8 us (35%)
  Pallas kernels  33.2 us (17%)
  matrix products  7.03 us (4%)
  local copies, waits for them, and re-layouts  6.02 us (3%)
  other arithmetic  2.31 us (1%)
    ppermute x33, starting transfers between devices, crossed(): return lax.ppermute(x, 'ctx', [(i, i ^ bits) for i in range(4)])  46.1 us
    ppermute x33, waiting for transfers between devices, crossed(): return lax.ppermute(x, 'ctx', [(i, i ^ bits) for i in range(4)])  41 us
    pallas_call x13, Pallas kernels, run_kernel(): pl.pallas_call(body, in_specs=[pl.BlockSpec(memory_space=pltpu.SMEM)] + [...  33.2 us
    ppermute x49, starting transfers between devices, swapped(): return lax.ppermute(x, 'exp', [(i, i ^ bits) for i in range(4)])  31.1 us
    ppermute x49, waiting for transfers between devices, swapped(): return lax.ppermute(x, 'exp', [(i, i ^ bits) for i in range(4)])  26.9 us
    dot_general x3, matrix products, tn(): lax.dot_general(a, b, (((0,), (0,)), ((), ())), preferred_element_type=F32)  7.03 us
  transfers between devices with their start and end apart: 82, of which 31 were waited for; matrix products, arithmetic and copies ran while one was open for 5% of the time, Pallas kernels for 13%

profile of v3, /device:TPU:0, one launch (start us, length us, event | category | flops | bytes accessed | tf_op | source)
XLA Modules:
  0.0 194.7 jit_solution(2301654946201496710)
XLA Ops:
  2.3 4.1 %collective-permute-start.1 = (bf16[128,256]{1,0:T(8,128)(2,1)S(1)}, bf16[128,256]{1,0:T(8,128)(2,1)S(1)}, u32[]{:S(2)}, u32[]{:S(2)}) collective-permute-start(bf16[128,256]{1,0:T(8,128)(2,1)S(1)} %constant_dynamic-update-slice_fusion.refs_0_.refs_4_), channel_id=1, source_target_pairs={{0,8},{4,12},{8,0},{12,4},{1,9},{5,13},{9,1},{13,5},{2,10},{6,14},... | collective-permute-start | bytes 196616 | tf_op jit(solution)/shard_map/gather_pairs/ppermute | solution.py:272
  12.9 2.7 %collective-permute-done.refs_1_.refs_5_ = bf16[128,256]{1,0:T(8,128)(2,1)S(1)} collective-permute-done((bf16[128,256]{1,0:T(8,128)(2,1)S(1)}, bf16[128,256]{1,0:T(8,128)(2,1)S(1)}, u32[]{:S(2)}, u32[]{:S(2)}) %collective-permute-start) | collective-permute-done | bytes 65568 | tf_op jit(solution)/shard_map/gather_pairs/ppermute | solution.py:272
  17.5 7.2 %collective-permute-done.2.refs_3_.refs_7_ = bf16[128,256]{1,0:T(8,128)(2,1)S(1)} collective-permute-done((bf16[128,256]{1,0:T(8,128)(2,1)S(1)}, bf16[128,256]{1,0:T(8,128)(2,1)S(1)}, u32[]{:S(2)}, u32[]{:S(2)}) %collective-permute-start.2) | collective-permute-done | bytes 65568 | tf_op jit(solution)/shard_map/gather_pairs/ppermute | solution.py:272
  26.9 3.0 %attend.4 = (bf16[128,1024]{1,0:T(8,128)(2,1)S(1)}, bf16[2,32,512]{2,1,0:T(8,128)(2,1)S(1)}, bf16[2,32,512]{2,1,0:T(8,128)(2,1)S(1)}) custom-call(s32[2]{0:T(128)S(1)} %pad_add_fusion.place_ref, bf16[128,1024]{1,0:T(8,128)(2,1)S(1)} %copy-done.4, bf16[128,256]{1,0:T(8,128)(2,1)S(1)} %constant_dynamic-update-slice_fusion.refs_0_.refs_4_, ...), custom_call_target="tpu_custom_call" | custom-call | flops 268435456 | bytes 1966080 | tf_op jit(solution)/shard_map/attend/pallas_call | solution.py:308
  30.2 3.0 %attend.6 = (bf16[128,1024]{1,0:T(8,128)(2,1)S(1)}, bf16[2,32,512]{2,1,0:T(8,128)(2,1)S(1)}, bf16[2,32,512]{2,1,0:T(8,128)(2,1)S(1)}) custom-call(s32[2]{0:T(128)S(1)} %pad_add_fusion.place_ref, bf16[128,1024]{1,0:T(8,128)(2,1)S(1)} %collective-permute-done.4.query_ref, bf16[128,256]{1,0:T(8,128)(2,1)S(1)} %constant_dynamic-update-slice_fusion.refs_0_.refs_4_, ...), custom_call_target="tpu_custom_call" | custom-call | flops 268435456 | bytes 1966080 | tf_op jit(solution)/shard_map/attend/pallas_call | solution.py:308
  35.9 3.0 %attend.5 = (bf16[128,1024]{1,0:T(8,128)(2,1)S(1)}, bf16[2,32,512]{2,1,0:T(8,128)(2,1)S(1)}, bf16[2,32,512]{2,1,0:T(8,128)(2,1)S(1)}) custom-call(s32[2]{0:T(128)S(1)} %pad_add_fusion.place_ref, bf16[128,1024]{1,0:T(8,128)(2,1)S(1)} %collective-permute-done.3.query_ref, bf16[128,256]{1,0:T(8,128)(2,1)S(1)} %constant_dynamic-update-slice_fusion.refs_0_.refs_4_, ...), custom_call_target="tpu_custom_call" | custom-call | flops 268435456 | bytes 1966080 | tf_op jit(solution)/shard_map/attend/pallas_call | solution.py:308
  39.0 3.2 %collective-permute-done.5.query_ref = bf16[128,1024]{1,0:T(8,128)(2,1)S(1)} collective-permute-done((bf16[128,1024]{1,0:T(8,128)(2,1)S(1)}, bf16[128,1024]{1,0:T(8,128)(2,1)S(1)}, u32[]{:S(2)}, u32[]{:S(2)}) %collective-permute-start.5) | collective-permute-done | bytes 262176 | tf_op jit(solution)/shard_map/gather_queries/ppermute | solution.py:272
  43.7 3.0 %attend.7 = (bf16[128,1024]{1,0:T(8,128)(2,1)S(1)}, bf16[2,32,512]{2,1,0:T(8,128)(2,1)S(1)}, bf16[2,32,512]{2,1,0:T(8,128)(2,1)S(1)}) custom-call(s32[2]{0:T(128)S(1)} %pad_add_fusion.place_ref, bf16[128,1024]{1,0:T(8,128)(2,1)S(1)} %collective-permute-done.5.query_ref, bf16[128,256]{1,0:T(8,128)(2,1)S(1)} %constant_dynamic-update-slice_fusion.refs_0_.refs_4_, ...), custom_call_target="tpu_custom_call" | custom-call | flops 268435456 | bytes 1966080 | tf_op jit(solution)/shard_map/attend/pallas_call | solution.py:308
  51.9 3.3 %collective-permute-done.14.refs_2_ = bf16[32,2176]{1,0:T(8,128)(2,1)S(1)} collective-permute-done((bf16[32,2176]{1,0:T(8,128)(2,1)S(1)}, bf16[32,2176]{1,0:T(8,128)(2,1)S(1)}, u32[]{:S(2)}, u32[]{:S(2)}) %collective-permute-start.14) | collective-permute-done | bytes 139296 | tf_op jit(solution)/shard_map/gather_grads/ppermute | solution.py:272
  63.0 2.7 %collective-permute-start.24 = (bf16[4,32,512]{2,1,0:T(8,128)(2,1)S(1)}, bf16[4,32,512]{2,1,0:T(8,128)(2,1)S(1)}, u32[]{:S(2)}, u32[]{:S(2)}) collective-permute-start(bf16[4,32,512]{2,1,0:T(8,128)(2,1)S(1)} %hidden_rows.1.refs_0_), channel_id=1, source_target_pairs={{0,8},{4,12},{8,0},{12,4},{1,9},{5,13},{9,1},{13,5},{2,10},{6,14},... | collective-permute-start | bytes 393224 | tf_op jit(solution)/shard_map/gather_hidden/ppermute | solution.py:272
  67.0 5.6 %collective-permute-done.24.refs_2_ = bf16[4,32,512]{2,1,0:T(8,128)(2,1)S(1)} collective-permute-done((bf16[4,32,512]{2,1,0:T(8,128)(2,1)S(1)}, bf16[4,32,512]{2,1,0:T(8,128)(2,1)S(1)}, u32[]{:S(2)}, u32[]{:S(2)}) %collective-permute-start.24) | collective-permute-done | bytes 131104 | tf_op jit(solution)/shard_map/gather_hidden/ppermute | solution.py:272
  90.7 6.2 %expert_rows.1 = (bf16[512,2048]{1,0:T(8,128)(2,1)S(1)}, bf16[512,384]{1,0:T(8,128)(2,1)S(1)}, bf16[512,384]{1,0:T(8,128)(2,1)S(1)}, bf16[512,384]{1,0:T(8,128)(...) custom-call(s32[2]{0:T(128)S(1)} %pad_add_fusion.place_ref, ...), custom_call_target="tpu_custom_call" | custom-call | flops 3221225472 | bytes 11542528 | tf_op jit(solution)/shard_map/expert_rows/pallas_call | solution.py:308
  102.9 2.5 %collective-permute-done.49 = bf16[32,2048]{1,0:T(8,128)(2,1)S(1)} collective-permute-done((bf16[32,2048]{1,0:T(8,128)(2,1)S(1)}, bf16[32,2048]{1,0:T(8,128)(2,1)S(1)}, u32[]{:S(2)}, u32[]{:S(2)}) %collective-permute-start.49) | collective-permute-done | bytes 131104 | tf_op jit(solution)/shard_map/sum_row_grads/ppermute | solution.py:276
  113.5 4.0 %collective-permute-start.59 = (bf16[32,2048]{1,0:T(8,128)(2,1)S(1)}, bf16[32,2048]{1,0:T(8,128)(2,1)S(1)}, u32[]{:S(2)}, u32[]{:S(2)}) collective-permute-start(bf16[32,2048]{1,0:T(8,128)(2,1)S(1)} %get-tuple-element.148), channel_id=1, source_target_pairs={{0,12},{4,8},{8,4},{12,0},{1,13},{5,9},{9,5},{13,1},{2,14},{6,10},... | collective-permute-start | bytes 393224 | tf_op jit(solution)/shard_map/sum_row_grads/ppermute | solution.py:272
  118.1 3.6 %collective-permute-done.59.refs_3_ = bf16[32,2048]{1,0:T(8,128)(2,1)S(1)} collective-permute-done((bf16[32,2048]{1,0:T(8,128)(2,1)S(1)}, bf16[32,2048]{1,0:T(8,128)(2,1)S(1)}, u32[]{:S(2)}, u32[]{:S(2)}) %collective-permute-start.59) | collective-permute-done | bytes 131104 | tf_op jit(solution)/shard_map/sum_row_grads/ppermute | solution.py:272
  121.7 4.9 %collective-permute-done.58.refs_2_ = bf16[32,2048]{1,0:T(8,128)(2,1)S(1)} collective-permute-done((bf16[32,2048]{1,0:T(8,128)(2,1)S(1)}, bf16[32,2048]{1,0:T(8,128)(2,1)S(1)}, u32[]{:S(2)}, u32[]{:S(2)}) %collective-permute-start.58) | collective-permute-done | bytes 131104 | tf_op jit(solution)/shard_map/sum_row_grads/ppermute | solution.py:272
  128.4 2.9 %collective-permute-start.66 = (bf16[32,512]{1,0:T(8,128)(2,1)S(1)}, bf16[32,512]{1,0:T(8,128)(2,1)S(1)}, u32[]{:S(2)}, u32[]{:S(2)}) collective-permute-start(bf16[32,512]{1,0:T(8,128)(2,1)S(1)} %get-tuple-element.115), channel_id=1, source_target_pairs={{0,8},{4,12},{8,0},{12,4},{1,9},{5,13},{9,1},{13,5},{2,10},{6,14},... | collective-permute-start | bytes 98312 | tf_op jit(solution)/shard_map/gather_cuts/ppermute | solution.py:272
  133.2 3.8 %collective-permute-done.67 = bf16[32,512]{1,0:T(8,128)(2,1)S(1)} collective-permute-done((bf16[32,512]{1,0:T(8,128)(2,1)S(1)}, bf16[32,512]{1,0:T(8,128)(2,1)S(1)}, u32[]{:S(2)}, u32[]{:S(2)}) %collective-permute-start.67) | collective-permute-done | bytes 32800 | tf_op jit(solution)/shard_map/gather_cuts/ppermute | solution.py:272
  138.9 3.2 %collective-permute-done.69.refs_2_.refs_6_ = bf16[4,32,512]{2,1,0:T(8,128)(2,1)S(1)} collective-permute-done((bf16[4,32,512]{2,1,0:T(8,128)(2,1)S(1)}, bf16[4,32,512]{2,1,0:T(8,128)(2,1)S(1)}, u32[]{:S(2)}, u32[]{:S(2)}) %collective-permute-start.69) | collective-permute-done | bytes 131104 | tf_op jit(solution)/shard_map/gather_cuts/ppermute | solution.py:276
  145.0 2.4 %convolution_convert_fusion.1 = bf16[2048,384]{1,0:T(8,128)(2,1)} fusion(bf16[512,2048]{1,0:T(8,128)(2,1)S(1)} %get-tuple-element.120, bf16[512,384]{1,0:T(8,128)(2,1)S(1)} %get-tuple-element.122), kind=kOutput, calls=%fused_computation.1 | convolution fusion | flops 806092800 | bytes 4063232 | tf_op jit(solution)/shard_map/dot_general | solution.py:297
  160.0 2.6 %collective-permute-done.61 = bf16[32,2048]{1,0:T(8,128)(2,1)S(1)} collective-permute-done((bf16[32,2048]{1,0:T(8,128)(2,1)S(1)}, bf16[32,2048]{1,0:T(8,128)(2,1)S(1)}, u32[]{:S(2)}, u32[]{:S(2)}) %collective-permute-start.61) | collective-permute-done | bytes 131104 | tf_op jit(solution)/shard_map/sum_outputs/ppermute | solution.py:276
  173.8 2.9 %collective-permute-start.79 = (f32[16,128]{1,0:T(8,128)S(1)}, f32[16,128]{1,0:T(8,128)S(1)}, u32[]{:S(2)}, u32[]{:S(2)}) collective-permute-start(f32[16,128]{1,0:T(8,128)S(1)} %add.205), channel_id=1, source_target_pairs={{0,4},{4,0},{8,12},{12,8},{1,5},{5,1},{9,13},{13,9},{2,6},{6,2},{1... | collective-permute-start | bytes 24584 | tf_op jit(solution)/shard_map/sum_gain/ppermute | solution.py:272
  176.7 4.3 %attend_backward.1 = (bf16[128,1024]{1,0:T(8,128)(2,1)}, bf16[128,256]{1,0:T(8,128)(2,1)S(1)}, bf16[128,256]{1,0:T(8,128)(2,1)S(1)}, bf16[128,256]{1,0:T(8,128)(2,1)S(1)}, bf16[128,256]{1,0:T(8,128)(2,1)S(1)}) custom-call(s32[2]{0:T(128)S(1)} %pad_add_fusion.place_ref, bf16[128,1024]{1,0:T(8,128)(2,1)S(1)} %get-tuple-element.128.refs_0_, ...), custom_call_target="tpu_custom_call" | custom-call | flops 671088640 | bytes 2097152 | tf_op jit(solution)/shard_map/attend_backward/pallas_call | solution.py:308
  190.3 3.7 %collective-permute-done.75 = bf16[128,256]{1,0:T(8,128)(2,1)S(1)} collective-permute-done((bf16[128,256]{1,0:T(8,128)(2,1)S(1)}, bf16[128,256]{1,0:T(8,128)(2,1)S(1)}, u32[]{:S(2)}, u32[]{:S(2)}) %collective-permute-start.75) | collective-permute-done | bytes 65568 | tf_op jit(solution)/shard_map/sum_pairs/ppermute | solution.py:272
  (205 shorter events, 105.6 us)
Async XLA Ops:
  2.3 10.1 %collective-permute-start.1 = (bf16[128,256]{1,0:T(8,128)(2,1)S(1)}, bf16[128,256]{1,0:T(8,128)(2,1)S(1)}, u32[]{:S(2)}, u32[]{:S(2)}) collective-permute-start(bf16[128,256]{1,0:T(8,128)(2,1)S(1)} %constant_dynamic-update-slice_fusion.refs_0_.refs_4_), channel_id=1, source_target_pairs={{0,8},{4,12},{8,0},{12,4},{1,9},{5,13},{9,1},{13,5},{2,10},{6,14},... | collective-permute-start | bytes 196616 | tf_op jit(solution)/shard_map/gather_pairs/ppermute | solution.py:272
  6.4 9.3 %collective-permute-start = (bf16[128,256]{1,0:T(8,128)(2,1)S(1)}, bf16[128,256]{1,0:T(8,128)(2,1)S(1)}, u32[]{:S(2)}, u32[]{:S(2)}) collective-permute-start(bf16[128,256]{1,0:T(8,128)(2,1)S(1)} %constant_dynamic-update-slice_fusion.refs_0_.refs_4_), channel_id=1, source_target_pairs={{0,4},{4,0},{8,12},{12,8},{1,5},{5,1},{9,13},{13,9},{2,6},{6,2},{1... | collective-permute-start | bytes 196616 | tf_op jit(solution)/shard_map/gather_pairs/ppermute | solution.py:272
  8.0 26.8 %collective-permute-start.3 = (bf16[128,1024]{1,0:T(8,128)(2,1)}, bf16[128,1024]{1,0:T(8,128)(2,1)S(1)}, u32[]{:S(2)}, u32[]{:S(2)}) collective-permute-start(bf16[128,1024]{1,0:T(8,128)(2,1)} %refs_3_.1), channel_id=1, source_target_pairs={{0,4},{4,0},{8,12},{12,8},{1,5},{5,1},{9,13},{13,9},{2,6},{6,2},{1... | collective-permute-start | bytes 786440 | tf_op jit(solution)/shard_map/gather_queries/ppermute | solution.py:272
  8.4 21.7 %collective-permute-start.4 = (bf16[128,1024]{1,0:T(8,128)(2,1)}, bf16[128,1024]{1,0:T(8,128)(2,1)S(1)}, u32[]{:S(2)}, u32[]{:S(2)}) collective-permute-start(bf16[128,1024]{1,0:T(8,128)(2,1)} %refs_3_.1), channel_id=1, source_target_pairs={{0,8},{4,12},{8,0},{12,4},{1,9},{5,13},{9,1},{13,5},{2,10},{6,14},... | collective-permute-start | bytes 786440 | tf_op jit(solution)/shard_map/gather_queries/ppermute | solution.py:272
  9.8 36.9 %collective-permute-start.16 = (bf16[32,512]{1,0:T(8,128)(2,1)S(1)}, bf16[32,512]{1,0:T(8,128)(2,1)S(1)}, u32[]{:S(2)}, u32[]{:S(2)}) collective-permute-start(bf16[32,512]{1,0:T(8,128)(2,1)S(1)} %bitcast.101), channel_id=1, source_target_pairs={{0,4},{4,0},{8,12},{12,8},{1,5},{5,1},{9,13},{13,9},{2,6},{6,2},{1... | collective-permute-start | bytes 98312 | tf_op jit(solution)/shard_map/gather_resid/ppermute | solution.py:272
  12.4 12.3 %collective-permute-start.2 = (bf16[128,256]{1,0:T(8,128)(2,1)S(1)}, bf16[128,256]{1,0:T(8,128)(2,1)S(1)}, u32[]{:S(2)}, u32[]{:S(2)}) collective-permute-start(bf16[128,256]{1,0:T(8,128)(2,1)S(1)} %collective-permute-done.1.refs_2_.refs_6_), channel_id=1, source_target_pairs={{0,4},{4,0},{8,12},{12,8},{1,5},{5,1},{9,13},{13,9},{2,6},{6,2},{1... | collective-permute-start | bytes 196616 | tf_op jit(solution)/shard_map/gather_pairs/ppermute | solution.py:272
  15.7 31.7 %collective-permute-start.17 = (bf16[32,512]{1,0:T(8,128)(2,1)S(1)}, bf16[32,512]{1,0:T(8,128)(2,1)S(1)}, u32[]{:S(2)}, u32[]{:S(2)}) collective-permute-start(bf16[32,512]{1,0:T(8,128)(2,1)S(1)} %bitcast.102), channel_id=1, source_target_pairs={{0,8},{4,12},{8,0},{12,4},{1,9},{5,13},{9,1},{13,5},{2,10},{6,14},... | collective-permute-start | bytes 98312 | tf_op jit(solution)/shard_map/gather_resid/ppermute | solution.py:272
  34.8 13.5 %collective-permute-start.18 = (bf16[32,512]{1,0:T(8,128)(2,1)S(1)}, bf16[32,512]{1,0:T(8,128)(2,1)S(1)}, u32[]{:S(2)}, u32[]{:S(2)}) collective-permute-start(bf16[32,512]{1,0:T(8,128)(2,1)S(1)} %bitcast.103), channel_id=1, source_target_pairs={{0,12},{4,8},{8,4},{12,0},{1,13},{5,9},{9,5},{13,1},{2,14},{6,10},... | collective-permute-start | bytes 98312 | tf_op jit(solution)/shard_map/gather_resid/ppermute | solution.py:272
  38.9 10.9 %collective-permute-start.7 = (bf16[2,32,512]{2,1,0:T(8,128)(2,1)S(1)}, bf16[2,32,512]{2,1,0:T(8,128)(2,1)S(1)}, u32[]{:S(2)}, u32[]{:S(2)}) collective-permute-start(bf16[2,32,512]{2,1,0:T(8,128)(2,1)S(1)} %get-tuple-element.80), channel_id=1, source_target_pairs={{0,1},{1,0},{2,3},{3,2},{4,5},{5,4},{6,7},{7,6},{8,9},{9,8},{10,11... | collective-permute-start | bytes 196616 | tf_op jit(solution)/shard_map/sum_heads/ppermute | solution.py:276
  63.0 9.7 %collective-permute-start.24 = (bf16[4,32,512]{2,1,0:T(8,128)(2,1)S(1)}, bf16[4,32,512]{2,1,0:T(8,128)(2,1)S(1)}, u32[]{:S(2)}, u32[]{:S(2)}) collective-permute-start(bf16[4,32,512]{2,1,0:T(8,128)(2,1)S(1)} %hidden_rows.1.refs_0_), channel_id=1, source_target_pairs={{0,8},{4,12},{8,0},{12,4},{1,9},{5,13},{9,1},{13,5},{2,10},{6,14},... | collective-permute-start | bytes 393224 | tf_op jit(solution)/shard_map/gather_hidden/ppermute | solution.py:272
  97.3 12.6 %collective-permute-start.47 = (bf16[4,32,2048]{2,1,0:T(8,128)(2,1)S(1)}, bf16[4,32,2048]{2,1,0:T(8,128)(2,1)S(1)}, u32[]{:S(2)}, u32[]{:S(2)}) collective-permute-start(bf16[4,32,2048]{2,1,0:T(8,128)(2,1)S(1)} %get-tuple-element.93), channel_id=1, source_target_pairs={{0,1},{1,0},{2,3},{3,2},{4,5},{5,4},{6,7},{7,6},{8,9},{9,8},{10,11... | collective-permute-start | bytes 1572872 | tf_op jit(solution)/shard_map/sum_row_grads/ppermute | solution.py:276
  117.5 9.1 %collective-permute-start.58 = (bf16[32,2048]{1,0:T(8,128)(2,1)S(1)}, bf16[32,2048]{1,0:T(8,128)(2,1)S(1)}, u32[]{:S(2)}, u32[]{:S(2)}) collective-permute-start(bf16[32,2048]{1,0:T(8,128)(2,1)S(1)} %get-tuple-element.149), channel_id=1, source_target_pairs={{0,8},{4,12},{8,0},{12,4},{1,9},{5,13},{9,1},{13,5},{2,10},{6,14},... | collective-permute-start | bytes 393224 | tf_op jit(solution)/shard_map/sum_row_grads/ppermute | solution.py:272
  117.5 9.1 %collective-permute-start.57 = (bf16[32,2048]{1,0:T(8,128)(2,1)S(1)}, bf16[32,2048]{1,0:T(8,128)(2,1)S(1)}, u32[]{:S(2)}, u32[]{:S(2)}) collective-permute-start(bf16[32,2048]{1,0:T(8,128)(2,1)S(1)} %get-tuple-element.150), channel_id=1, source_target_pairs={{0,4},{4,0},{8,12},{12,8},{1,5},{5,1},{9,13},{13,9},{2,6},{6,2},{1... | collective-permute-start | bytes 393224 | tf_op jit(solution)/shard_map/sum_row_grads/ppermute | solution.py:272
  138.3 9.1 %collective-permute-start.52 = (bf16[4,32,2048]{2,1,0:T(8,128)(2,1)S(1)}, bf16[4,32,2048]{2,1,0:T(8,128)(2,1)S(1)}, u32[]{:S(2)}, u32[]{:S(2)}) collective-permute-start(bf16[4,32,2048]{2,1,0:T(8,128)(2,1)S(1)} %get-tuple-element.103), channel_id=1, source_target_pairs={{0,1},{1,0},{2,3},{3,2},{4,5},{5,4},{6,7},{7,6},{8,9},{9,8},{10,11... | collective-permute-start | bytes 1572872 | tf_op jit(solution)/shard_map/sum_outputs/ppermute | solution.py:276
  142.1 16.2 %collective-permute-start.51 = (bf16[4,32,2048]{2,1,0:T(8,128)(2,1)S(1)}, bf16[4,32,2048]{2,1,0:T(8,128)(2,1)S(1)}, u32[]{:S(2)}, u32[]{:S(2)}) collective-permute-start(bf16[4,32,2048]{2,1,0:T(8,128)(2,1)S(1)} %get-tuple-element.99), channel_id=1, source_target_pairs={{0,1},{1,0},{2,3},{3,2},{4,5},{5,4},{6,7},{7,6},{8,9},{9,8},{10,11... | collective-permute-start | bytes 1572872 | tf_op jit(solution)/shard_map/sum_outputs/ppermute | solution.py:276
  144.7 12.7 %collective-permute-start.72 = (bf16[128,1024]{1,0:T(8,128)(2,1)S(1)}, bf16[128,1024]{1,0:T(8,128)(2,1)S(1)}, u32[]{:S(2)}, u32[]{:S(2)}) collective-permute-start(bf16[128,1024]{1,0:T(8,128)(2,1)S(1)} %get-tuple-element.119), channel_id=1, source_target_pairs={{0,4},{4,0},{8,12},{12,8},{1,5},{5,1},{9,13},{13,9},{2,6},{6,2},{1... | collective-permute-start | bytes 786440 | tf_op jit(solution)/shard_map/sum_mix_grad/ppermute | solution.py:272
  144.8 23.8 %collective-permute-start.77 = (f32[16,128]{1,0:T(8,128)S(1)}, f32[16,128]{1,0:T(8,128)S(1)}, u32[]{:S(2)}, u32[]{:S(2)}) collective-permute-start(f32[16,128]{1,0:T(8,128)S(1)} %bitcast.97), channel_id=1, source_target_pairs={{0,1},{1,0},{2,3},{3,2},{4,5},{5,4},{6,7},{7,6},{8,9},{9,8},{10,11... | collective-permute-start | bytes 24584 | tf_op jit(solution)/shard_map/sum_gain/ppermute | solution.py:276
  154.0 19.8 %collective-permute-start.71 = (bf16[128,1024]{1,0:T(8,128)(2,1)S(1)}, bf16[128,1024]{1,0:T(8,128)(2,1)S(1)}, u32[]{:S(2)}, u32[]{:S(2)}) collective-permute-start(bf16[128,1024]{1,0:T(8,128)(2,1)S(1)} %get-tuple-element.129), channel_id=1, source_target_pairs={{0,4},{4,0},{8,12},{12,8},{1,5},{5,1},{9,13},{13,9},{2,6},{6,2},{1... | collective-permute-start | bytes 786440 | tf_op jit(solution)/shard_map/sum_mix_grad/ppermute | solution.py:272
  158.3 18.4 %collective-permute-start.73 = (bf16[128,1024]{1,0:T(8,128)(2,1)S(1)}, bf16[128,1024]{1,0:T(8,128)(2,1)S(1)}, u32[]{:S(2)}, u32[]{:S(2)}) collective-permute-start(bf16[128,1024]{1,0:T(8,128)(2,1)S(1)} %add_convert_fusion), channel_id=1, source_target_pairs={{0,8},{4,12},{8,0},{12,4},{1,9},{5,13},{9,1},{13,5},{2,10},{6,14},... | collective-permute-start | bytes 786440 | tf_op jit(solution)/shard_map/sum_mix_grad/ppermute | solution.py:272
  164.2 21.2 %collective-permute-start.62 = (bf16[32,2048]{1,0:T(8,128)(2,1)S(1)}, bf16[32,2048]{1,0:T(8,128)(2,1)S(1)}, u32[]{:S(2)}, u32[]{:S(2)}) collective-permute-start(bf16[32,2048]{1,0:T(8,128)(2,1)S(1)} %get-tuple-element.108), channel_id=1, source_target_pairs={{0,4},{4,0},{8,12},{12,8},{1,5},{5,1},{9,13},{13,9},{2,6},{6,2},{1... | collective-permute-start | bytes 393224 | tf_op jit(solution)/shard_map/sum_outputs/ppermute | solution.py:272
  173.4 10.1 %collective-permute-start.80 = (f32[16,128]{1,0:T(8,128)S(1)}, f32[16,128]{1,0:T(8,128)S(1)}, u32[]{:S(2)}, u32[]{:S(2)}) collective-permute-start(f32[16,128]{1,0:T(8,128)S(1)} %add.205), channel_id=1, source_target_pairs={{0,8},{4,12},{8,0},{12,4},{1,9},{5,13},{9,1},{13,5},{2,10},{6,14},... | collective-permute-start | bytes 24584 | tf_op jit(solution)/shard_map/sum_gain/ppermute | solution.py:272
  173.8 10.8 %collective-permute-start.79 = (f32[16,128]{1,0:T(8,128)S(1)}, f32[16,128]{1,0:T(8,128)S(1)}, u32[]{:S(2)}, u32[]{:S(2)}) collective-permute-start(f32[16,128]{1,0:T(8,128)S(1)} %add.205), channel_id=1, source_target_pairs={{0,4},{4,0},{8,12},{12,8},{1,5},{5,1},{9,13},{13,9},{2,6},{6,2},{1... | collective-permute-start | bytes 24584 | tf_op jit(solution)/shard_map/sum_gain/ppermute | solution.py:272
  176.7 12.3 %collective-permute-start.63 = (bf16[32,2048]{1,0:T(8,128)(2,1)S(1)}, bf16[32,2048]{1,0:T(8,128)(2,1)S(1)}, u32[]{:S(2)}, u32[]{:S(2)}) collective-permute-start(bf16[32,2048]{1,0:T(8,128)(2,1)S(1)} %get-tuple-element.109), channel_id=1, source_target_pairs={{0,8},{4,12},{8,0},{12,4},{1,9},{5,13},{9,1},{13,5},{2,10},{6,14},... | collective-permute-start | bytes 393224 | tf_op jit(solution)/shard_map/sum_outputs/ppermute | solution.py:272
  184.6 9.5 %collective-permute-start.75 = (bf16[128,256]{1,0:T(8,128)(2,1)S(1)}, bf16[128,256]{1,0:T(8,128)(2,1)S(1)}, u32[]{:S(2)}, u32[]{:S(2)}) collective-permute-start(bf16[128,256]{1,0:T(8,128)(2,1)S(1)} %get-tuple-element.134), channel_id=1, source_target_pairs={{0,8},{4,12},{8,0},{12,4},{1,9},{5,13},{9,1},{13,5},{2,10},{6,14},... | collective-permute-start | bytes 196616 | tf_op jit(solution)/shard_map/sum_pairs/ppermute | solution.py:272
  (67 other events, 546.2 us)

commit v4 on v3

--- a/solution.py
+++ b/solution.py
@@ -280,15 +280,6 @@
     return lax.optimization_barrier((x, *others))[0]
 
 
-def from_all(x):
-    far, near = crossed(x, 2), crossed(x, 1)
-    return [x, near, far, crossed(far, 1)]
-
-
-def pick(x, index, axis):
-    return lax.dynamic_index_in_dim(x, index, axis, keepdims=False)
-
-
 def nt(a, b):
     return lax.dot_general(a, b, (((1,), (1,)), ((), ())), preferred_element_type=F32)
 
@@ -301,7 +292,7 @@
     return lax.dot_general(a, b, (((1,), (0,)), ((), ())), preferred_element_type=F32)
 
 
-def run_kernel(body, name, place, args, outs, scratch=(), flops=0, limit=40):
+def run_kernel(body, name, place, args, outs, scratch=(), flops=0, limit=16):
     vmem = pl.BlockSpec(memory_space=pltpu.VMEM)
     shapes = [jax.ShapeDtypeStruct(shape, dtype) for shape, dtype in outs]
     moved = sum(x.size * x.dtype.itemsize for x in list(args) + shapes)
@@ -327,79 +318,147 @@
     return (block < query_block) | ((block == query_block) & diagonal)
 
 
-def attend(place, turn, query, pairs, out_proj):
-    n = len(pairs)
+def pack_heads(place, key, value, query):
     rows, width = query.shape
+
+    def body(place_ref, key_ref, value_ref, query_ref, out_ref):
+        out_ref[:, :HEAD_SIZE] = key_ref[...]
+        out_ref[:, HEAD_SIZE : 2 * HEAD_SIZE] = value_ref[...]
+        out_ref[:, 2 * HEAD_SIZE :] = query_ref[...]
+
+    shape = (rows, width + 2 * HEAD_SIZE)
+    return run_kernel(body, "pack_heads", place, [key, value, query], [(shape, BF16)])[0]
+
+
+def pack_rows(place, grad_out, routes, gate_weights, resid, cols):
+    tok, width = grad_out.shape
+    experts = 4 * (width // cols)
+
+    def body(place_ref, grad_ref, route_ref, weight_ref, resid_ref, far_ref, near_ref, third_ref):
+        lane = lax.broadcasted_iota(jnp.int32, (tok, 128), 1)
+        weight = weight_ref[...]
+        high = weight.astype(BF16).astype(F32)
+        low = weight - high
+        gates = jnp.zeros((tok, 128), F32)
+        for k in range(routes.shape[1]):
+            route = route_ref[:, k : k + 1]
+            gates = gates + jnp.where(lane == route, high[:, k : k + 1], 0.0)
+            gates = gates + jnp.where(lane == route + experts, low[:, k : k + 1], 0.0)
+
+        def columns(turn):
+            return resid_ref[:, pl.ds(pl.multiple_of((place_ref[0] ^ turn) * cols, cols), cols)]
+
+        for ref, turn in ((far_ref, 2), (near_ref, 1)):
+            ref[:, :width] = grad_ref[...]
+            ref[:, width : width + 128] = gates.astype(BF16)
+            ref[:, width + 128 :] = columns(turn)
+        third_ref[...] = columns(3)
+
+    message = ((tok, width + 128 + cols), BF16)
+    return run_kernel(
+        body,
+        "pack_rows",
+        place,
+        [grad_out, routes, gate_weights, resid],
+        [message, message, ((tok, cols), BF16)],
+    )
+
+
+def attend(place, parts, out_proj):
+    n = len(parts)
+    rows = parts[0].shape[0]
+    width = out_proj.shape[0]
     tok = rows // 4
     cols = out_proj.shape[1]
     heads = width // HEAD_SIZE
     factor = HEAD_SIZE ** (-0.5) * LOG2E
 
-    def body(place_ref, query_ref, *refs):
-        proj_ref, mix_ref, keep_ref, send_ref, ks, vs, ps = refs[n:]
+    def body(place_ref, *refs):
+        proj_ref, mix_ref, own_ref, keep_ref, send_ref, pairs_ref, everything, ps = refs[n:]
         c, e = place_ref[0], place_ref[1]
         for r in range(n):
-            ks[r * rows : (r + 1) * rows, :] = refs[r][:, :HEAD_SIZE]
-            vs[r * rows : (r + 1) * rows, :] = refs[r][:, HEAD_SIZE:]
-        visible = visible_keys(rows, n, c ^ turn, c)
-        for head in range(heads):
-            at = slice(head * HEAD_SIZE, (head + 1) * HEAD_SIZE)
-            scores = jnp.where(visible, nt(query_ref[:, at], ks[...]), NEG)
-            peak = jnp.max(scores, -1, keepdims=True)
-            weights = jnp.exp2((scores - peak) * factor)
-            total = jnp.sum(weights, -1, keepdims=True)
-            mix_ref[:, at] = (nn(weights.astype(BF16), vs[...]) / total).astype(BF16)
-        ps[...] = nn(mix_ref[...], proj_ref[...]).astype(BF16)
-        for x in range(2):
-            same, other = e ^ (2 * x), e ^ (2 * x + 1)
-            keep_ref[x] = ps[pl.ds(pl.multiple_of(same * tok, tok), tok), :]
-            send_ref[x] = ps[pl.ds(pl.multiple_of(other * tok, tok), tok), :]
+            everything[pl.ds(pl.multiple_of((c ^ r) * rows, rows), rows), :] = refs[r][...]
+            pairs_ref[r * rows : (r + 1) * rows, :] = refs[r][:, : 2 * HEAD_SIZE]
+        keys, values = everything.at[:, :HEAD_SIZE], everything.at[:, HEAD_SIZE : 2 * HEAD_SIZE]
+        below = lax.broadcasted_iota(jnp.int32, (rows, rows), 1) <= lax.broadcasted_iota(
+            jnp.int32, (rows, rows), 0
+        )
+        for b in range(n):
+            lo, hi = b * rows, (b + 1) * rows
+            for head in range(heads):
+                at = slice(head * HEAD_SIZE, (head + 1) * HEAD_SIZE)
+                query = everything[lo:hi, (head + 2) * HEAD_SIZE : (head + 3) * HEAD_SIZE]
+                scores = nt(query, keys[:hi, :])
+                last = jnp.where(below, scores[:, lo:], NEG)
+                scores = jnp.concatenate([scores[:, :lo], last], 1) if b else last
+                peak = jnp.max(scores, -1, keepdims=True)
+                weights = jnp.exp2((scores - peak) * factor)
+                total = jnp.sum(weights, -1, keepdims=True)
+                mix_ref[lo:hi, at] = (nn(weights.astype(BF16), values[:hi, :]) / total).astype(BF16)
+            ps[...] = nn(mix_ref[lo:hi, :], proj_ref[...]).astype(BF16)
+            for turn in range(2):
+                same, other = e ^ (2 * turn), e ^ (2 * turn + 1)
+                keep_ref[turn, c ^ b] = ps[pl.ds(pl.multiple_of(same * tok, tok), tok), :]
+                send_ref[turn, c ^ b] = ps[pl.ds(pl.multiple_of(other * tok, tok), tok), :]
+        own_ref[...] = mix_ref[pl.ds(pl.multiple_of(c * rows, rows), rows), :]
 
     return run_kernel(
         body,
         "attend",
         place,
-        [query, *pairs, out_proj],
-        [((rows, width), BF16), ((2, tok, cols), BF16), ((2, tok, cols), BF16)],
-        [((n * rows, HEAD_SIZE), BF16), ((n * rows, HEAD_SIZE), BF16), ((rows, cols), BF16)],
-        flops=4 * rows * n * rows * width,
-    )
-
-
-def hidden_rows(place, keep, received, line, resid_parts):
-    n = len(resid_parts)
-
-    def body(place_ref, *refs):
-        for d in range(n):
-            total = refs[d][0].astype(F32) + refs[n + d][0].astype(F32)
-            total = total + refs[2 * n + d][...].astype(F32) + refs[3 * n + d][...].astype(F32)
-            refs[4 * n][d] = total.astype(BF16)
+        [*parts, out_proj],
+        [
+            ((n * rows, width), BF16),
+            ((rows, width), BF16),
+            ((2, n, tok, cols), BF16),
+            ((2, n, tok, cols), BF16),
+            ((n * rows, 2 * HEAD_SIZE), BF16),
+        ],
+        [((n * rows, width + 2 * HEAD_SIZE), BF16), ((rows, cols), BF16)],
+        flops=4 * n * rows * n * rows * width,
+    )
+
+
+def hidden_rows(place, keep, received, line, resid, near, far, third):
+    cols = line.shape[2]
+    last = near.shape[1] - cols
+
+    def body(place_ref, keep_ref, received_ref, line_ref, resid_ref, near_ref, far_ref, third_ref, out_ref):
+        total = keep_ref[0].astype(F32) + received_ref[0].astype(F32) + line_ref[...].astype(F32)
+        own = resid_ref[:, pl.ds(pl.multiple_of(place_ref[0] * cols, cols), cols)]
+        blocks = [own, near_ref[:, last:], far_ref[:, last:], third_ref[...]]
+        for r, block in enumerate(blocks):
+            out_ref[r] = (total[r] + block.astype(F32)).astype(BF16)
 
     return run_kernel(
         body,
         "hidden_rows",
         place,
-        [*keep, *received, *line, *resid_parts],
-        [((n, *line[0].shape), BF16)],
+        [keep, received, line, resid, near, far, third],
+        [(line.shape, BF16)],
     )[0]
 
 
-def grad_rows_of(place, grad_sets, w_down, width):
-    n, tok = len(grad_sets[0]), grad_sets[0][0].shape[0]
+def grad_rows_of(place, grad_sets, w_down):
+    lead, tok = grad_sets[0][0].shape[:2]
+    n = lead + 1
     total = 4 * n * tok
     experts = 4 * n
+    units, width = w_down.shape
 
     def body(place_ref, *refs):
-        down_ref, rows_ref, gate_ref, act_ref = refs[4 * n :]
+        down_ref, rows_ref, gate_ref, act_ref = refs[8:]
         expert = place_ref[0] * 4 + place_ref[1]
         lane = lax.broadcasted_iota(jnp.int32, (tok, 128), 1)
         wanted = (lane == expert) | (lane == expert + experts)
-        for s in range(4 * n):
-            at = slice(s * tok, (s + 1) * tok)
-            gate = jnp.where(wanted, refs[s][:, width:].astype(F32), 0.0)
-            gate = jnp.sum(gate, -1, keepdims=True)
-            gate_ref[at, :] = gate
-            rows_ref[at, :] = (refs[s][:, :width].astype(F32) * gate).astype(BF16)
+        for s in range(4):
+            for j in range(n):
+                at = slice((s * n + j) * tok, (s * n + j + 1) * tok)
+                block = refs[2 * s].at[j] if j < lead else refs[2 * s + 1]
+                gate = jnp.where(wanted, block[:, width:].astype(F32), 0.0)
+                gate = jnp.sum(gate, -1, keepdims=True)
+                gate_ref[at, :] = gate
+                rows_ref[at, :] = (block[:, :width].astype(F32) * gate).astype(BF16)
         act_ref[...] = nt(rows_ref[...], down_ref[...])
 
     return run_kernel(
@@ -407,8 +466,9 @@
         "grad_rows",
         place,
         [*sum(grad_sets, []), w_down],
-        [((total, width), BF16), ((total, 1), F32), ((total, w_down.shape[0]), F32)],
-        flops=2 * total * width * w_down.shape[0],
+        [((total, width), BF16), ((total, 1), F32), ((total, units), F32)],
+        flops=2 * total * width * units,
+        limit=24,
     )
 
 
@@ -422,7 +482,7 @@
         pieces = refs[: 4 * n]
         act_grad_ref, gain_ref, gate_ref, up_ref = refs[4 * n : 4 * n + 4]
         normed_ref, act_ref, gate_grad_ref, up_grad_ref, own_ref = refs[4 * n + 4 : 4 * n + 9]
-        grads, hid = refs[4 * n + 9 : 4 * n + 13], refs[4 * n + 13]
+        grads, sides, hid = refs[4 * n + 9 : 4 * n + 13], refs[4 * n + 13 : 4 * n + 15], refs[4 * n + 15]
         c = place_ref[0]
         for s in range(4):
             for d in range(n):
@@ -448,8 +508,11 @@
             at = slice(j * cols, (j + 1) * cols)
             part = nt(gate_grad_ref[...], gate_ref[at, :]) + nt(up_grad_ref[...], up_ref[at, :])
             for s in range(4):
-                block = part[s * group : (s + 1) * group].astype(BF16)
-                grads[s][:, :, at] = block.reshape(n, tok, cols)
+                block = part[s * group : (s + 1) * group].astype(BF16).reshape(n, tok, cols)
+                if j < n - 1:
+                    grads[s][:, :, at] = block
+                else:
+                    sides[s // 2][:, s % 2] = block
 
     units = ((total, hidden_units), BF16)
     return run_kernel(
@@ -458,9 +521,11 @@
         place,
         [*sum(hidden_sets, []), act_grad, norm_gain.reshape(1, width), w_gate, w_up],
         [((total, width), BF16), units, units, units, ((tok, width), BF16)]
-        + [((n, tok, width), BF16)] * 4,
+        + [((n, tok, width - cols), BF16)] * 4
+        + [((n, 2, tok, cols), BF16)] * 2,
         [((total, width), BF16)],
         flops=8 * total * width * hidden_units,
+        limit=32,
     )
 
 
@@ -475,66 +540,70 @@
             part = nn(act_ref[...], down_ref[:, at]).astype(BF16).astype(F32) * gate_ref[...]
             for s in range(4):
                 block = part[s * group : (s + 1) * group].astype(BF16)
-                outs[s][:, :, at] = block.reshape(n, group // n, cols)
+                outs[s // 2][s % 2, :, :, at] = block.reshape(n, group // n, cols)
 
     return run_kernel(
         body,
         "weighted_rows",
         place,
         [act_rows, gate, w_down],
-        [((n, group // n, width), BF16)] * 4,
+        [((2, n, group // n, width), BF16)] * 2,
         flops=2 * total * width * w_down.shape[0],
     )
 
 
-def sum_back(parts, before_exp=(), before_ctx=(), beside=()):
-    def add(*xs):
-        return sum([x.astype(F32) for x in xs[1:]], xs[0].astype(F32)).astype(BF16)
-
-    if before_exp:
-        parts = [after(x, *before_exp) for x in parts]
-    far, near = swapped(parts[3], 1), swapped(parts[2], 1)
-    line = {}
-    for j in (3, 2, 1, 0):
-        part = add(parts[1][j], far[j])
-        if j == 1:
-            part = after(part, line[3], *beside)
-        elif j == 0:
-            part = after(part, line[2])
-        line[j] = swapped(part, 2)
-    sums = [add(parts[0][j], near[j], line[j]) for j in range(4)]
-    if before_ctx:
-        sums = [after(x, *before_ctx) for x in sums]
-    return [sums[0]] + [crossed(sums[j], j) for j in (1, 2, 3)]
-
-
-def norm_backward(place, summed, hidden, grad_out, norm_gain, cols):
-    n = len(summed)
+def add(*xs):
+    return sum([x.astype(F32) for x in xs[1:]], xs[0].astype(F32)).astype(BF16)
+
+
+def sum_rows(parts, keep, send, beside, ready):
+    side = swapped(send, 1)
+    far = after(swapped(parts[3], 1), beside, side, ready)
+    near = swapped(parts[2], 1)
+    line = swapped(add(parts[1], far), 2)
+    sides = [add(keep[j], side[j]) for j in range(4)]
+    got = [crossed(sides[j], j) for j in range(1, 4)]
+    total = add(sides[0], *got)
+    sums = [after(add(parts[0][j], near[j], line[j]), total) for j in range(4)]
+    wide = [sums[0]] + [crossed(sums[j], j) for j in range(1, 4)]
+    return wide, [total[0], swapped(total[1], 2)]
+
+
+def norm_backward(place, wide, narrow, hidden, grad_out, norm_gain, cols):
+    n = len(wide) + len(narrow)
     tok, width = hidden.shape
     blocks = width // cols
 
     def body(place_ref, *refs):
         hidden_ref, grad_ref, gain_ref = refs[n : n + 3]
-        out_ref, part_ref, cuts = refs[n + 3], refs[n + 4], refs[n + 5 :]
+        out_ref, cuts, part_ref = refs[n + 3], refs[n + 4 : -1], refs[-1]
         c = place_ref[0]
-        normed_grad = sum([r[...].astype(F32) for r in refs[1:n]], refs[0][...].astype(F32))
+        sums = [[r[...].astype(F32) for r in rs] for rs in (refs[: len(wide)], refs[len(wide) : n])]
+        normed_grad = jnp.concatenate([sum(x[1:], x[0]) for x in sums], 1)
         value = hidden_ref[...].astype(F32)
         inv_rms = lax.rsqrt(jnp.mean(value * value, -1, keepdims=True) + EPS)
         unit_rows = value * inv_rms
-        part_ref[...] = jnp.sum(normed_grad * unit_rows, 0, keepdims=True)
+        part = jnp.sum(normed_grad * unit_rows, 0, keepdims=True)
+        high = part.astype(BF16)
+        spare = jnp.zeros((14, width), BF16)
+        part_ref[...] = jnp.concatenate([high, (part - high.astype(F32)).astype(BF16), spare], 0)
         scaled = gain_ref[...] * normed_grad
         mean = jnp.mean(scaled * unit_rows, -1, keepdims=True)
         grad = grad_ref[...].astype(F32) + inv_rms * (scaled - unit_rows * mean)
         out_ref[...] = grad.astype(BF16)
         for d in range(blocks):
-            cuts[d][...] = out_ref[:, pl.ds(pl.multiple_of((c ^ d) * cols, cols), cols)]
+            at = pl.ds(pl.multiple_of((c ^ d) * cols, cols), cols)
+            to = slice(d % 2 * cols, (d % 2 + 1) * cols)
+            cuts[d // 2][:tok, to] = out_ref[:, at]
+            cuts[d // 2][tok:, to] = part_ref[:, at]
 
     return run_kernel(
         body,
         "norm_backward",
         place,
-        [*summed, hidden, grad_out, norm_gain.reshape(1, width)],
-        [((tok, width), BF16), ((1, width), F32)] + [((tok, cols), BF16)] * blocks,
+        [*wide, *narrow, hidden, grad_out, norm_gain.reshape(1, width)],
+        [((tok, width), BF16)] + [((tok + 16, 2 * cols), BF16)] * (blocks // 2),
+        [((16, width), BF16)],
     )
 
 
@@ -548,51 +617,61 @@
     return run_kernel(body, "layer_rows", place, [*summed, hidden], [(hidden.shape, BF16)])[0]
 
 
-def mix_grad_parts(place, cut_sets, out_proj):
-    n, tok, cols = cut_sets[0].shape
+def mix_grad_parts(place, cut_sets, out_proj, proj_here, proj_there):
+    count, cut, cols = cut_sets[0].shape
+    tok, cols = cut - 16, cols // 2
     rows, width = 4 * tok, out_proj.shape[0]
 
     def body(place_ref, *refs):
-        proj_ref, outs, grads = refs[4], refs[5 : 5 + n], refs[5 + n]
-        e = place_ref[1]
-        for d in range(n):
+        proj_ref, here_ref, there_ref, own_ref, far_ref, keep_ref, send_ref, grads, acc = refs[4:]
+        e, g = place_ref[1], place_ref[2]
+        gain = sum([refs[r][i, tok : tok + 2, :].astype(F32) for r in range(4) for i in range(count)])
+        gain = jnp.sum(gain, 0, keepdims=True)
+        high = gain.astype(BF16)
+        spare = jnp.zeros((14, 2 * cols), BF16)
+        gain = jnp.concatenate([high, (gain - high.astype(F32)).astype(BF16), spare], 0)
+        for i in range(count):
             for r in range(4):
-                at = pl.multiple_of(d * rows + (e ^ r) * tok, tok)
-                grads[pl.ds(at, tok), :] = refs[r][d]
-        for half in range(2):
-            at = slice(half * width // 2, (half + 1) * width // 2)
-            part = nt(grads[...], proj_ref[at, :]).astype(BF16)
-            for d in range(n):
-                outs[d][:, at] = part[d * rows : (d + 1) * rows]
+                at = pl.multiple_of(i * rows + (e ^ r) * tok, tok)
+                grads[pl.ds(at, tok), :] = refs[r][i, :tok, :]
+        for ref, at in ((keep_ref, slice(0, cols)), (send_ref, slice(cols, 2 * cols))):
+            ref[: count * rows, :] = grads[:, at]
+            ref[count * rows :, :] = gain[:, at]
+        half = width // 2
+        for ref, index in ((here_ref, g), (there_ref, 1 - g)):
+            at = pl.ds(pl.multiple_of(index * half, half), half)
+            acc[:, at] = nt(grads[:, cols:], ref[...])
+        for h in range(2):
+            at = slice(h * half, (h + 1) * half)
+            total = (acc[:, at] + nt(grads[:, :cols], proj_ref[at, :])).astype(BF16)
+            own_ref[:, at] = total[:rows]
+            far_ref[:, at] = total[rows:]
 
     return run_kernel(
         body,
         "mix_grad_parts",
         place,
-        [*cut_sets, out_proj],
-        [((rows, width), BF16)] * n,
-        [((n * rows, cols), BF16)],
-        flops=2 * n * rows * cols * width,
-    )
-
-
-def attend_backward(place, grad_parts, query, pairs, mix):
-    n, g = len(pairs), len(grad_parts)
+        [*cut_sets, out_proj, proj_here, proj_there],
+        [((rows, width), BF16)] * 2 + [((count * rows + 16, cols), BF16)] * 2,
+        [((count * rows, 2 * cols), BF16), ((count * rows, width), F32)],
+        flops=4 * count * rows * cols * width,
+    )
+
+
+def attend_backward(place, grad_parts, query, pairs, mix, gain):
+    g = len(grad_parts)
     rows, width = mix.shape
+    n = pairs.shape[0] // rows
     heads = width // HEAD_SIZE
     scale = HEAD_SIZE ** (-0.5)
 
     def body(place_ref, *refs):
-        g_refs, query_ref = refs[:g], refs[g]
-        p_refs = refs[g + 1 : g + 1 + n]
-        mix_ref, dq_ref = refs[g + 1 + n : g + 3 + n]
-        outs = refs[g + 3 + n : g + 3 + 2 * n]
-        qs, ms, ks, vs, score_half, prob_half = refs[g + 3 + 2 * n :]
+        g_refs, (query_ref, pairs_ref, mix_ref, gain_ref, dq_ref) = refs[:g], refs[g : g + 5]
+        outs = refs[g + 5 : g + 5 + n]
+        qs, ms, score_half, prob_half = refs[g + 5 + n :]
+        ks, vs = pairs_ref.at[:, :HEAD_SIZE], pairs_ref.at[:, HEAD_SIZE:]
         c = place_ref[0]
         visible = visible_keys(rows, n, c, c)
-        for d in range(n):
-            ks[d * rows : (d + 1) * rows, :] = p_refs[d][:, :HEAD_SIZE]
-            vs[d * rows : (d + 1) * rows, :] = p_refs[d][:, HEAD_SIZE:]
         for head in range(heads):
             at = slice(head * HEAD_SIZE, (head + 1) * HEAD_SIZE)
             rs = slice(head * rows, (head + 1) * rows)
@@ -612,46 +691,76 @@
         value_sum = tn(prob_half[...], ms[...]).astype(BF16)
         for j in range(n):
             rs = slice(j * rows, (j + 1) * rows)
-            outs[j][:, :HEAD_SIZE] = key_sum[rs]
-            outs[j][:, HEAD_SIZE:] = value_sum[rs]
+            outs[j][:rows, :HEAD_SIZE] = key_sum[rs]
+            outs[j][:rows, HEAD_SIZE:] = value_sum[rs]
+            outs[j][rows:, :] = gain_ref[...]
 
     stacked = ((heads * rows, HEAD_SIZE), BF16)
-    keys = ((n * rows, HEAD_SIZE), BF16)
     halves = ((heads * rows, n * rows), BF16)
     return run_kernel(
         body,
         "attend_backward",
         place,
-        [*grad_parts, query, *pairs, mix],
-        [((rows, width), BF16)] + [((rows, 2 * HEAD_SIZE), BF16)] * n,
-        [stacked, stacked, keys, keys, halves, halves],
+        [*grad_parts, query, pairs, mix, gain],
+        [((rows, width), BF16)] + [((rows + 16, 2 * HEAD_SIZE), BF16)] * n,
+        [stacked, stacked, halves, halves],
         flops=10 * rows * width * n * rows,
     )
 
 
-def proj_grad(place, mixes, cut_sets):
-    n, tok, cols = cut_sets[0].shape
-    rows, width = mixes[0].shape
+def proj_grad(place, mix_all, keep, near):
+    total, width = mix_all.shape
+    rows, cols = total // 4, keep.shape[1]
+
+    def body(place_ref, mix_ref, keep_ref, near_ref, out_ref, gain_ref, grads):
+        c = place_ref[0]
+        for d in range(4):
+            ref = near_ref if d % 2 else keep_ref
+            at = pl.multiple_of((c ^ d) * rows, rows)
+            grads[pl.ds(at, rows), :] = ref[d // 2 * rows : (d // 2 + 1) * rows, :]
+        out_ref[...] = tn(mix_ref[...], grads[...]).astype(BF16)
+        gain = keep_ref[2 * rows :, :].astype(F32) + near_ref[2 * rows :, :].astype(F32)
+        gain = jnp.sum(gain[:2], 0, keepdims=True)
+        high = gain.astype(BF16)
+        low = (gain - high.astype(F32)).astype(BF16)
+        pieces = [x[:, i : i + cols // 2] for x in (high, low) for i in (0, cols // 2)]
+        gain_ref[...] = jnp.concatenate([*pieces, jnp.zeros((12, cols // 2), BF16)], 0)
+
+    return run_kernel(
+        body,
+        "proj_grad",
+        place,
+        [mix_all, keep, near],
+        [((width, cols), BF16), ((16, cols // 2), BF16)],
+        [((total, cols), BF16)],
+        flops=2 * total * cols * width,
+    )
+
+
+def pair_sums(place, parts):
+    n = len(parts)
+    rows = parts[0].shape[0] - 16
+    half = parts[0].shape[1]
 
     def body(place_ref, *refs):
-        out_ref, grads, mix = refs[n + 4 :]
-        e = place_ref[1]
-        for d in range(n):
-            mix[d * rows : (d + 1) * rows, :] = refs[d][...]
-            for r in range(4):
-                at = pl.multiple_of(d * rows + (e ^ r) * tok, tok)
-                grads[pl.ds(at, tok), :] = refs[n + r][d]
-        out_ref[...] = tn(mix[...], grads[...]).astype(BF16)
-
-    return run_kernel(
-        body,
-        "proj_grad",
-        place,
-        [*mixes, *cut_sets],
-        [((width, cols), BF16)],
-        [((n * rows, cols), BF16), ((n * rows, width), BF16)],
-        flops=8 * n * tok * cols * width,
-    )[0]
+        key_ref, value_ref, gain_ref = refs[n:]
+        c = place_ref[0]
+        total = sum([r[:rows, :].astype(F32) for r in refs[1:n]], refs[0][:rows, :].astype(F32))
+        key_ref[...] = total[:, :HEAD_SIZE].astype(BF16)
+        value_ref[...] = total[:, HEAD_SIZE:].astype(BF16)
+        for j in range(n):
+            tail = refs[j][rows:, :].astype(F32)
+            for i in range(2):
+                at = pl.multiple_of(((c ^ j) * 2 + i) * half, half)
+                gain_ref[:, pl.ds(at, half)] = tail[i : i + 1] + tail[i + 2 : i + 3]
+
+    return run_kernel(
+        body,
+        "pair_sums",
+        place,
+        parts,
+        [((rows, HEAD_SIZE), BF16), ((rows, HEAD_SIZE), BF16), ((1, 2 * n * half), F32)],
+    )
 
 
 def local_dense(
@@ -669,109 +778,117 @@
     grad_out,
 ):
     n = lax.axis_size("ctx")
-    c, e = lax.axis_index("ctx"), lax.axis_index("exp")
-    place = jnp.stack([c, e]).astype(jnp.int32)
+    c, e, g = lax.axis_index("ctx"), lax.axis_index("exp"), lax.axis_index("groups")
+    place = jnp.stack([c, e, g]).astype(jnp.int32)
     tok, width = resid.shape
     cols = out_proj.shape[1]
-    experts = 4 * n
     scope = jax.named_scope
 
     def across(blocks):
         return [blocks[0]] + [crossed(blocks[r], r) for r in range(1, n)]
 
-    with scope("gather_pairs"):
-        pairs = from_all(jnp.concatenate([key, value], 1))
-    with scope("gather_queries"):
-        queries = from_all(query)
-
-    gates = jnp.sum(
-        jnp.where(
-            routes[:, :, None] == jnp.arange(experts, dtype=jnp.int32), gate_weights[:, :, None], 0.0
-        ),
-        1,
-    )
-    gate_high = lax.reduce_precision(gates, 8, 7)
-    payload = jnp.concatenate(
-        [
-            grad_out,
-            gate_high.astype(BF16),
-            (gates - gate_high).astype(BF16),
-            jnp.zeros((tok, 128 - 2 * experts), BF16),
-        ],
-        1,
-    )
-    with scope("gather_resid"):
-        resid_cut = resid.reshape(tok, n, cols)
-        resid_parts = across([pick(resid_cut, c ^ r, 1) for r in range(n)])
-    with scope("gather_grads"):
-        grad_own = from_all(after(payload, *queries[1:3]))
-        grad_line = [swapped(payload, 2)] + [swapped(x, 2) for x in grad_own[1:]]
+    with scope("gather_rows"):
+        to_far, to_near, to_third = pack_rows(place, grad_out, routes, gate_weights, resid, cols)
+    with scope("gather_heads"):
+        heads = pack_heads(place, key, value, query)
+        far, near = crossed(heads, 2), crossed(heads, 1)
+        parts = [heads, near, far, crossed(after(far, to_far, to_near, to_third), 1)]
+
+    with scope("gather_rows"):
+        row_third = crossed(after(to_third, far, near), 3)
+        parts[3] = after(parts[3], row_third)
+        to_far, to_near = lax.optimization_barrier((to_far, to_near, parts[3]))[:2]
+        row_far, row_near = crossed(to_far, 2), crossed(to_near, 1)
+
+    mix_all, mix, keep, send, pairs = attend(place, parts, out_proj)
+    with scope("sum_heads"):
+        received = swapped(send, 1)
+        line = swapped(add(keep[1], received[1]), 2)
+    hidden_block = hidden_rows(
+        place, keep, received, line, resid, row_near, row_far, row_third
+    )
+    with scope("gather_rows"):
+        size = width + 128
+        to_far, row_far, row_near = lax.optimization_barrier((to_far, row_far, row_near, line))[:3]
+        rest = crossed(row_far[:, :size], 1)
+        grad_own = jnp.stack([to_far[:, :size], row_near[:, :size], row_far[:, :size]])
+        grad_own, grad_line = [grad_own, rest], [swapped(grad_own, 2), swapped(rest, 2)]
         grad_sets = [grad_own, grad_line] + [
-            [swapped(x, 1) for x in xs] for xs in (grad_own, grad_line)
+            [swapped(after(x, grad_line[1]), 1) for x in xs] for xs in (grad_own, grad_line)
         ]
-    grad_rows, gate, act_grad = grad_rows_of(place, grad_sets, w_down[0], width)
-
-    mixes, keep, send = zip(*[attend(place, r, queries[r], pairs, out_proj) for r in range(n)])
-    with scope("sum_heads"):
-        received = [swapped(x, 1) for x in send]
-        sums = [(k[1].astype(F32) + r[1].astype(F32)).astype(BF16) for k, r in zip(keep, received)]
-        sums[3] = after(sums[3], *grad_own[1:3])
-        line = [swapped(x, 2) for x in sums]
-    hidden_block = hidden_rows(place, keep, received, line, resid_parts)
+    grad_rows, gate, act_grad = grad_rows_of(place, grad_sets, w_down[0])
+
     with scope("gather_hidden"):
-        hidden_own = from_all(after(hidden_block, grad_own[3], *grad_line[:3]))
-        hidden_line = [swapped(x, 2) for x in hidden_own]
-        hidden_line[-1], act_grad = lax.optimization_barrier((hidden_line[-1], act_grad))
+        far, near = crossed(hidden_block, 2), crossed(hidden_block, 1)
+        line = swapped(hidden_block, 2)
+        hidden_own = [hidden_block, near, far, crossed(after(far, near), 1)]
+        hidden_line = [line] + [swapped(after(x, line), 2) for x in hidden_own[1:3]]
+        hidden_line.append(swapped(after(hidden_own[3], *hidden_line), 2))
+    with scope("gather_proj"):
+        half = out_proj.shape[0] // 2
+        proj_half = lax.dynamic_slice_in_dim(out_proj, g * half, half, 0)
+        proj_here = crossed(after(proj_half, hidden_own[3]), 1)
+    with scope("gather_hidden"):
+        hidden_line[-1], act_grad, proj_here = lax.optimization_barrier(
+            (hidden_line[-1], act_grad, proj_here)
+        )
         hidden_sets = [hidden_own, hidden_line] + [
             [swapped(x, 1) for x in xs] for xs in (hidden_own, hidden_line)
         ]
 
+    with scope("gather_proj"):
+        proj_there = lax.ppermute(proj_here, "groups", [(0, 1), (1, 0)])
+
     normed, act_rows, gate_grad, up_grad, hidden, *row_grads = expert_rows(
         place, hidden_sets, act_grad, norm_gain, w_gate[0], w_up[0]
     )
-    weighted = weighted_rows(place, act_rows, gate, w_down[0], n)
+    out_keep, out_send = weighted_rows(place, act_rows, gate, w_down[0], n)
     with scope("sum_row_grads"):
-        summed = sum_back(row_grads, beside=weighted[:1])
-    grad_resid, gain_part, *cuts = norm_backward(place, summed, hidden, grad_out, norm_gain, cols)
+        wide, narrow = sum_rows(row_grads[:4], *row_grads[4:], out_keep, proj_there)
+
+    with scope("sum_outputs"):
+        out_sent = swapped(out_send, 1)
+        out_line = swapped(after(add(out_keep[1], out_sent[1]), wide[0]), 2)
+    grad_resid, *cuts = norm_backward(
+        place, wide, narrow, after(hidden, out_line), grad_out, norm_gain, cols
+    )
 
     with scope("gather_cuts"):
-        cut_own = jnp.stack(across(cuts))
+        cut_own = jnp.stack([cuts[0], crossed(cuts[1], 2)])
         cut_line = swapped(cut_own, 2)
         cut_sets = [cut_own, swapped(cut_own, 1), cut_line, swapped(cut_line, 1)]
-    mix_parts = mix_grad_parts(place, cut_sets, out_proj)
+    mix_own, mix_far, cut_keep, cut_send = mix_grad_parts(
+        place, cut_sets, out_proj, proj_here, proj_there
+    )
     with scope("sum_mix_grad"):
-        second = (mix_parts[2].astype(F32) + crossed(mix_parts[3], 1).astype(F32)).astype(BF16)
-        mix_grads = [mix_parts[0], crossed(mix_parts[1], 1), crossed(second, 2)]
-
-    normed, act_rows, cut_own = lax.optimization_barrier((normed, act_rows, cut_own, mix_parts[3]))[:3]
-    cut_sets[0] = cut_own
+        mix_grads = [mix_own, crossed(mix_far, 2)]
+    with scope("gather_cuts"):
+        cut_near = crossed(cut_send, 1)
+
+    with scope("sum_outputs"):
+        out_sums = [add(out_keep[0][j], out_sent[0][j], out_line[j]) for j in range(n)]
+        out_sums = [after(x, cut_own) for x in out_sums]
+        out_sums = [out_sums[0]] + [crossed(out_sums[j], j) for j in range(1, n)]
+    normed, act_rows = lax.optimization_barrier((normed, act_rows, mix_own))[:2]
     grad_w_gate = tn(normed, gate_grad).astype(BF16)
     grad_w_up = tn(normed, up_grad).astype(BF16)
     grad_w_down = tn(act_rows, grad_rows).astype(BF16)
-    grad_out_proj = proj_grad(place, mixes, cut_sets)
-    mix_grads[0] = after(mix_grads[0], grad_w_gate, grad_w_up, grad_out_proj)
-
-    grad_query, *pair_parts = attend_backward(place, mix_grads, query, pairs, mixes[0])
+    grad_out_proj, gain_rows = proj_grad(place, mix_all, cut_keep, cut_near)
+    mix_grads[0] = after(mix_own, grad_w_gate, grad_w_up, *out_sums[1:])
+
+    grad_query, *pair_parts = attend_backward(place, mix_grads, query, pairs, mix, gain_rows)
     with scope("sum_pairs"):
-        pair_parts = across(pair_parts)
-        pair_sum = sum([x.astype(F32) for x in pair_parts[1:]], pair_parts[0].astype(F32)).astype(BF16)
-
-    with scope("sum_gain"):
-        grad_gain = after(gain_part.reshape(-1, 128), mix_parts[3])
-        for bit in (1, 2):
-            grad_gain = grad_gain + swapped(grad_gain, bit)
-        grad_gain = sum(across([grad_gain] * n)[1:], grad_gain).reshape(width)
-
-    with scope("sum_outputs"):
-        layer_out = layer_rows(place, sum_back(weighted, summed[:1], summed[1:]), hidden)
+        key_gradient, value_gradient, grad_gain = pair_sums(place, across(pair_parts))
+    layer_out = layer_rows(place, out_sums, after(hidden, grad_query))
+
     return (
         layer_out,
         grad_resid,
         grad_query,
-        pair_sum[:, :HEAD_SIZE],
-        pair_sum[:, HEAD_SIZE:],
+        key_gradient,
+        value_gradient,
         grad_out_proj,
-        grad_gain,
+        grad_gain.reshape(width),
         grad_w_gate[None],
         grad_w_up[None],
         grad_w_down[None],

time: 195 us -> 186 us (0.954)
  starting transfers between devices: 77.2 us -> 56.6 us
  waiting for transfers between devices: 67.8 us -> 79.2 us
    ppermute x33 -> x26, waiting for transfers between devices: 41 us -> 59.4 us  [crossed(): return lax.ppermute(x, 'ctx', [(i, i ^ bits) for i in range(4)])]
    ppermute x49 -> x30, starting transfers between devices: 31.1 us -> 17.2 us  [swapped(): return lax.ppermute(x, 'exp', [(i, i ^ bits) for i in range(4)])]
    ppermute x49 -> x30, waiting for transfers between devices: 26.9 us -> 17 us  [swapped(): return lax.ppermute(x, 'exp', [(i, i ^ bits) for i in range(4)])]
    ppermute x33 -> x26, starting transfers between devices: 46.1 us -> 37.8 us  [crossed(): return lax.ppermute(x, 'ctx', [(i, i ^ bits) for i in range(4)])]
    unnamed x23 -> x42, local copies, waits for them, and re-layouts: 3.11 us -> 7.1 us
    ppermute x0 -> x1, waiting for transfers between devices: none -> 2.76 us  [local_dense(): proj_there = lax.ppermute(proj_here, 'groups', [(0, 1), (1, 0)])]
  transfers between devices with their start and end apart: 82 -> 57, of which waited for: 31 -> 24; matrix products, arithmetic and copies ran while one was open for 5% -> 5% of each run, Pallas kernels for 13% -> 10%
where the time goes in v4:
time: 186 us
  waiting for transfers between devices  79.2 us (43%)
  starting transfers between devices  56.6 us (30%)
  Pallas kernels  34 us (18%)
  local copies, waits for them, and re-layouts  7.18 us (4%)
  matrix products  7.06 us (4%)
    ppermute x26, waiting for transfers between devices, crossed(): return lax.ppermute(x, 'ctx', [(i, i ^ bits) for i in range(4)])  59.4 us
    ppermute x26, starting transfers between devices, crossed(): return lax.ppermute(x, 'ctx', [(i, i ^ bits) for i in range(4)])  37.8 us
    pallas_call x13, Pallas kernels, run_kernel(): pl.pallas_call(body, in_specs=[pl.BlockSpec(memory_space=pltpu.SMEM)] + [...  34 us
    ppermute x30, starting transfers between devices, swapped(): return lax.ppermute(x, 'exp', [(i, i ^ bits) for i in range(4)])  17.2 us
    ppermute x30, waiting for transfers between devices, swapped(): return lax.ppermute(x, 'exp', [(i, i ^ bits) for i in range(4)])  17 us
    unnamed x42, local copies, waits for them, and re-layouts  7.1 us
    dot_general x3, matrix products, tn(): lax.dot_general(a, b, (((0,), (0,)), ((), ())), preferred_element_type=F32)  7.06 us
  transfers between devices with their start and end apart: 57, of which 24 were waited for; matrix products, arithmetic and copies ran while one was open for 5% of the time, Pallas kernels for 10%

profile of v4, /device:TPU:0, one launch (start us, length us, event | category | flops | bytes accessed | tf_op | source)
XLA Modules:
  0.0 185.8 jit_solution(18174190710269202433)
XLA Ops:
  3.8 4.1 %collective-permute-start.1 = (bf16[128,1280]{1,0:T(8,128)(2,1)S(1)}, bf16[128,1280]{1,0:T(8,128)(2,1)S(1)}, u32[]{:S(2)}, u32[]{:S(2)}) collective-permute-start(bf16[128,1280]{1,0:T(8,128)(2,1)S(1)} %pack_heads.1.refs_0_), channel_id=1, source_target_pairs={{0,8},{4,12},{8,0},{12,4},{1,9},{5,13},{9,1},{13,5},{2,10},{6,14},... | collective-permute-start | bytes 983048 | tf_op jit(solution)/shard_map/gather_heads/ppermute | solution.py:272
  13.5 9.2 %collective-permute-done.1.refs_2_ = bf16[128,1280]{1,0:T(8,128)(2,1)S(1)} collective-permute-done((bf16[128,1280]{1,0:T(8,128)(2,1)S(1)}, bf16[128,1280]{1,0:T(8,128)(2,1)S(1)}, u32[]{:S(2)}, u32[]{:S(2)}) %collective-permute-start.1) | collective-permute-done | bytes 327712 | tf_op jit(solution)/shard_map/gather_heads/ppermute | solution.py:272
  23.3 2.8 %collective-permute-start.3 = (bf16[32,512]{1,0:T(8,128)(2,1)S(1)}, bf16[32,512]{1,0:T(8,128)(2,1)S(1)}, u32[]{:S(2)}, u32[]{:S(2)}) collective-permute-start(bf16[32,512]{1,0:T(8,128)(2,1)S(1)} %get-tuple-element.90), channel_id=1, source_target_pairs={{0,12},{4,8},{8,4},{12,0},{1,13},{5,9},{9,5},{13,1},{2,14},{6,10},... | collective-permute-start | bytes 98312 | tf_op jit(solution)/shard_map/gather_rows/ppermute | solution.py:272
  26.1 8.6 %collective-permute-done.3.third_ref = bf16[32,512]{1,0:T(8,128)(2,1)S(1)} collective-permute-done((bf16[32,512]{1,0:T(8,128)(2,1)S(1)}, bf16[32,512]{1,0:T(8,128)(2,1)S(1)}, u32[]{:S(2)}, u32[]{:S(2)}) %collective-permute-start.3) | collective-permute-done | bytes 32800 | tf_op jit(solution)/shard_map/gather_rows/ppermute | solution.py:272
  36.0 8.1 %attend.1 = (bf16[512,1024]{1,0:T(8,128)(2,1)S(1)}, bf16[128,1024]{1,0:T(8,128)(2,1)S(1)}, bf16[2,4,32,512]{3,2,1,0:T(8,128)(2,1)S(1)}, bf16[2,4,32,512]{3,2,1,0:T(8,128)(2,1)S(1)}, bf16[512,256]{1,0:T(8,128)(2,1)S(1)}) custom-call(s32[3]{0:T(128)S(1)} %pad_add_fusion.place_ref, bf16[128,1280]{1,0:T(8,128)(2,1)S(1)} %pack_heads.1.refs_0_, ...), custom_call_target="tpu_custom_call" | custom-call | flops 1073741824 | bytes 4456448 | tf_op jit(solution)/shard_map/attend/pallas_call | solution.py:299
  48.2 6.6 %collective-permute-done.7.far_ref = bf16[32,2688]{1,0:T(8,128)(2,1)S(1)} collective-permute-done((bf16[32,2688]{1,0:T(8,128)(2,1)S(1)}, bf16[32,2688]{1,0:T(8,128)(2,1)S(1)}, u32[]{:S(2)}, u32[]{:S(2)}) %collective-permute-start.7) | collective-permute-done | bytes 172064 | tf_op jit(solution)/shard_map/gather_rows/ppermute | solution.py:272
  56.7 5.2 %collective-permute-done.15.refs_1_ = bf16[32,2176]{1,0:T(8,128)(2,1)} collective-permute-done((bf16[32,2176]{1,0:T(8,128)(2,1)S(1)}, bf16[32,2176]{1,0:T(8,128)(2,1)}, u32[]{:S(2)}, u32[]{:S(2)}) %collective-permute-start.15) | collective-permute-done | bytes 139296 | tf_op jit(solution)/shard_map/gather_rows/ppermute | solution.py:272
  66.3 4.1 %collective-permute-done.8.refs_1_ = bf16[4,32,512]{2,1,0:T(8,128)(2,1)} collective-permute-done((bf16[4,32,512]{2,1,0:T(8,128)(2,1)}, bf16[4,32,512]{2,1,0:T(8,128)(2,1)}, u32[]{:S(2)}, u32[]{:S(2)}) %collective-permute-start.8) | collective-permute-done | bytes 131104 | tf_op jit(solution)/shard_map/gather_hidden/ppermute | solution.py:272
  74.1 3.0 %collective-permute-done.10.refs_3_ = bf16[4,32,512]{2,1,0:T(8,128)(2,1)} collective-permute-done((bf16[4,32,512]{2,1,0:T(8,128)(2,1)}, bf16[4,32,512]{2,1,0:T(8,128)(2,1)}, u32[]{:S(2)}, u32[]{:S(2)}) %collective-permute-start.10) | collective-permute-done | bytes 131104 | tf_op jit(solution)/shard_map/gather_hidden/ppermute | solution.py:272
  77.3 2.4 %collective-permute-start.13 = (bf16[4,32,512]{2,1,0:T(8,128)(2,1)}, bf16[4,32,512]{2,1,0:T(8,128)(2,1)S(1)}, u32[]{:S(2)}, u32[]{:S(2)}) collective-permute-start(bf16[4,32,512]{2,1,0:T(8,128)(2,1)} %collective-permute-done.9.refs_2_), channel_id=1, source_target_pairs={{0,2},{1,3},{2,0},{3,1},{4,6},{5,7},{6,4},{7,5},{8,10},{9,11},{10,... | collective-permute-start | bytes 393224 | tf_op jit(solution)/shard_map/gather_hidden/ppermute | solution.py:276
  79.8 3.1 %collective-permute-done.13.refs_6_ = bf16[4,32,512]{2,1,0:T(8,128)(2,1)S(1)} collective-permute-done((bf16[4,32,512]{2,1,0:T(8,128)(2,1)}, bf16[4,32,512]{2,1,0:T(8,128)(2,1)S(1)}, u32[]{:S(2)}, u32[]{:S(2)}) %collective-permute-start.13) | collective-permute-done | bytes 131104 | tf_op jit(solution)/shard_map/gather_hidden/ppermute | solution.py:276
  87.1 2.4 %grad_rows.1 = (bf16[512,2048]{1,0:T(8,128)(2,1)S(1)}, f32[512,1]{1,0:T(8,128)S(1)}, f32[512,384]{1,0:T(8,128)S(1)}) custom-call(s32[3]{0:T(128)S(1)} %pad_add_fusion.place_ref, bf16[3,32,2176]{2,1,0:T(8,128)(2,1)S(1)} %pad_maximum_fusion.refs_0_, bf16[32,2176]{1,0:T(8,128)(2,1)} %collective-permute-done.15.refs_1_, ...), custom_call_target="tpu_custom_call" | custom-call | flops 805306368 | bytes 6686720 | tf_op jit(solution)/shard_map/grad_rows/pallas_call | solution.py:299
  93.9 6.7 %expert_rows.1 = (bf16[512,2048]{1,0:T(8,128)(2,1)S(1)}, bf16[512,384]{1,0:T(8,128)(2,1)S(1)}, bf16[512,384]{1,0:T(8,128)(2,1)S(1)}, bf16[512,384]{1,0:T(8,128)(...) custom-call(s32[3]{0:T(128)S(1)} %pad_add_fusion.place_ref, ...), custom_call_target="tpu_custom_call" | custom-call | flops 3221225472 | bytes 11542528 | tf_op jit(solution)/shard_map/expert_rows/pallas_call | solution.py:299
  103.6 2.8 %collective-permute-done.35.refs_6_ = bf16[512,512]{1,0:T(8,128)(2,1)S(1)} collective-permute-done((bf16[512,512]{1,0:T(8,128)(2,1)S(1)}, bf16[512,512]{1,0:T(8,128)(2,1)S(1)}, u32[]{:S(2)}, u32[]{:S(2)}) %collective-permute-start.35) | collective-permute-done | bytes 524320 | tf_op jit(solution)/shard_map/gather_proj/ppermute | solution.py:840
  114.4 2.8 %collective-permute-done.38 = bf16[2,32,512]{2,1,0:T(8,128)(2,1)S(1)} collective-permute-done((bf16[2,32,512]{2,1,0:T(8,128)(2,1)S(1)}, bf16[2,32,512]{2,1,0:T(8,128)(2,1)S(1)}, u32[]{:S(2)}, u32[]{:S(2)}) %collective-permute-start.38) | collective-permute-done | bytes 65568 | tf_op jit(solution)/shard_map/sum_row_grads/ppermute | solution.py:272
  125.4 5.0 %collective-permute-done.40 = bf16[4,32,2048]{2,1,0:T(8,128)(2,1)S(1)} collective-permute-done((bf16[4,32,2048]{2,1,0:T(8,128)(2,1)S(1)}, bf16[4,32,2048]{2,1,0:T(8,128)(2,1)S(1)}, u32[]{:S(2)}, u32[]{:S(2)}) %collective-permute-start.40) | collective-permute-done | bytes 524320 | tf_op jit(solution)/shard_map/sum_outputs/ppermute | solution.py:276
  132.2 2.4 %collective-permute-start.45 = (bf16[48,1024]{1,0:T(8,128)(2,1)S(1)}, bf16[48,1024]{1,0:T(8,128)(2,1)S(1)}, u32[]{:S(2)}, u32[]{:S(2)}) collective-permute-start(bf16[48,1024]{1,0:T(8,128)(2,1)S(1)} %get-tuple-element.131), channel_id=1, source_target_pairs={{0,8},{4,12},{8,0},{12,4},{1,9},{5,13},{9,1},{13,5},{2,10},{6,14},... | collective-permute-start | bytes 294920 | tf_op jit(solution)/shard_map/gather_cuts/ppermute | solution.py:272
  134.6 3.1 %collective-permute-done.45 = bf16[48,1024]{1,0:T(8,128)(2,1)S(1)} collective-permute-done((bf16[48,1024]{1,0:T(8,128)(2,1)S(1)}, bf16[48,1024]{1,0:T(8,128)(2,1)S(1)}, u32[]{:S(2)}, u32[]{:S(2)}) %collective-permute-start.45) | collective-permute-done | bytes 98336 | tf_op jit(solution)/shard_map/gather_cuts/ppermute | solution.py:272
  138.8 4.7 %collective-permute-done.50.refs_2_ = bf16[2,48,1024]{2,1,0:T(8,128)(2,1)S(1)} collective-permute-done((bf16[2,48,1024]{2,1,0:T(8,128)(2,1)S(1)}, bf16[2,48,1024]{2,1,0:T(8,128)(2,1)S(1)}, u32[]{:S(2)}, u32[]{:S(2)}) %collective-permute-start.50) | collective-permute-done | bytes 196640 | tf_op jit(solution)/shard_map/gather_cuts/ppermute | solution.py:276
  152.4 2.5 %convolution_convert_fusion.1 = bf16[2048,384]{1,0:T(8,128)(2,1)} fusion(bf16[512,2048]{1,0:T(8,128)(2,1)S(1)} %get-tuple-element.138, bf16[512,384]{1,0:T(8,128)(2,1)S(1)} %get-tuple-element.140), kind=kOutput, calls=%fused_computation.1 | convolution fusion | flops 806092800 | bytes 4063232 | tf_op jit(solution)/shard_map/dot_general | solution.py:288
  154.8 2.5 %convolution_convert_fusion.2 = bf16[2048,384]{1,0:T(8,128)(2,1)} fusion(bf16[512,2048]{1,0:T(8,128)(2,1)S(1)} %get-tuple-element.138, bf16[512,384]{1,0:T(8,128)(2,1)S(1)} %get-tuple-element.139), kind=kOutput, calls=%fused_computation.2 | convolution fusion | flops 806092800 | bytes 4063232 | tf_op jit(solution)/shard_map/dot_general | solution.py:288
  157.3 2.9 %collective-permute-done.47.refs_2_ = bf16[32,2048]{1,0:T(8,128)(2,1)S(1)} collective-permute-done((bf16[32,2048]{1,0:T(8,128)(2,1)S(1)}, bf16[32,2048]{1,0:T(8,128)(2,1)S(1)}, u32[]{:S(2)}, u32[]{:S(2)}) %collective-permute-start.47) | collective-permute-done | bytes 131104 | tf_op jit(solution)/shard_map/sum_outputs/ppermute | solution.py:272
  160.2 6.6 %collective-permute-done.53.near_ref = bf16[272,512]{1,0:T(8,128)(2,1)S(1)} collective-permute-done((bf16[272,512]{1,0:T(8,128)(2,1)S(1)}, bf16[272,512]{1,0:T(8,128)(2,1)S(1)}, u32[]{:S(2)}, u32[]{:S(2)}) %collective-permute-start.53) | collective-permute-done | bytes 278560 | tf_op jit(solution)/shard_map/gather_cuts/ppermute | solution.py:272
  171.0 4.8 %attend_backward.1 = (bf16[128,1024]{1,0:T(8,128)(2,1)}, bf16[144,256]{1,0:T(8,128)(2,1)S(1)}, bf16[144,256]{1,0:T(8,128)(2,1)S(1)}, bf16[144,256]{1,0:T(8,128)(2,1)S(1)}, bf16[144,256]{1,0:T(8,128)(2,1)S(1)}) custom-call(s32[3]{0:T(128)S(1)} %pad_add_fusion.place_ref, bf16[128,1024]{1,0:T(8,128)(2,1)S(1)} %get-tuple-element.141.refs_0_, ...), custom_call_target="tpu_custom_call" | custom-call | flops 671088640 | bytes 1875968 | tf_op jit(solution)/shard_map/attend_backward/pallas_call | solution.py:299
  (162 shorter events, 78.6 us)
Async XLA Ops:
  3.8 18.9 %collective-permute-start.1 = (bf16[128,1280]{1,0:T(8,128)(2,1)S(1)}, bf16[128,1280]{1,0:T(8,128)(2,1)S(1)}, u32[]{:S(2)}, u32[]{:S(2)}) collective-permute-start(bf16[128,1280]{1,0:T(8,128)(2,1)S(1)} %pack_heads.1.refs_0_), channel_id=1, source_target_pairs={{0,8},{4,12},{8,0},{12,4},{1,9},{5,13},{9,1},{13,5},{2,10},{6,14},... | collective-permute-start | bytes 983048 | tf_op jit(solution)/shard_map/gather_heads/ppermute | solution.py:272
  7.9 15.5 %collective-permute-start = (bf16[128,1280]{1,0:T(8,128)(2,1)S(1)}, bf16[128,1280]{1,0:T(8,128)(2,1)S(1)}, u32[]{:S(2)}, u32[]{:S(2)}) collective-permute-start(bf16[128,1280]{1,0:T(8,128)(2,1)S(1)} %pack_heads.1.refs_0_), channel_id=1, source_target_pairs={{0,4},{4,0},{8,12},{12,8},{1,5},{5,1},{9,13},{13,9},{2,6},{6,2},{1... | collective-permute-start | bytes 983048 | tf_op jit(solution)/shard_map/gather_heads/ppermute | solution.py:272
  22.7 12.0 %collective-permute-start.2 = (bf16[128,1280]{1,0:T(8,128)(2,1)S(1)}, bf16[128,1280]{1,0:T(8,128)(2,1)S(1)}, u32[]{:S(2)}, u32[]{:S(2)}) collective-permute-start(bf16[128,1280]{1,0:T(8,128)(2,1)S(1)} %collective-permute-done.1.refs_2_), channel_id=1, source_target_pairs={{0,4},{4,0},{8,12},{12,8},{1,5},{5,1},{9,13},{13,9},{2,6},{6,2},{1... | collective-permute-start | bytes 983048 | tf_op jit(solution)/shard_map/gather_heads/ppermute | solution.py:272
  23.3 11.4 %collective-permute-start.3 = (bf16[32,512]{1,0:T(8,128)(2,1)S(1)}, bf16[32,512]{1,0:T(8,128)(2,1)S(1)}, u32[]{:S(2)}, u32[]{:S(2)}) collective-permute-start(bf16[32,512]{1,0:T(8,128)(2,1)S(1)} %get-tuple-element.90), channel_id=1, source_target_pairs={{0,12},{4,8},{8,4},{12,0},{1,13},{5,9},{9,5},{13,1},{2,14},{6,10},... | collective-permute-start | bytes 98312 | tf_op jit(solution)/shard_map/gather_rows/ppermute | solution.py:272
  44.2 10.6 %collective-permute-start.7 = (bf16[32,2688]{1,0:T(8,128)(2,1)S(1)}, bf16[32,2688]{1,0:T(8,128)(2,1)S(1)}, u32[]{:S(2)}, u32[]{:S(2)}) collective-permute-start(bf16[32,2688]{1,0:T(8,128)(2,1)S(1)} %get-tuple-element.100), channel_id=1, source_target_pairs={{0,8},{4,12},{8,0},{12,4},{1,9},{5,13},{9,1},{13,5},{2,10},{6,14},... | collective-permute-start | bytes 516104 | tf_op jit(solution)/shard_map/gather_rows/ppermute | solution.py:272
  44.5 10.5 %collective-permute-start.6 = (bf16[32,2688]{1,0:T(8,128)(2,1)S(1)}, bf16[32,2688]{1,0:T(8,128)(2,1)S(1)}, u32[]{:S(2)}, u32[]{:S(2)}) collective-permute-start(bf16[32,2688]{1,0:T(8,128)(2,1)S(1)} %get-tuple-element.94), channel_id=1, source_target_pairs={{0,4},{4,0},{8,12},{12,8},{1,5},{5,1},{9,13},{13,9},{2,6},{6,2},{1... | collective-permute-start | bytes 516104 | tf_op jit(solution)/shard_map/gather_rows/ppermute | solution.py:272
  55.1 18.4 %collective-permute-start.16 = (bf16[3,32,2176]{2,1,0:T(8,128)(2,1)S(1)}, bf16[3,32,2176]{2,1,0:T(8,128)(2,1)S(1)}, u32[]{:S(2)}, u32[]{:S(2)}) collective-permute-start(bf16[3,32,2176]{2,1,0:T(8,128)(2,1)S(1)} %pad_maximum_fusion.refs_0_), channel_id=1, source_target_pairs={{0,2},{1,3},{2,0},{3,1},{4,6},{5,7},{6,4},{7,5},{8,10},{9,11},{10,... | collective-permute-start | bytes 1253384 | tf_op jit(solution)/shard_map/gather_rows/ppermute | solution.py:276
  61.9 11.6 %collective-permute-start.17 = (bf16[32,2176]{1,0:T(8,128)(2,1)}, bf16[32,2176]{1,0:T(8,128)(2,1)}, u32[]{:S(2)}, u32[]{:S(2)}) collective-permute-start(bf16[32,2176]{1,0:T(8,128)(2,1)} %collective-permute-done.15.refs_1_), channel_id=1, source_target_pairs={{0,2},{1,3},{2,0},{3,1},{4,6},{5,7},{6,4},{7,5},{8,10},{9,11},{10,... | collective-permute-start | bytes 417800 | tf_op jit(solution)/shard_map/gather_rows/ppermute | solution.py:276
  73.5 13.1 %collective-permute-start.18 = (bf16[3,32,2176]{2,1,0:T(8,128)(2,1)S(1)}, bf16[3,32,2176]{2,1,0:T(8,128)(2,1)S(1)}, u32[]{:S(2)}, u32[]{:S(2)}) collective-permute-start(bf16[3,32,2176]{2,1,0:T(8,128)(2,1)S(1)} %pad_maximum_fusion.refs_0_), channel_id=1, source_target_pairs={{0,1},{1,0},{2,3},{3,2},{4,5},{5,4},{6,7},{7,6},{8,9},{9,8},{10,11... | collective-permute-start | bytes 1253384 | tf_op jit(solution)/shard_map/gather_rows/ppermute | solution.py:276
  73.5 13.5 %collective-permute-start.20 = (bf16[3,32,2176]{2,1,0:T(8,128)(2,1)S(1)}, bf16[3,32,2176]{2,1,0:T(8,128)(2,1)S(1)}, u32[]{:S(2)}, u32[]{:S(2)}) collective-permute-start(bf16[3,32,2176]{2,1,0:T(8,128)(2,1)S(1)} %collective-permute-done.16.refs_2_), channel_id=1, source_target_pairs={{0,1},{1,0},{2,3},{3,2},{4,5},{5,4},{6,7},{7,6},{8,9},{9,8},{10,11... | collective-permute-start | bytes 1253384 | tf_op jit(solution)/shard_map/gather_rows/ppermute | solution.py:276
  77.1 13.9 %collective-permute-start.22 = (bf16[512,512]{1,0:T(8,128)(2,1)S(1)}, bf16[512,512]{1,0:T(8,128)(2,1)S(1)}, u32[]{:S(2)}, u32[]{:S(2)}) collective-permute-start(bf16[512,512]{1,0:T(8,128)(2,1)S(1)} %constant_dynamic-slice_fusion), channel_id=1, source_target_pairs={{0,4},{4,0},{8,12},{12,8},{1,5},{5,1},{9,13},{13,9},{2,6},{6,2},{1... | collective-permute-start | bytes 1572872 | tf_op jit(solution)/shard_map/gather_proj/ppermute | solution.py:272
  92.3 14.0 %collective-permute-start.35 = (bf16[512,512]{1,0:T(8,128)(2,1)S(1)}, bf16[512,512]{1,0:T(8,128)(2,1)S(1)}, u32[]{:S(2)}, u32[]{:S(2)}) collective-permute-start(bf16[512,512]{1,0:T(8,128)(2,1)S(1)} %collective-permute-done.22.refs_5_), channel_id=1, source_target_pairs={{0,16},{16,0},{1,17},{17,1},{2,18},{18,2},{3,19},{19,3},{4,20},{20... | collective-permute-start | bytes 1572872 | tf_op jit(solution)/shard_map/gather_proj/ppermute | solution.py:840
  101.2 17.3 %collective-permute-start.32 = (bf16[4,32,1536]{2,1,0:T(8,128)(2,1)S(1)}, bf16[4,32,1536]{2,1,0:T(8,128)(2,1)S(1)}, u32[]{:S(2)}, u32[]{:S(2)}) collective-permute-start(bf16[4,32,1536]{2,1,0:T(8,128)(2,1)S(1)} %get-tuple-element.116), channel_id=1, source_target_pairs={{0,1},{1,0},{2,3},{3,2},{4,5},{5,4},{6,7},{7,6},{8,9},{9,8},{10,11... | collective-permute-start | bytes 1179656 | tf_op jit(solution)/shard_map/sum_row_grads/ppermute | solution.py:276
  103.1 15.6 %collective-permute-start.31 = (bf16[2,4,32,2048]{3,2,1,0:T(8,128)(2,1)S(1)}, bf16[2,4,32,2048]{3,2,1,0:T(8,128)(2,1)S(1)}, u32[]{:S(2)}, u32[]{:S(2)}) collective-permute-start(bf16[2,4,32,2048]{3,2,1,0:T(8,128)(2,1)S(1)} %get-tuple-element.114), channel_id=1, source_target_pairs={{0,1},{1,0},{2,3},{3,2},{4,5},{5,4},{6,7},{7,6},{8,9},{9,8},{10,11... | collective-permute-start | bytes 3145736 | tf_op jit(solution)/shard_map/sum_outputs/ppermute | solution.py:276
  106.5 12.1 %collective-permute-start.36 = (bf16[4,32,1536]{2,1,0:T(8,128)(2,1)S(1)}, bf16[4,32,1536]{2,1,0:T(8,128)(2,1)S(1)}, u32[]{:S(2)}, u32[]{:S(2)}) collective-permute-start(bf16[4,32,1536]{2,1,0:T(8,128)(2,1)S(1)} %add_convert_fusion.1), channel_id=1, source_target_pairs={{0,2},{1,3},{2,0},{3,1},{4,6},{5,7},{6,4},{7,5},{8,10},{9,11},{10,... | collective-permute-start | bytes 1179656 | tf_op jit(solution)/shard_map/sum_row_grads/ppermute | solution.py:276
  118.9 11.5 %collective-permute-start.40 = (bf16[4,32,2048]{2,1,0:T(8,128)(2,1)S(1)}, bf16[4,32,2048]{2,1,0:T(8,128)(2,1)S(1)}, u32[]{:S(2)}, u32[]{:S(2)}) collective-permute-start(bf16[4,32,2048]{2,1,0:T(8,128)(2,1)S(1)} %fusion.1), channel_id=1, source_target_pairs={{0,2},{1,3},{2,0},{3,1},{4,6},{5,7},{6,4},{7,5},{8,10},{9,11},{10,... | collective-permute-start | bytes 1572872 | tf_op jit(solution)/shard_map/sum_outputs/ppermute | solution.py:276
  119.6 11.2 %collective-permute-start.43 = (bf16[32,1536]{1,0:T(8,128)(2,1)S(1)}, bf16[32,1536]{1,0:T(8,128)(2,1)S(1)}, u32[]{:S(2)}, u32[]{:S(2)}) collective-permute-start(bf16[32,1536]{1,0:T(8,128)(2,1)S(1)} %get-tuple-element.127), channel_id=1, source_target_pairs={{0,12},{4,8},{8,4},{12,0},{1,13},{5,9},{9,5},{13,1},{2,14},{6,10},... | collective-permute-start | bytes 294920 | tf_op jit(solution)/shard_map/sum_row_grads/ppermute | solution.py:272
  121.6 9.1 %collective-permute-start.42 = (bf16[32,1536]{1,0:T(8,128)(2,1)S(1)}, bf16[32,1536]{1,0:T(8,128)(2,1)S(1)}, u32[]{:S(2)}, u32[]{:S(2)}) collective-permute-start(bf16[32,1536]{1,0:T(8,128)(2,1)S(1)} %get-tuple-element.126), channel_id=1, source_target_pairs={{0,8},{4,12},{8,0},{12,4},{1,9},{5,13},{9,1},{13,5},{2,10},{6,14},... | collective-permute-start | bytes 294920 | tf_op jit(solution)/shard_map/sum_row_grads/ppermute | solution.py:272
  138.8 9.4 %collective-permute-start.49 = (bf16[2,48,1024]{2,1,0:T(8,128)(2,1)S(1)}, bf16[2,48,1024]{2,1,0:T(8,128)(2,1)S(1)}, u32[]{:S(2)}, u32[]{:S(2)}) collective-permute-start(bf16[2,48,1024]{2,1,0:T(8,128)(2,1)S(1)} %pad_maximum_fusion.1.refs_0_), channel_id=1, source_target_pairs={{0,1},{1,0},{2,3},{3,2},{4,5},{5,4},{6,7},{7,6},{8,9},{9,8},{10,11... | collective-permute-start | bytes 589832 | tf_op jit(solution)/shard_map/gather_cuts/ppermute | solution.py:276
  143.8 13.5 %collective-permute-start.48 = (bf16[32,2048]{1,0:T(8,128)(2,1)S(1)}, bf16[32,2048]{1,0:T(8,128)(2,1)S(1)}, u32[]{:S(2)}, u32[]{:S(2)}) collective-permute-start(bf16[32,2048]{1,0:T(8,128)(2,1)S(1)} %get-tuple-element.135), channel_id=1, source_target_pairs={{0,12},{4,8},{8,4},{12,0},{1,13},{5,9},{9,5},{13,1},{2,14},{6,10},... | collective-permute-start | bytes 393224 | tf_op jit(solution)/shard_map/sum_outputs/ppermute | solution.py:272
  146.0 14.1 %collective-permute-start.47 = (bf16[32,2048]{1,0:T(8,128)(2,1)S(1)}, bf16[32,2048]{1,0:T(8,128)(2,1)S(1)}, u32[]{:S(2)}, u32[]{:S(2)}) collective-permute-start(bf16[32,2048]{1,0:T(8,128)(2,1)S(1)} %get-tuple-element.134), channel_id=1, source_target_pairs={{0,8},{4,12},{8,0},{12,4},{1,9},{5,13},{9,1},{13,5},{2,10},{6,14},... | collective-permute-start | bytes 393224 | tf_op jit(solution)/shard_map/sum_outputs/ppermute | solution.py:272
  147.4 12.7 %collective-permute-start.46 = (bf16[32,2048]{1,0:T(8,128)(2,1)S(1)}, bf16[32,2048]{1,0:T(8,128)(2,1)S(1)}, u32[]{:S(2)}, u32[]{:S(2)}) collective-permute-start(bf16[32,2048]{1,0:T(8,128)(2,1)S(1)} %get-tuple-element.133), channel_id=1, source_target_pairs={{0,4},{4,0},{8,12},{12,8},{1,5},{5,1},{9,13},{13,9},{2,6},{6,2},{1... | collective-permute-start | bytes 393224 | tf_op jit(solution)/shard_map/sum_outputs/ppermute | solution.py:272
  149.5 17.2 %collective-permute-start.53 = (bf16[272,512]{1,0:T(8,128)(2,1)S(1)}, bf16[272,512]{1,0:T(8,128)(2,1)S(1)}, u32[]{:S(2)}, u32[]{:S(2)}) collective-permute-start(bf16[272,512]{1,0:T(8,128)(2,1)S(1)} %get-tuple-element.147), channel_id=1, source_target_pairs={{0,4},{4,0},{8,12},{12,8},{1,5},{5,1},{9,13},{13,9},{2,6},{6,2},{1... | collective-permute-start | bytes 835592 | tf_op jit(solution)/shard_map/gather_cuts/ppermute | solution.py:272
  150.8 20.2 %collective-permute-start.52 = (bf16[128,1024]{1,0:T(8,128)(2,1)S(1)}, bf16[128,1024]{1,0:T(8,128)(2,1)S(1)}, u32[]{:S(2)}, u32[]{:S(2)}) collective-permute-start(bf16[128,1024]{1,0:T(8,128)(2,1)S(1)} %get-tuple-element.142), channel_id=1, source_target_pairs={{0,8},{4,12},{8,0},{12,4},{1,9},{5,13},{9,1},{13,5},{2,10},{6,14},... | collective-permute-start | bytes 786440 | tf_op jit(solution)/shard_map/sum_mix_grad/ppermute | solution.py:272
  (53 other events, 463.9 us)

commit v5 on v4

--- a/solution.py
+++ b/solution.py
@@ -385,16 +385,21 @@
         )
         for b in range(n):
             lo, hi = b * rows, (b + 1) * rows
-            for head in range(heads):
-                at = slice(head * HEAD_SIZE, (head + 1) * HEAD_SIZE)
-                query = everything[lo:hi, (head + 2) * HEAD_SIZE : (head + 3) * HEAD_SIZE]
-                scores = nt(query, keys[:hi, :])
-                last = jnp.where(below, scores[:, lo:], NEG)
+            for first in range(0, heads, 8):
+                queries = [
+                    everything[lo:hi, (first + i + 2) * HEAD_SIZE : (first + i + 3) * HEAD_SIZE]
+                    for i in range(8)
+                ]
+                scores = nt(jnp.concatenate(queries, 0), keys[:hi, :])
+                last = jnp.where(jnp.concatenate([below] * 8, 0), scores[:, lo:], NEG)
                 scores = jnp.concatenate([scores[:, :lo], last], 1) if b else last
                 peak = jnp.max(scores, -1, keepdims=True)
                 weights = jnp.exp2((scores - peak) * factor)
                 total = jnp.sum(weights, -1, keepdims=True)
-                mix_ref[lo:hi, at] = (nn(weights.astype(BF16), values[:hi, :]) / total).astype(BF16)
+                mixed = nn(weights.astype(BF16), values[:hi, :]) * (1.0 / total)
+                for i in range(8):
+                    at = slice((first + i) * HEAD_SIZE, (first + i + 1) * HEAD_SIZE)
+                    mix_ref[lo:hi, at] = mixed[i * rows : (i + 1) * rows].astype(BF16)
             ps[...] = nn(mix_ref[lo:hi, :], proj_ref[...]).astype(BF16)
             for turn in range(2):
                 same, other = e ^ (2 * turn), e ^ (2 * turn + 1)
@@ -623,20 +628,21 @@
     rows, width = 4 * tok, out_proj.shape[0]
 
     def body(place_ref, *refs):
-        proj_ref, here_ref, there_ref, own_ref, far_ref, keep_ref, send_ref, grads, acc = refs[4:]
+        proj_ref, here_ref, there_ref, own_ref, far_ref, keep_ref, send_ref, gain_ref, grads, acc = refs[4:]
         e, g = place_ref[1], place_ref[2]
         gain = sum([refs[r][i, tok : tok + 2, :].astype(F32) for r in range(4) for i in range(count)])
         gain = jnp.sum(gain, 0, keepdims=True)
         high = gain.astype(BF16)
-        spare = jnp.zeros((14, 2 * cols), BF16)
-        gain = jnp.concatenate([high, (gain - high.astype(F32)).astype(BF16), spare], 0)
+        low = (gain - high.astype(F32)).astype(BF16)
+        half = cols // 2
+        pieces = [x[:, i * half : (i + 1) * half] for x in (high, low) for i in range(4)]
+        gain_ref[...] = jnp.concatenate([*pieces, jnp.zeros((8, half), BF16)], 0)
         for i in range(count):
             for r in range(4):
                 at = pl.multiple_of(i * rows + (e ^ r) * tok, tok)
                 grads[pl.ds(at, tok), :] = refs[r][i, :tok, :]
         for ref, at in ((keep_ref, slice(0, cols)), (send_ref, slice(cols, 2 * cols))):
-            ref[: count * rows, :] = grads[:, at]
-            ref[count * rows :, :] = gain[:, at]
+            ref[...] = grads[:, at]
         half = width // 2
         for ref, index in ((here_ref, g), (there_ref, 1 - g)):
             at = pl.ds(pl.multiple_of(index * half, half), half)
@@ -652,7 +658,7 @@
         "mix_grad_parts",
         place,
         [*cut_sets, out_proj, proj_here, proj_there],
-        [((rows, width), BF16)] * 2 + [((count * rows + 16, cols), BF16)] * 2,
+        [((rows, width), BF16)] * 2 + [((count * rows, cols), BF16)] * 2 + [((16, cols // 2), BF16)],
         [((count * rows, 2 * cols), BF16), ((count * rows, width), F32)],
         flops=4 * count * rows * cols * width,
     )
@@ -676,17 +682,26 @@
             at = slice(head * HEAD_SIZE, (head + 1) * HEAD_SIZE)
             rs = slice(head * rows, (head + 1) * rows)
             grad = sum([x[:, at].astype(F32) for x in g_refs[1:]], g_refs[0][:, at].astype(F32))
-            grad = grad.astype(BF16)
             qs[rs, :] = query_ref[:, at]
-            ms[rs, :] = grad
-            scores = jnp.where(visible, nt(query_ref[:, at], ks[...]), NEG)
+            ms[rs, :] = grad.astype(BF16)
+        for first in range(0, heads, 2):
+            rs = slice(first * rows, (first + 2) * rows)
+            scores = nt(qs[rs, :], ks[...]).reshape(2, rows, n * rows)
+            scores = jnp.where(visible[None], scores, NEG).reshape(2 * rows, n * rows)
             peak = jnp.max(scores, -1, keepdims=True)
             weights = jnp.exp2((scores - peak) * (scale * LOG2E))
             prob = weights * (1.0 / jnp.sum(weights, -1, keepdims=True))
-            delta = jnp.sum(grad.astype(F32) * mix_ref[:, at].astype(F32), -1, keepdims=True)
-            score_half[rs, :] = (prob * (nt(grad, vs[...]) - delta)).astype(BF16)
+            mixes = [
+                mix_ref[:, (first + i) * HEAD_SIZE : (first + i + 1) * HEAD_SIZE] for i in range(2)
+            ]
+            mixes = jnp.concatenate(mixes, 0).astype(F32)
+            delta = jnp.sum(ms[rs, :].astype(F32) * mixes, -1, keepdims=True)
+            score_half[rs, :] = (prob * (nt(ms[rs, :], vs[...]) - delta)).astype(BF16)
             prob_half[rs, :] = prob.astype(BF16)
-            dq_ref[:, at] = (nn(score_half[rs, :], ks[...]) * scale).astype(BF16)
+        query_grad = nn(score_half[...], ks[...]) * scale
+        for head in range(heads):
+            at = slice(head * HEAD_SIZE, (head + 1) * HEAD_SIZE)
+            dq_ref[:, at] = query_grad[head * rows : (head + 1) * rows].astype(BF16)
         key_sum = (tn(score_half[...], qs[...]) * scale).astype(BF16)
         value_sum = tn(prob_half[...], ms[...]).astype(BF16)
         for j in range(n):
@@ -712,29 +727,23 @@
     total, width = mix_all.shape
     rows, cols = total // 4, keep.shape[1]
 
-    def body(place_ref, mix_ref, keep_ref, near_ref, out_ref, gain_ref, grads):
+    def body(place_ref, mix_ref, keep_ref, near_ref, out_ref, grads):
         c = place_ref[0]
         for d in range(4):
             ref = near_ref if d % 2 else keep_ref
             at = pl.multiple_of((c ^ d) * rows, rows)
             grads[pl.ds(at, rows), :] = ref[d // 2 * rows : (d // 2 + 1) * rows, :]
         out_ref[...] = tn(mix_ref[...], grads[...]).astype(BF16)
-        gain = keep_ref[2 * rows :, :].astype(F32) + near_ref[2 * rows :, :].astype(F32)
-        gain = jnp.sum(gain[:2], 0, keepdims=True)
-        high = gain.astype(BF16)
-        low = (gain - high.astype(F32)).astype(BF16)
-        pieces = [x[:, i : i + cols // 2] for x in (high, low) for i in (0, cols // 2)]
-        gain_ref[...] = jnp.concatenate([*pieces, jnp.zeros((12, cols // 2), BF16)], 0)
 
     return run_kernel(
         body,
         "proj_grad",
         place,
         [mix_all, keep, near],
-        [((width, cols), BF16), ((16, cols // 2), BF16)],
+        [((width, cols), BF16)],
         [((total, cols), BF16)],
         flops=2 * total * cols * width,
-    )
+    )[0]
 
 
 def pair_sums(place, parts):
@@ -748,11 +757,12 @@
         total = sum([r[:rows, :].astype(F32) for r in refs[1:n]], refs[0][:rows, :].astype(F32))
         key_ref[...] = total[:, :HEAD_SIZE].astype(BF16)
         value_ref[...] = total[:, HEAD_SIZE:].astype(BF16)
+        gain_ref[...] = jnp.zeros(gain_ref.shape, F32)
         for j in range(n):
-            tail = refs[j][rows:, :].astype(F32)
-            for i in range(2):
-                at = pl.multiple_of(((c ^ j) * 2 + i) * half, half)
-                gain_ref[:, pl.ds(at, half)] = tail[i : i + 1] + tail[i + 2 : i + 3]
+            tail = refs[j][rows : rows + 8, :].astype(F32)
+            for i in range(4):
+                at = pl.multiple_of(((c ^ j ^ (i // 2)) * 2 + i % 2) * half, half)
+                gain_ref[:, pl.ds(at, half)] += tail[i : i + 1] + tail[i + 4 : i + 5]
 
     return run_kernel(
         body,
@@ -792,11 +802,10 @@
     with scope("gather_heads"):
         heads = pack_heads(place, key, value, query)
         far, near = crossed(heads, 2), crossed(heads, 1)
-        parts = [heads, near, far, crossed(after(far, to_far, to_near, to_third), 1)]
+        row_third = crossed(to_third, 3)
+        parts = [heads, near, far, crossed(after(far, near, to_far, to_near, row_third), 1)]
 
     with scope("gather_rows"):
-        row_third = crossed(after(to_third, far, near), 3)
-        parts[3] = after(parts[3], row_third)
         to_far, to_near = lax.optimization_barrier((to_far, to_near, parts[3]))[:2]
         row_far, row_near = crossed(to_far, 2), crossed(to_near, 1)
 
@@ -809,12 +818,12 @@
     )
     with scope("gather_rows"):
         size = width + 128
-        to_far, row_far, row_near = lax.optimization_barrier((to_far, row_far, row_near, line))[:3]
-        rest = crossed(row_far[:, :size], 1)
+        rest = crossed(after(row_far[:, :size], line), 1)
+        to_far, row_far, row_near = lax.optimization_barrier((to_far, row_far, row_near, hidden_block))[:3]
         grad_own = jnp.stack([to_far[:, :size], row_near[:, :size], row_far[:, :size]])
         grad_own, grad_line = [grad_own, rest], [swapped(grad_own, 2), swapped(rest, 2)]
         grad_sets = [grad_own, grad_line] + [
-            [swapped(after(x, grad_line[1]), 1) for x in xs] for xs in (grad_own, grad_line)
+            [swapped(x, 1) for x in xs] for xs in (grad_own, grad_line)
         ]
     grad_rows, gate, act_grad = grad_rows_of(place, grad_sets, w_down[0])
 
@@ -849,15 +858,16 @@
     with scope("sum_outputs"):
         out_sent = swapped(out_send, 1)
         out_line = swapped(after(add(out_keep[1], out_sent[1]), wide[0]), 2)
+    grad_w_down = tn(after(act_rows, wide[0]), grad_rows).astype(BF16)
     grad_resid, *cuts = norm_backward(
-        place, wide, narrow, after(hidden, out_line), grad_out, norm_gain, cols
+        place, wide, narrow, after(hidden, out_line, grad_w_down), grad_out, norm_gain, cols
     )
 
     with scope("gather_cuts"):
         cut_own = jnp.stack([cuts[0], crossed(cuts[1], 2)])
         cut_line = swapped(cut_own, 2)
         cut_sets = [cut_own, swapped(cut_own, 1), cut_line, swapped(cut_line, 1)]
-    mix_own, mix_far, cut_keep, cut_send = mix_grad_parts(
+    mix_own, mix_far, cut_keep, cut_send, gain_rows = mix_grad_parts(
         place, cut_sets, out_proj, proj_here, proj_there
     )
     with scope("sum_mix_grad"):
@@ -868,12 +878,12 @@
     with scope("sum_outputs"):
         out_sums = [add(out_keep[0][j], out_sent[0][j], out_line[j]) for j in range(n)]
         out_sums = [after(x, cut_own) for x in out_sums]
-        out_sums = [out_sums[0]] + [crossed(out_sums[j], j) for j in range(1, n)]
+        second = add(out_sums[2], crossed(out_sums[3], 1))
+        out_sums = [out_sums[0], crossed(out_sums[1], 1), crossed(second, 2)]
     normed, act_rows = lax.optimization_barrier((normed, act_rows, mix_own))[:2]
     grad_w_gate = tn(normed, gate_grad).astype(BF16)
     grad_w_up = tn(normed, up_grad).astype(BF16)
-    grad_w_down = tn(act_rows, grad_rows).astype(BF16)
-    grad_out_proj, gain_rows = proj_grad(place, mix_all, cut_keep, cut_near)
+    grad_out_proj = proj_grad(place, mix_all, cut_keep, cut_near)
     mix_grads[0] = after(mix_own, grad_w_gate, grad_w_up, *out_sums[1:])
 
     grad_query, *pair_parts = attend_backward(place, mix_grads, query, pairs, mix, gain_rows)

time: 186 us -> 172 us (0.925)
  Pallas kernels: 34 us -> 27.4 us
  starting transfers between devices: 56.6 us -> 51.2 us
  waiting for transfers between devices: 79.2 us -> 75.8 us
    pallas_call x13, Pallas kernels: 34 us -> 27.4 us  [run_kernel(): pl.pallas_call(body, in_specs=[pl.BlockSpec(memory_space=pltpu.SMEM)] + [...]
    ppermute x26, starting transfers between devices: 37.8 us -> 33.3 us  [crossed(): return lax.ppermute(x, 'ctx', [(i, i ^ bits) for i in range(4)])]
    ppermute x30, waiting for transfers between devices: 17 us -> 14.4 us  [swapped(): return lax.ppermute(x, 'exp', [(i, i ^ bits) for i in range(4)])]
  transfers between devices with their start and end apart: 57 -> 57, of which waited for: 24 -> 26; matrix products, arithmetic and copies ran while one was open for 5% -> 5% of each run, Pallas kernels for 10% -> 11%
where the time goes in v5:
time: 172 us; the launch traced here: 171 us
  waiting for transfers between devices  75.8 us (44%)
  starting transfers between devices  51.2 us (30%)
  Pallas kernels  27.4 us (16%)
  local copies, waits for them, and re-layouts  7.88 us (5%)
  matrix products  7.04 us (4%)
    ppermute x26, waiting for transfers between devices, crossed(): return lax.ppermute(x, 'ctx', [(i, i ^ bits) for i in range(4)])  58.6 us
    ppermute x26, starting transfers between devices, crossed(): return lax.ppermute(x, 'ctx', [(i, i ^ bits) for i in range(4)])  33.3 us
    pallas_call x13, Pallas kernels, run_kernel(): pl.pallas_call(body, in_specs=[pl.BlockSpec(memory_space=pltpu.SMEM)] + [...  27.4 us
    ppermute x30, starting transfers between devices, swapped(): return lax.ppermute(x, 'exp', [(i, i ^ bits) for i in range(4)])  16.3 us
    ppermute x30, waiting for transfers between devices, swapped(): return lax.ppermute(x, 'exp', [(i, i ^ bits) for i in range(4)])  14.4 us
    unnamed x42, local copies, waits for them, and re-layouts  7.78 us
    dot_general x3, matrix products, tn(): lax.dot_general(a, b, (((0,), (0,)), ((), ())), preferred_element_type=F32)  7.04 us
  transfers between devices with their start and end apart: 57, of which 26 were waited for; matrix products, arithmetic and copies ran while one was open for 5% of the time, Pallas kernels for 11%

profile of v5, /device:TPU:0, one launch (start us, length us, event | category | flops | bytes accessed | tf_op | source)
XLA Modules:
  0.0 171.2 jit_solution(1988808636840823437)
XLA Ops:
  3.8 3.1 %collective-permute-start = (bf16[128,1280]{1,0:T(8,128)(2,1)S(1)}, bf16[128,1280]{1,0:T(8,128)(2,1)S(1)}, u32[]{:S(2)}, u32[]{:S(2)}) collective-permute-start(bf16[128,1280]{1,0:T(8,128)(2,1)S(1)} %pack_heads.1.refs_0_), channel_id=1, source_target_pairs={{0,4},{4,0},{8,12},{12,8},{1,5},{5,1},{9,13},{13,9},{2,6},{6,2},{1... | collective-permute-start | bytes 983048 | tf_op jit(solution)/shard_map/gather_heads/ppermute | solution.py:272
  6.9 2.6 %collective-permute-start.1 = (bf16[128,1280]{1,0:T(8,128)(2,1)S(1)}, bf16[128,1280]{1,0:T(8,128)(2,1)S(1)}, u32[]{:S(2)}, u32[]{:S(2)}) collective-permute-start(bf16[128,1280]{1,0:T(8,128)(2,1)S(1)} %pack_heads.1.refs_0_), channel_id=1, source_target_pairs={{0,8},{4,12},{8,0},{12,4},{1,9},{5,13},{9,1},{13,5},{2,10},{6,14},... | collective-permute-start | bytes 983048 | tf_op jit(solution)/shard_map/gather_heads/ppermute | solution.py:272
  13.6 11.0 %collective-permute-done.2.third_ref = bf16[32,512]{1,0:T(8,128)(2,1)S(1)} collective-permute-done((bf16[32,512]{1,0:T(8,128)(2,1)S(1)}, bf16[32,512]{1,0:T(8,128)(2,1)S(1)}, u32[]{:S(2)}, u32[]{:S(2)}) %collective-permute-start.2) | collective-permute-done | bytes 32800 | tf_op jit(solution)/shard_map/gather_heads/ppermute | solution.py:272
  26.0 6.9 %collective-permute-done.3.refs_3_ = bf16[128,1280]{1,0:T(8,128)(2,1)S(1)} collective-permute-done((bf16[128,1280]{1,0:T(8,128)(2,1)S(1)}, bf16[128,1280]{1,0:T(8,128)(2,1)S(1)}, u32[]{:S(2)}, u32[]{:S(2)}) %collective-permute-start.3) | collective-permute-done | bytes 327712 | tf_op jit(solution)/shard_map/gather_heads/ppermute | solution.py:272
  34.1 3.9 %attend.1 = (bf16[512,1024]{1,0:T(8,128)(2,1)S(1)}, bf16[128,1024]{1,0:T(8,128)(2,1)S(1)}, bf16[2,4,32,512]{3,2,1,0:T(8,128)(2,1)S(1)}, bf16[2,4,32,512]{3,2,1,0:T(8,128)(2,1)S(1)}, bf16[512,256]{1,0:T(8,128)(2,1)S(1)}) custom-call(s32[3]{0:T(128)S(1)} %pad_add_fusion.place_ref, bf16[128,1280]{1,0:T(8,128)(2,1)S(1)} %pack_heads.1.refs_0_, ...), custom_call_target="tpu_custom_call" | custom-call | flops 1073741824 | bytes 4456448 | tf_op jit(solution)/shard_map/attend/pallas_call | solution.py:299
  42.8 7.2 %collective-permute-done.7.far_ref = bf16[32,2688]{1,0:T(8,128)(2,1)S(1)} collective-permute-done((bf16[32,2688]{1,0:T(8,128)(2,1)S(1)}, bf16[32,2688]{1,0:T(8,128)(2,1)S(1)}, u32[]{:S(2)}, u32[]{:S(2)}) %collective-permute-start.7) | collective-permute-done | bytes 172064 | tf_op jit(solution)/shard_map/gather_rows/ppermute | solution.py:272
  55.4 3.5 %collective-permute-done.8.refs_1_ = bf16[4,32,512]{2,1,0:T(8,128)(2,1)S(1)} collective-permute-done((bf16[4,32,512]{2,1,0:T(8,128)(2,1)S(1)}, bf16[4,32,512]{2,1,0:T(8,128)(2,1)S(1)}, u32[]{:S(2)}, u32[]{:S(2)}) %collective-permute-start.8) | collective-permute-done | bytes 131104 | tf_op jit(solution)/shard_map/gather_hidden/ppermute | solution.py:272
  58.9 3.1 %collective-permute-done.9.refs_2_ = bf16[4,32,512]{2,1,0:T(8,128)(2,1)} collective-permute-done((bf16[4,32,512]{2,1,0:T(8,128)(2,1)S(1)}, bf16[4,32,512]{2,1,0:T(8,128)(2,1)}, u32[]{:S(2)}, u32[]{:S(2)}) %collective-permute-start.9) | collective-permute-done | bytes 131104 | tf_op jit(solution)/shard_map/gather_hidden/ppermute | solution.py:272
  73.1 3.7 %collective-permute-done.12.refs_5_ = bf16[4,32,512]{2,1,0:T(8,128)(2,1)S(1)} collective-permute-done((bf16[4,32,512]{2,1,0:T(8,128)(2,1)S(1)}, bf16[4,32,512]{2,1,0:T(8,128)(2,1)S(1)}, u32[]{:S(2)}, u32[]{:S(2)}) %collective-permute-start.12) | collective-permute-done | bytes 131104 | tf_op jit(solution)/shard_map/gather_hidden/ppermute | solution.py:276
  80.0 2.4 %grad_rows.1 = (bf16[512,2048]{1,0:T(8,128)(2,1)S(1)}, f32[512,1]{1,0:T(8,128)S(1)}, f32[512,384]{1,0:T(8,128)S(1)}) custom-call(s32[3]{0:T(128)S(1)} %pad_add_fusion.place_ref, bf16[3,32,2176]{2,1,0:T(8,128)(2,1)S(1)} %pad_maximum_fusion.refs_0_, bf16[32,2176]{1,0:T(8,128)(2,1)S(1)} %collective-permute-done.15.refs_1_, ...), custom_call_target="tpu_custom_call" | custom-call | flops 805306368 | bytes 6686720 | tf_op jit(solution)/shard_map/grad_rows/pallas_call | solution.py:299
  87.1 6.4 %expert_rows.1 = (bf16[512,2048]{1,0:T(8,128)(2,1)S(1)}, bf16[512,384]{1,0:T(8,128)(2,1)S(1)}, bf16[512,384]{1,0:T(8,128)(2,1)S(1)}, bf16[512,384]{1,0:T(8,128)(...) custom-call(s32[3]{0:T(128)S(1)} %pad_add_fusion.place_ref, ...), custom_call_target="tpu_custom_call" | custom-call | flops 3221225472 | bytes 11542528 | tf_op jit(solution)/shard_map/expert_rows/pallas_call | solution.py:299
  96.7 2.8 %collective-permute-done.35.refs_6_ = bf16[512,512]{1,0:T(8,128)(2,1)S(1)} collective-permute-done((bf16[512,512]{1,0:T(8,128)(2,1)S(1)}, bf16[512,512]{1,0:T(8,128)(2,1)S(1)}, u32[]{:S(2)}, u32[]{:S(2)}) %collective-permute-start.35) | collective-permute-done | bytes 524320 | tf_op jit(solution)/shard_map/gather_proj/ppermute | solution.py:849
  103.0 2.5 %collective-permute-done.37 = bf16[2,32,512]{2,1,0:T(8,128)(2,1)S(1)} collective-permute-done((bf16[2,32,512]{2,1,0:T(8,128)(2,1)S(1)}, bf16[2,32,512]{2,1,0:T(8,128)(2,1)S(1)}, u32[]{:S(2)}, u32[]{:S(2)}) %collective-permute-start.37) | collective-permute-done | bytes 65568 | tf_op jit(solution)/shard_map/sum_row_grads/ppermute | solution.py:272
  108.8 2.7 %collective-permute-done.39 = bf16[2,32,512]{2,1,0:T(8,128)(2,1)S(1)} collective-permute-done((bf16[2,32,512]{2,1,0:T(8,128)(2,1)S(1)}, bf16[2,32,512]{2,1,0:T(8,128)(2,1)S(1)}, u32[]{:S(2)}, u32[]{:S(2)}) %collective-permute-start.39) | collective-permute-done | bytes 65568 | tf_op jit(solution)/shard_map/sum_row_grads/ppermute | solution.py:272
  115.4 3.0 %collective-permute-start.41 = (bf16[32,1536]{1,0:T(8,128)(2,1)S(1)}, bf16[32,1536]{1,0:T(8,128)(2,1)S(1)}, u32[]{:S(2)}, u32[]{:S(2)}) collective-permute-start(bf16[32,1536]{1,0:T(8,128)(2,1)S(1)} %get-tuple-element.114), channel_id=1, source_target_pairs={{0,4},{4,0},{8,12},{12,8},{1,5},{5,1},{9,13},{13,9},{2,6},{6,2},{1... | collective-permute-start | bytes 294920 | tf_op jit(solution)/shard_map/sum_row_grads/ppermute | solution.py:272
  120.6 2.5 %collective-permute-done.40 = bf16[4,32,2048]{2,1,0:T(8,128)(2,1)S(1)} collective-permute-done((bf16[4,32,2048]{2,1,0:T(8,128)(2,1)S(1)}, bf16[4,32,2048]{2,1,0:T(8,128)(2,1)S(1)}, u32[]{:S(2)}, u32[]{:S(2)}) %collective-permute-start.40) | collective-permute-done | bytes 524320 | tf_op jit(solution)/shard_map/sum_outputs/ppermute | solution.py:276
  125.8 5.7 %collective-permute-done.45 = bf16[48,1024]{1,0:T(8,128)(2,1)S(1)} collective-permute-done((bf16[48,1024]{1,0:T(8,128)(2,1)S(1)}, bf16[48,1024]{1,0:T(8,128)(2,1)S(1)}, u32[]{:S(2)}, u32[]{:S(2)}) %collective-permute-start.45) | collective-permute-done | bytes 98336 | tf_op jit(solution)/shard_map/gather_cuts/ppermute | solution.py:272
  134.0 3.2 %collective-permute-done.50.refs_2_ = bf16[2,48,1024]{2,1,0:T(8,128)(2,1)S(1)} collective-permute-done((bf16[2,48,1024]{2,1,0:T(8,128)(2,1)S(1)}, bf16[2,48,1024]{2,1,0:T(8,128)(2,1)S(1)}, u32[]{:S(2)}, u32[]{:S(2)}) %collective-permute-start.50) | collective-permute-done | bytes 196640 | tf_op jit(solution)/shard_map/gather_cuts/ppermute | solution.py:276
  140.2 2.5 %collective-permute-start.56 = (bf16[256,512]{1,0:T(8,128)(2,1)S(1)}, bf16[256,512]{1,0:T(8,128)(2,1)S(1)}, u32[]{:S(2)}, u32[]{:S(2)}) collective-permute-start(bf16[256,512]{1,0:T(8,128)(2,1)S(1)} %get-tuple-element.148), channel_id=1, source_target_pairs={{0,4},{4,0},{8,12},{12,8},{1,5},{5,1},{9,13},{13,9},{2,6},{6,2},{1... | collective-permute-start | bytes 786440 | tf_op jit(solution)/shard_map/gather_cuts/ppermute | solution.py:272
  144.5 2.4 %convolution_convert_fusion = bf16[2048,384]{1,0:T(8,128)(2,1)} fusion(bf16[512,2048]{1,0:T(8,128)(2,1)S(1)} %get-tuple-element.129, bf16[512,384]{1,0:T(8,128)(2,1)S(1)} %get-tuple-element.131), kind=kOutput, calls=%fused_computation | convolution fusion | flops 806092800 | bytes 4063232 | tf_op jit(solution)/shard_map/dot_general | solution.py:288
  146.9 2.4 %convolution_convert_fusion.1 = bf16[2048,384]{1,0:T(8,128)(2,1)} fusion(bf16[512,2048]{1,0:T(8,128)(2,1)S(1)} %get-tuple-element.129, bf16[512,384]{1,0:T(8,128)(2,1)S(1)} %get-tuple-element.130), kind=kOutput, calls=%fused_computation.1 | convolution fusion | flops 806092800 | bytes 4063232 | tf_op jit(solution)/shard_map/dot_general | solution.py:288
  149.4 8.7 %collective-permute-done.52.refs_1_ = bf16[128,1024]{1,0:T(8,128)(2,1)S(1)} collective-permute-done((bf16[128,1024]{1,0:T(8,128)(2,1)S(1)}, bf16[128,1024]{1,0:T(8,128)(2,1)S(1)}, u32[]{:S(2)}, u32[]{:S(2)}) %collective-permute-start.52) | collective-permute-done | bytes 262176 | tf_op jit(solution)/shard_map/sum_mix_grad/ppermute | solution.py:272
  158.1 3.2 %attend_backward.1 = (bf16[128,1024]{1,0:T(8,128)(2,1)}, bf16[144,256]{1,0:T(8,128)(2,1)S(1)}, bf16[144,256]{1,0:T(8,128)(2,1)S(1)}, bf16[144,256]{1,0:T(8,128)(2,1)S(1)}, bf16[144,256]{1,0:T(8,128)(2,1)S(1)}) custom-call(s32[3]{0:T(128)S(1)} %pad_add_fusion.place_ref, bf16[128,1024]{1,0:T(8,128)(2,1)S(1)} %get-tuple-element.132.refs_0_, ...), custom_call_target="tpu_custom_call" | custom-call | flops 671088640 | bytes 1875968 | tf_op jit(solution)/shard_map/attend_backward/pallas_call | solution.py:299
  163.3 2.3 %collective-permute-start.55 = (bf16[144,256]{1,0:T(8,128)(2,1)S(1)}, bf16[144,256]{1,0:T(8,128)(2,1)S(1)}, u32[]{:S(2)}, u32[]{:S(2)}) collective-permute-start(bf16[144,256]{1,0:T(8,128)(2,1)S(1)} %get-tuple-element.143), channel_id=1, source_target_pairs={{0,12},{4,8},{8,4},{12,0},{1,13},{5,9},{9,5},{13,1},{2,14},{6,10},... | collective-permute-start | bytes 221192 | tf_op jit(solution)/shard_map/sum_pairs/ppermute | solution.py:272
  (164 shorter events, 72.4 us)
Async XLA Ops:
  3.8 20.8 %collective-permute-start = (bf16[128,1280]{1,0:T(8,128)(2,1)S(1)}, bf16[128,1280]{1,0:T(8,128)(2,1)S(1)}, u32[]{:S(2)}, u32[]{:S(2)}) collective-permute-start(bf16[128,1280]{1,0:T(8,128)(2,1)S(1)} %pack_heads.1.refs_0_), channel_id=1, source_target_pairs={{0,4},{4,0},{8,12},{12,8},{1,5},{5,1},{9,13},{13,9},{2,6},{6,2},{1... | collective-permute-start | bytes 983048 | tf_op jit(solution)/shard_map/gather_heads/ppermute | solution.py:272
  6.9 18.2 %collective-permute-start.1 = (bf16[128,1280]{1,0:T(8,128)(2,1)S(1)}, bf16[128,1280]{1,0:T(8,128)(2,1)S(1)}, u32[]{:S(2)}, u32[]{:S(2)}) collective-permute-start(bf16[128,1280]{1,0:T(8,128)(2,1)S(1)} %pack_heads.1.refs_0_), channel_id=1, source_target_pairs={{0,8},{4,12},{8,0},{12,4},{1,9},{5,13},{9,1},{13,5},{2,10},{6,14},... | collective-permute-start | bytes 983048 | tf_op jit(solution)/shard_map/gather_heads/ppermute | solution.py:272
  13.5 11.1 %collective-permute-start.2 = (bf16[32,512]{1,0:T(8,128)(2,1)S(1)}, bf16[32,512]{1,0:T(8,128)(2,1)S(1)}, u32[]{:S(2)}, u32[]{:S(2)}) collective-permute-start(bf16[32,512]{1,0:T(8,128)(2,1)S(1)} %get-tuple-element.82), channel_id=1, source_target_pairs={{0,12},{4,8},{8,4},{12,0},{1,13},{5,9},{9,5},{13,1},{2,14},{6,10},... | collective-permute-start | bytes 98312 | tf_op jit(solution)/shard_map/gather_heads/ppermute | solution.py:272
  38.8 11.3 %collective-permute-start.7 = (bf16[32,2688]{1,0:T(8,128)(2,1)S(1)}, bf16[32,2688]{1,0:T(8,128)(2,1)S(1)}, u32[]{:S(2)}, u32[]{:S(2)}) collective-permute-start(bf16[32,2688]{1,0:T(8,128)(2,1)S(1)} %get-tuple-element.92), channel_id=1, source_target_pairs={{0,8},{4,12},{8,0},{12,4},{1,9},{5,13},{9,1},{13,5},{2,10},{6,14},... | collective-permute-start | bytes 516104 | tf_op jit(solution)/shard_map/gather_rows/ppermute | solution.py:272
  40.9 10.0 %collective-permute-start.6 = (bf16[32,2688]{1,0:T(8,128)(2,1)S(1)}, bf16[32,2688]{1,0:T(8,128)(2,1)S(1)}, u32[]{:S(2)}, u32[]{:S(2)}) collective-permute-start(bf16[32,2688]{1,0:T(8,128)(2,1)S(1)} %get-tuple-element.86), channel_id=1, source_target_pairs={{0,4},{4,0},{8,12},{12,8},{1,5},{5,1},{9,13},{13,9},{2,6},{6,2},{1... | collective-permute-start | bytes 516104 | tf_op jit(solution)/shard_map/gather_rows/ppermute | solution.py:272
  41.3 9.7 %collective-permute-start.5 = (bf16[4,32,512]{2,1,0:T(8,128)(2,1)S(1)}, bf16[4,32,512]{2,1,0:T(8,128)(2,1)S(1)}, u32[]{:S(2)}, u32[]{:S(2)}) collective-permute-start(bf16[4,32,512]{2,1,0:T(8,128)(2,1)S(1)} %fusion.5), channel_id=1, source_target_pairs={{0,2},{1,3},{2,0},{3,1},{4,6},{5,7},{6,4},{7,5},{8,10},{9,11},{10,... | collective-permute-start | bytes 393224 | tf_op jit(solution)/shard_map/sum_heads/ppermute | solution.py:276
  51.7 15.4 %collective-permute-start.16 = (bf16[3,32,2176]{2,1,0:T(8,128)(2,1)S(1)}, bf16[3,32,2176]{2,1,0:T(8,128)(2,1)}, u32[]{:S(2)}, u32[]{:S(2)}) collective-permute-start(bf16[3,32,2176]{2,1,0:T(8,128)(2,1)S(1)} %pad_maximum_fusion.refs_0_), channel_id=1, source_target_pairs={{0,2},{1,3},{2,0},{3,1},{4,6},{5,7},{6,4},{7,5},{8,10},{9,11},{10,... | collective-permute-start | bytes 1253384 | tf_op jit(solution)/shard_map/gather_rows/ppermute | solution.py:276
  53.7 8.3 %collective-permute-start.9 = (bf16[4,32,512]{2,1,0:T(8,128)(2,1)S(1)}, bf16[4,32,512]{2,1,0:T(8,128)(2,1)}, u32[]{:S(2)}, u32[]{:S(2)}) collective-permute-start(bf16[4,32,512]{2,1,0:T(8,128)(2,1)S(1)} %hidden_rows.1.refs_0_), channel_id=1, source_target_pairs={{0,8},{4,12},{8,0},{12,4},{1,9},{5,13},{9,1},{13,5},{2,10},{6,14},... | collective-permute-start | bytes 393224 | tf_op jit(solution)/shard_map/gather_hidden/ppermute | solution.py:272
  54.9 10.7 %collective-permute-start.11 = (bf16[4,32,512]{2,1,0:T(8,128)(2,1)S(1)}, bf16[4,32,512]{2,1,0:T(8,128)(2,1)}, u32[]{:S(2)}, u32[]{:S(2)}) collective-permute-start(bf16[4,32,512]{2,1,0:T(8,128)(2,1)S(1)} %hidden_rows.1.refs_0_), channel_id=1, source_target_pairs={{0,2},{1,3},{2,0},{3,1},{4,6},{5,7},{6,4},{7,5},{8,10},{9,11},{10,... | collective-permute-start | bytes 393224 | tf_op jit(solution)/shard_map/gather_hidden/ppermute | solution.py:276
  62.0 17.4 %collective-permute-start.18 = (bf16[3,32,2176]{2,1,0:T(8,128)(2,1)S(1)}, bf16[3,32,2176]{2,1,0:T(8,128)(2,1)S(1)}, u32[]{:S(2)}, u32[]{:S(2)}) collective-permute-start(bf16[3,32,2176]{2,1,0:T(8,128)(2,1)S(1)} %pad_maximum_fusion.refs_0_), channel_id=1, source_target_pairs={{0,1},{1,0},{2,3},{3,2},{4,5},{5,4},{6,7},{7,6},{8,9},{9,8},{10,11... | collective-permute-start | bytes 1253384 | tf_op jit(solution)/shard_map/gather_rows/ppermute | solution.py:276
  67.1 12.9 %collective-permute-start.20 = (bf16[3,32,2176]{2,1,0:T(8,128)(2,1)}, bf16[3,32,2176]{2,1,0:T(8,128)(2,1)S(1)}, u32[]{:S(2)}, u32[]{:S(2)}) collective-permute-start(bf16[3,32,2176]{2,1,0:T(8,128)(2,1)} %collective-permute-done.16.refs_2_), channel_id=1, source_target_pairs={{0,1},{1,0},{2,3},{3,2},{4,5},{5,4},{6,7},{7,6},{8,9},{9,8},{10,11... | collective-permute-start | bytes 1253384 | tf_op jit(solution)/shard_map/gather_rows/ppermute | solution.py:276
  68.5 15.4 %collective-permute-start.22 = (bf16[512,512]{1,0:T(8,128)(2,1)S(1)}, bf16[512,512]{1,0:T(8,128)(2,1)S(1)}, u32[]{:S(2)}, u32[]{:S(2)}) collective-permute-start(bf16[512,512]{1,0:T(8,128)(2,1)S(1)} %constant_dynamic-slice_fusion), channel_id=1, source_target_pairs={{0,4},{4,0},{8,12},{12,8},{1,5},{5,1},{9,13},{13,9},{2,6},{6,2},{1... | collective-permute-start | bytes 1572872 | tf_op jit(solution)/shard_map/gather_proj/ppermute | solution.py:272
  85.5 14.0 %collective-permute-start.35 = (bf16[512,512]{1,0:T(8,128)(2,1)S(1)}, bf16[512,512]{1,0:T(8,128)(2,1)S(1)}, u32[]{:S(2)}, u32[]{:S(2)}) collective-permute-start(bf16[512,512]{1,0:T(8,128)(2,1)S(1)} %collective-permute-done.22.refs_5_), channel_id=1, source_target_pairs={{0,16},{16,0},{1,17},{17,1},{2,18},{18,2},{3,19},{19,3},{4,20},{20... | collective-permute-start | bytes 1572872 | tf_op jit(solution)/shard_map/gather_proj/ppermute | solution.py:849
  94.1 17.5 %collective-permute-start.32 = (bf16[4,32,1536]{2,1,0:T(8,128)(2,1)S(1)}, bf16[4,32,1536]{2,1,0:T(8,128)(2,1)S(1)}, u32[]{:S(2)}, u32[]{:S(2)}) collective-permute-start(bf16[4,32,1536]{2,1,0:T(8,128)(2,1)S(1)} %get-tuple-element.105), channel_id=1, source_target_pairs={{0,1},{1,0},{2,3},{3,2},{4,5},{5,4},{6,7},{7,6},{8,9},{9,8},{10,11... | collective-permute-start | bytes 1179656 | tf_op jit(solution)/shard_map/sum_row_grads/ppermute | solution.py:276
  96.2 15.6 %collective-permute-start.31 = (bf16[2,4,32,2048]{3,2,1,0:T(8,128)(2,1)S(1)}, bf16[2,4,32,2048]{3,2,1,0:T(8,128)(2,1)S(1)}, u32[]{:S(2)}, u32[]{:S(2)}) collective-permute-start(bf16[2,4,32,2048]{3,2,1,0:T(8,128)(2,1)S(1)} %get-tuple-element.103), channel_id=1, source_target_pairs={{0,1},{1,0},{2,3},{3,2},{4,5},{5,4},{6,7},{7,6},{8,9},{9,8},{10,11... | collective-permute-start | bytes 3145736 | tf_op jit(solution)/shard_map/sum_outputs/ppermute | solution.py:276
  99.6 12.0 %collective-permute-start.36 = (bf16[4,32,1536]{2,1,0:T(8,128)(2,1)S(1)}, bf16[4,32,1536]{2,1,0:T(8,128)(2,1)S(1)}, u32[]{:S(2)}, u32[]{:S(2)}) collective-permute-start(bf16[4,32,1536]{2,1,0:T(8,128)(2,1)S(1)} %add_convert_fusion.1), channel_id=1, source_target_pairs={{0,2},{1,3},{2,0},{3,1},{4,6},{5,7},{6,4},{7,5},{8,10},{9,11},{10,... | collective-permute-start | bytes 1179656 | tf_op jit(solution)/shard_map/sum_row_grads/ppermute | solution.py:276
  111.9 11.1 %collective-permute-start.40 = (bf16[4,32,2048]{2,1,0:T(8,128)(2,1)S(1)}, bf16[4,32,2048]{2,1,0:T(8,128)(2,1)S(1)}, u32[]{:S(2)}, u32[]{:S(2)}) collective-permute-start(bf16[4,32,2048]{2,1,0:T(8,128)(2,1)S(1)} %fusion), channel_id=1, source_target_pairs={{0,2},{1,3},{2,0},{3,1},{4,6},{5,7},{6,4},{7,5},{8,10},{9,11},{10,... | collective-permute-start | bytes 1572872 | tf_op jit(solution)/shard_map/sum_outputs/ppermute | solution.py:276
  112.8 10.6 %collective-permute-start.44 = (bf16[32,512]{1,0:T(8,128)(2,1)S(1)}, bf16[32,512]{1,0:T(8,128)(2,1)S(1)}, u32[]{:S(2)}, u32[]{:S(2)}) collective-permute-start(bf16[32,512]{1,0:T(8,128)(2,1)S(1)} %get-tuple-element.161), channel_id=1, source_target_pairs={{0,2},{1,3},{2,0},{3,1},{4,6},{5,7},{6,4},{7,5},{8,10},{9,11},{10,... | collective-permute-start | bytes 98312 | tf_op jit(solution)/shard_map/sum_row_grads/ppermute | solution.py:276
  114.0 9.4 %collective-permute-start.43 = (bf16[32,1536]{1,0:T(8,128)(2,1)S(1)}, bf16[32,1536]{1,0:T(8,128)(2,1)S(1)}, u32[]{:S(2)}, u32[]{:S(2)}) collective-permute-start(bf16[32,1536]{1,0:T(8,128)(2,1)S(1)} %get-tuple-element.116), channel_id=1, source_target_pairs={{0,12},{4,8},{8,4},{12,0},{1,13},{5,9},{9,5},{13,1},{2,14},{6,10},... | collective-permute-start | bytes 294920 | tf_op jit(solution)/shard_map/sum_row_grads/ppermute | solution.py:272
  133.8 15.5 %collective-permute-start.46 = (bf16[32,2048]{1,0:T(8,128)(2,1)S(1)}, bf16[32,2048]{1,0:T(8,128)(2,1)S(1)}, u32[]{:S(2)}, u32[]{:S(2)}) collective-permute-start(bf16[32,2048]{1,0:T(8,128)(2,1)S(1)} %get-tuple-element.124), channel_id=1, source_target_pairs={{0,4},{4,0},{8,12},{12,8},{1,5},{5,1},{9,13},{13,9},{2,6},{6,2},{1... | collective-permute-start | bytes 393224 | tf_op jit(solution)/shard_map/sum_outputs/ppermute | solution.py:272
  137.6 11.8 %collective-permute-start.48 = (bf16[32,2048]{1,0:T(8,128)(2,1)S(1)}, bf16[32,2048]{1,0:T(8,128)(2,1)S(1)}, u32[]{:S(2)}, u32[]{:S(2)}) collective-permute-start(bf16[32,2048]{1,0:T(8,128)(2,1)S(1)} %add_convert_fusion.2), channel_id=1, source_target_pairs={{0,8},{4,12},{8,0},{12,4},{1,9},{5,13},{9,1},{13,5},{2,10},{6,14},... | collective-permute-start | bytes 393224 | tf_op jit(solution)/shard_map/sum_outputs/ppermute | solution.py:272
  140.2 26.8 %collective-permute-start.56 = (bf16[256,512]{1,0:T(8,128)(2,1)S(1)}, bf16[256,512]{1,0:T(8,128)(2,1)S(1)}, u32[]{:S(2)}, u32[]{:S(2)}) collective-permute-start(bf16[256,512]{1,0:T(8,128)(2,1)S(1)} %get-tuple-element.148), channel_id=1, source_target_pairs={{0,4},{4,0},{8,12},{12,8},{1,5},{5,1},{9,13},{13,9},{2,6},{6,2},{1... | collective-permute-start | bytes 786440 | tf_op jit(solution)/shard_map/gather_cuts/ppermute | solution.py:272
  142.7 15.4 %collective-permute-start.52 = (bf16[128,1024]{1,0:T(8,128)(2,1)S(1)}, bf16[128,1024]{1,0:T(8,128)(2,1)S(1)}, u32[]{:S(2)}, u32[]{:S(2)}) collective-permute-start(bf16[128,1024]{1,0:T(8,128)(2,1)S(1)} %get-tuple-element.133), channel_id=1, source_target_pairs={{0,8},{4,12},{8,0},{12,4},{1,9},{5,13},{9,1},{13,5},{2,10},{6,14},... | collective-permute-start | bytes 786440 | tf_op jit(solution)/shard_map/sum_mix_grad/ppermute | solution.py:272
  161.3 8.7 %collective-permute-start.54 = (bf16[144,256]{1,0:T(8,128)(2,1)S(1)}, bf16[144,256]{1,0:T(8,128)(2,1)S(1)}, u32[]{:S(2)}, u32[]{:S(2)}) collective-permute-start(bf16[144,256]{1,0:T(8,128)(2,1)S(1)} %get-tuple-element.142), channel_id=1, source_target_pairs={{0,8},{4,12},{8,0},{12,4},{1,9},{5,13},{9,1},{13,5},{2,10},{6,14},... | collective-permute-start | bytes 221192 | tf_op jit(solution)/shard_map/sum_pairs/ppermute | solution.py:272
  (53 other events, 413.2 us)

commit v6 on v5

--- a/solution.py
+++ b/solution.py
@@ -316,18 +316,6 @@
     diagonal = offset <= lax.broadcasted_iota(jnp.int32, shape, 0)
     block = turn ^ base
     return (block < query_block) | ((block == query_block) & diagonal)
-
-
-def pack_heads(place, key, value, query):
-    rows, width = query.shape
-
-    def body(place_ref, key_ref, value_ref, query_ref, out_ref):
-        out_ref[:, :HEAD_SIZE] = key_ref[...]
-        out_ref[:, HEAD_SIZE : 2 * HEAD_SIZE] = value_ref[...]
-        out_ref[:, 2 * HEAD_SIZE :] = query_ref[...]
-
-    shape = (rows, width + 2 * HEAD_SIZE)
-    return run_kernel(body, "pack_heads", place, [key, value, query], [(shape, BF16)])[0]
 
 
 def pack_rows(place, grad_out, routes, gate_weights, resid, cols):
@@ -800,7 +788,7 @@
     with scope("gather_rows"):
         to_far, to_near, to_third = pack_rows(place, grad_out, routes, gate_weights, resid, cols)
     with scope("gather_heads"):
-        heads = pack_heads(place, key, value, query)
+        heads = jnp.concatenate([key, value, query], 1)
         far, near = crossed(heads, 2), crossed(heads, 1)
         row_third = crossed(to_third, 3)
         parts = [heads, near, far, crossed(after(far, near, to_far, to_near, row_third), 1)]

time: 172 us -> 171 us (level)
    unnamed x42 -> x38, local copies, waits for them, and re-layouts: 7.78 us -> 6.16 us
    pallas_call x13 -> x12, Pallas kernels: 27.4 us -> 26.9 us  [run_kernel(): pl.pallas_call(body, in_specs=[pl.BlockSpec(memory_space=pltpu.SMEM)] + [...]
  transfers between devices with their start and end apart: 57 -> 57, of which waited for: 26 -> 26; matrix products, arithmetic and copies ran while one was open for 5% -> 5% of each run, Pallas kernels for 11% -> 12%
where the time goes in v6:
time: 171 us; the launch traced here: 170 us
  waiting for transfers between devices  75.7 us (44%)
  starting transfers between devices  51.2 us (30%)
  Pallas kernels  26.9 us (16%)
  local copies, waits for them, and re-layouts  7.23 us (4%)
  matrix products  7.03 us (4%)
    ppermute x26, waiting for transfers between devices, crossed(): return lax.ppermute(x, 'ctx', [(i, i ^ bits) for i in range(4)])  58.5 us
    ppermute x26, starting transfers between devices, crossed(): return lax.ppermute(x, 'ctx', [(i, i ^ bits) for i in range(4)])  33.3 us
    pallas_call x12, Pallas kernels, run_kernel(): pl.pallas_call(body, in_specs=[pl.BlockSpec(memory_space=pltpu.SMEM)] + [...  26.9 us
    ppermute x30, starting transfers between devices, swapped(): return lax.ppermute(x, 'exp', [(i, i ^ bits) for i in range(4)])  16.4 us
    ppermute x30, waiting for transfers between devices, swapped(): return lax.ppermute(x, 'exp', [(i, i ^ bits) for i in range(4)])  14.4 us
    dot_general x3, matrix products, tn(): lax.dot_general(a, b, (((0,), (0,)), ((), ())), preferred_element_type=F32)  7.03 us
    unnamed x38, local copies, waits for them, and re-layouts  6.16 us
  transfers between devices with their start and end apart: 57, of which 26 were waited for; matrix products, arithmetic and copies ran while one was open for 5% of the time, Pallas kernels for 12%

profile of v6, /device:TPU:0, one launch (start us, length us, event | category | flops | bytes accessed | tf_op | source)
XLA Modules:
  0.0 170.0 jit_solution(18399237590187750353)
XLA Ops:
  3.1 3.1 %collective-permute-start = (bf16[128,1280]{1,0:T(8,128)(2,1)S(1)}, bf16[128,1280]{1,0:T(8,128)(2,1)S(1)}, u32[]{:S(2)}, u32[]{:S(2)}) collective-permute-start(bf16[128,1280]{1,0:T(8,128)(2,1)S(1)} %constant_dynamic-update-slice_fusion.refs_0_), channel_id=1, source_target_pairs={{0,4},{4,0},{8,12},{12,8},{1,5},{5,1},{9,13},{13,9},{2,6},{6,2},{1... | collective-permute-start | bytes 983048 | tf_op jit(solution)/shard_map/gather_heads/ppermute | solution.py:272
  6.2 2.6 %collective-permute-start.1 = (bf16[128,1280]{1,0:T(8,128)(2,1)S(1)}, bf16[128,1280]{1,0:T(8,128)(2,1)S(1)}, u32[]{:S(2)}, u32[]{:S(2)}) collective-permute-start(bf16[128,1280]{1,0:T(8,128)(2,1)S(1)} %constant_dynamic-update-slice_fusion.refs_0_), channel_id=1, source_target_pairs={{0,8},{4,12},{8,0},{12,4},{1,9},{5,13},{9,1},{13,5},{2,10},{6,14},... | collective-permute-start | bytes 983048 | tf_op jit(solution)/shard_map/gather_heads/ppermute | solution.py:272
  13.1 10.9 %collective-permute-done.2.third_ref = bf16[32,512]{1,0:T(8,128)(2,1)S(1)} collective-permute-done((bf16[32,512]{1,0:T(8,128)(2,1)S(1)}, bf16[32,512]{1,0:T(8,128)(2,1)S(1)}, u32[]{:S(2)}, u32[]{:S(2)}) %collective-permute-start.2) | collective-permute-done | bytes 32800 | tf_op jit(solution)/shard_map/gather_heads/ppermute | solution.py:272
  25.4 6.9 %collective-permute-done.3.refs_3_ = bf16[128,1280]{1,0:T(8,128)(2,1)S(1)} collective-permute-done((bf16[128,1280]{1,0:T(8,128)(2,1)S(1)}, bf16[128,1280]{1,0:T(8,128)(2,1)S(1)}, u32[]{:S(2)}, u32[]{:S(2)}) %collective-permute-start.3) | collective-permute-done | bytes 327712 | tf_op jit(solution)/shard_map/gather_heads/ppermute | solution.py:272
  33.5 3.9 %attend.1 = (bf16[512,1024]{1,0:T(8,128)(2,1)S(1)}, bf16[128,1024]{1,0:T(8,128)(2,1)S(1)}, bf16[2,4,32,512]{3,2,1,0:T(8,128)(2,1)S(1)}, bf16[2,4,32,512]{3,2,1,0:T(8,128)(2,1)S(1)}, bf16[512,256]{1,0:T(8,128)(2,1)S(1)}) custom-call(s32[3]{0:T(128)S(1)} %pad_add_fusion.place_ref, bf16[128,1280]{1,0:T(8,128)(2,1)S(1)} %constant_dynamic-update-slice_fusion.refs_0_, ...), custom_call_target="tpu_custom_call" | custom-call | flops 1073741824 | bytes 4456448 | tf_op jit(solution)/shard_map/attend/pallas_call | solution.py:299
  41.6 7.2 %collective-permute-done.7.far_ref = bf16[32,2688]{1,0:T(8,128)(2,1)S(1)} collective-permute-done((bf16[32,2688]{1,0:T(8,128)(2,1)S(1)}, bf16[32,2688]{1,0:T(8,128)(2,1)S(1)}, u32[]{:S(2)}, u32[]{:S(2)}) %collective-permute-start.7) | collective-permute-done | bytes 172064 | tf_op jit(solution)/shard_map/gather_rows/ppermute | solution.py:272
  54.2 3.5 %collective-permute-done.8.refs_1_ = bf16[4,32,512]{2,1,0:T(8,128)(2,1)S(1)} collective-permute-done((bf16[4,32,512]{2,1,0:T(8,128)(2,1)S(1)}, bf16[4,32,512]{2,1,0:T(8,128)(2,1)S(1)}, u32[]{:S(2)}, u32[]{:S(2)}) %collective-permute-start.8) | collective-permute-done | bytes 131104 | tf_op jit(solution)/shard_map/gather_hidden/ppermute | solution.py:272
  57.7 3.1 %collective-permute-done.9.refs_2_ = bf16[4,32,512]{2,1,0:T(8,128)(2,1)} collective-permute-done((bf16[4,32,512]{2,1,0:T(8,128)(2,1)S(1)}, bf16[4,32,512]{2,1,0:T(8,128)(2,1)}, u32[]{:S(2)}, u32[]{:S(2)}) %collective-permute-start.9) | collective-permute-done | bytes 131104 | tf_op jit(solution)/shard_map/gather_hidden/ppermute | solution.py:272
  69.6 2.3 %collective-permute-start.12 = (bf16[4,32,512]{2,1,0:T(8,128)(2,1)S(1)}, bf16[4,32,512]{2,1,0:T(8,128)(2,1)S(1)}, u32[]{:S(2)}, u32[]{:S(2)}) collective-permute-start(bf16[4,32,512]{2,1,0:T(8,128)(2,1)S(1)} %collective-permute-done.8.refs_1_), channel_id=1, source_target_pairs={{0,2},{1,3},{2,0},{3,1},{4,6},{5,7},{6,4},{7,5},{8,10},{9,11},{10,... | collective-permute-start | bytes 393224 | tf_op jit(solution)/shard_map/gather_hidden/ppermute | solution.py:276
  71.9 3.7 %collective-permute-done.12.refs_5_ = bf16[4,32,512]{2,1,0:T(8,128)(2,1)S(1)} collective-permute-done((bf16[4,32,512]{2,1,0:T(8,128)(2,1)S(1)}, bf16[4,32,512]{2,1,0:T(8,128)(2,1)S(1)}, u32[]{:S(2)}, u32[]{:S(2)}) %collective-permute-start.12) | collective-permute-done | bytes 131104 | tf_op jit(solution)/shard_map/gather_hidden/ppermute | solution.py:276
  78.8 2.4 %grad_rows.1 = (bf16[512,2048]{1,0:T(8,128)(2,1)S(1)}, f32[512,1]{1,0:T(8,128)S(1)}, f32[512,384]{1,0:T(8,128)S(1)}) custom-call(s32[3]{0:T(128)S(1)} %pad_add_fusion.place_ref, bf16[3,32,2176]{2,1,0:T(8,128)(2,1)S(1)} %pad_maximum_fusion.refs_0_, bf16[32,2176]{1,0:T(8,128)(2,1)S(1)} %collective-permute-done.15.refs_1_, ...), custom_call_target="tpu_custom_call" | custom-call | flops 805306368 | bytes 6686720 | tf_op jit(solution)/shard_map/grad_rows/pallas_call | solution.py:299
  85.9 6.4 %expert_rows.1 = (bf16[512,2048]{1,0:T(8,128)(2,1)S(1)}, bf16[512,384]{1,0:T(8,128)(2,1)S(1)}, bf16[512,384]{1,0:T(8,128)(2,1)S(1)}, bf16[512,384]{1,0:T(8,128)(...) custom-call(s32[3]{0:T(128)S(1)} %pad_add_fusion.place_ref, ...), custom_call_target="tpu_custom_call" | custom-call | flops 3221225472 | bytes 11542528 | tf_op jit(solution)/shard_map/expert_rows/pallas_call | solution.py:299
  95.5 2.8 %collective-permute-done.35.refs_6_ = bf16[512,512]{1,0:T(8,128)(2,1)S(1)} collective-permute-done((bf16[512,512]{1,0:T(8,128)(2,1)S(1)}, bf16[512,512]{1,0:T(8,128)(2,1)S(1)}, u32[]{:S(2)}, u32[]{:S(2)}) %collective-permute-start.35) | collective-permute-done | bytes 524320 | tf_op jit(solution)/shard_map/gather_proj/ppermute | solution.py:837
  101.8 2.5 %collective-permute-done.37 = bf16[2,32,512]{2,1,0:T(8,128)(2,1)S(1)} collective-permute-done((bf16[2,32,512]{2,1,0:T(8,128)(2,1)S(1)}, bf16[2,32,512]{2,1,0:T(8,128)(2,1)S(1)}, u32[]{:S(2)}, u32[]{:S(2)}) %collective-permute-start.37) | collective-permute-done | bytes 65568 | tf_op jit(solution)/shard_map/sum_row_grads/ppermute | solution.py:272
  107.6 2.7 %collective-permute-done.39 = bf16[2,32,512]{2,1,0:T(8,128)(2,1)S(1)} collective-permute-done((bf16[2,32,512]{2,1,0:T(8,128)(2,1)S(1)}, bf16[2,32,512]{2,1,0:T(8,128)(2,1)S(1)}, u32[]{:S(2)}, u32[]{:S(2)}) %collective-permute-start.39) | collective-permute-done | bytes 65568 | tf_op jit(solution)/shard_map/sum_row_grads/ppermute | solution.py:272
  114.2 3.0 %collective-permute-start.41 = (bf16[32,1536]{1,0:T(8,128)(2,1)S(1)}, bf16[32,1536]{1,0:T(8,128)(2,1)S(1)}, u32[]{:S(2)}, u32[]{:S(2)}) collective-permute-start(bf16[32,1536]{1,0:T(8,128)(2,1)S(1)} %get-tuple-element.114), channel_id=1, source_target_pairs={{0,4},{4,0},{8,12},{12,8},{1,5},{5,1},{9,13},{13,9},{2,6},{6,2},{1... | collective-permute-start | bytes 294920 | tf_op jit(solution)/shard_map/sum_row_grads/ppermute | solution.py:272
  119.4 2.5 %collective-permute-done.40 = bf16[4,32,2048]{2,1,0:T(8,128)(2,1)S(1)} collective-permute-done((bf16[4,32,2048]{2,1,0:T(8,128)(2,1)S(1)}, bf16[4,32,2048]{2,1,0:T(8,128)(2,1)S(1)}, u32[]{:S(2)}, u32[]{:S(2)}) %collective-permute-start.40) | collective-permute-done | bytes 524320 | tf_op jit(solution)/shard_map/sum_outputs/ppermute | solution.py:276
  124.6 5.7 %collective-permute-done.45 = bf16[48,1024]{1,0:T(8,128)(2,1)S(1)} collective-permute-done((bf16[48,1024]{1,0:T(8,128)(2,1)S(1)}, bf16[48,1024]{1,0:T(8,128)(2,1)S(1)}, u32[]{:S(2)}, u32[]{:S(2)}) %collective-permute-start.45) | collective-permute-done | bytes 98336 | tf_op jit(solution)/shard_map/gather_cuts/ppermute | solution.py:272
  132.8 3.2 %collective-permute-done.50.refs_2_ = bf16[2,48,1024]{2,1,0:T(8,128)(2,1)S(1)} collective-permute-done((bf16[2,48,1024]{2,1,0:T(8,128)(2,1)S(1)}, bf16[2,48,1024]{2,1,0:T(8,128)(2,1)S(1)}, u32[]{:S(2)}, u32[]{:S(2)}) %collective-permute-start.50) | collective-permute-done | bytes 196640 | tf_op jit(solution)/shard_map/gather_cuts/ppermute | solution.py:276
  139.0 2.5 %collective-permute-start.56 = (bf16[256,512]{1,0:T(8,128)(2,1)S(1)}, bf16[256,512]{1,0:T(8,128)(2,1)S(1)}, u32[]{:S(2)}, u32[]{:S(2)}) collective-permute-start(bf16[256,512]{1,0:T(8,128)(2,1)S(1)} %get-tuple-element.148), channel_id=1, source_target_pairs={{0,4},{4,0},{8,12},{12,8},{1,5},{5,1},{9,13},{13,9},{2,6},{6,2},{1... | collective-permute-start | bytes 786440 | tf_op jit(solution)/shard_map/gather_cuts/ppermute | solution.py:272
  143.3 2.4 %convolution_convert_fusion = bf16[2048,384]{1,0:T(8,128)(2,1)} fusion(bf16[512,2048]{1,0:T(8,128)(2,1)S(1)} %get-tuple-element.129, bf16[512,384]{1,0:T(8,128)(2,1)S(1)} %get-tuple-element.131), kind=kOutput, calls=%fused_computation | convolution fusion | flops 806092800 | bytes 4063232 | tf_op jit(solution)/shard_map/dot_general | solution.py:288
  145.7 2.4 %convolution_convert_fusion.1 = bf16[2048,384]{1,0:T(8,128)(2,1)} fusion(bf16[512,2048]{1,0:T(8,128)(2,1)S(1)} %get-tuple-element.129, bf16[512,384]{1,0:T(8,128)(2,1)S(1)} %get-tuple-element.130), kind=kOutput, calls=%fused_computation.1 | convolution fusion | flops 806092800 | bytes 4063232 | tf_op jit(solution)/shard_map/dot_general | solution.py:288
  148.2 8.7 %collective-permute-done.52.refs_1_ = bf16[128,1024]{1,0:T(8,128)(2,1)S(1)} collective-permute-done((bf16[128,1024]{1,0:T(8,128)(2,1)S(1)}, bf16[128,1024]{1,0:T(8,128)(2,1)S(1)}, u32[]{:S(2)}, u32[]{:S(2)}) %collective-permute-start.52) | collective-permute-done | bytes 262176 | tf_op jit(solution)/shard_map/sum_mix_grad/ppermute | solution.py:272
  156.9 3.2 %attend_backward.1 = (bf16[128,1024]{1,0:T(8,128)(2,1)}, bf16[144,256]{1,0:T(8,128)(2,1)S(1)}, bf16[144,256]{1,0:T(8,128)(2,1)S(1)}, bf16[144,256]{1,0:T(8,128)(2,1)S(1)}, bf16[144,256]{1,0:T(8,128)(2,1)S(1)}) custom-call(s32[3]{0:T(128)S(1)} %pad_add_fusion.place_ref, bf16[128,1024]{1,0:T(8,128)(2,1)S(1)} %get-tuple-element.132.refs_0_, ...), custom_call_target="tpu_custom_call" | custom-call | flops 671088640 | bytes 1875968 | tf_op jit(solution)/shard_map/attend_backward/pallas_call | solution.py:299
  (160 shorter events, 71.2 us)
Async XLA Ops:
  3.1 20.8 %collective-permute-start = (bf16[128,1280]{1,0:T(8,128)(2,1)S(1)}, bf16[128,1280]{1,0:T(8,128)(2,1)S(1)}, u32[]{:S(2)}, u32[]{:S(2)}) collective-permute-start(bf16[128,1280]{1,0:T(8,128)(2,1)S(1)} %constant_dynamic-update-slice_fusion.refs_0_), channel_id=1, source_target_pairs={{0,4},{4,0},{8,12},{12,8},{1,5},{5,1},{9,13},{13,9},{2,6},{6,2},{1... | collective-permute-start | bytes 983048 | tf_op jit(solution)/shard_map/gather_heads/ppermute | solution.py:272
  6.2 18.2 %collective-permute-start.1 = (bf16[128,1280]{1,0:T(8,128)(2,1)S(1)}, bf16[128,1280]{1,0:T(8,128)(2,1)S(1)}, u32[]{:S(2)}, u32[]{:S(2)}) collective-permute-start(bf16[128,1280]{1,0:T(8,128)(2,1)S(1)} %constant_dynamic-update-slice_fusion.refs_0_), channel_id=1, source_target_pairs={{0,8},{4,12},{8,0},{12,4},{1,9},{5,13},{9,1},{13,5},{2,10},{6,14},... | collective-permute-start | bytes 983048 | tf_op jit(solution)/shard_map/gather_heads/ppermute | solution.py:272
  13.0 11.0 %collective-permute-start.2 = (bf16[32,512]{1,0:T(8,128)(2,1)S(1)}, bf16[32,512]{1,0:T(8,128)(2,1)S(1)}, u32[]{:S(2)}, u32[]{:S(2)}) collective-permute-start(bf16[32,512]{1,0:T(8,128)(2,1)S(1)} %get-tuple-element.82), channel_id=1, source_target_pairs={{0,12},{4,8},{8,4},{12,0},{1,13},{5,9},{9,5},{13,1},{2,14},{6,10},... | collective-permute-start | bytes 98312 | tf_op jit(solution)/shard_map/gather_heads/ppermute | solution.py:272
  37.5 11.3 %collective-permute-start.7 = (bf16[32,2688]{1,0:T(8,128)(2,1)S(1)}, bf16[32,2688]{1,0:T(8,128)(2,1)S(1)}, u32[]{:S(2)}, u32[]{:S(2)}) collective-permute-start(bf16[32,2688]{1,0:T(8,128)(2,1)S(1)} %get-tuple-element.92), channel_id=1, source_target_pairs={{0,8},{4,12},{8,0},{12,4},{1,9},{5,13},{9,1},{13,5},{2,10},{6,14},... | collective-permute-start | bytes 516104 | tf_op jit(solution)/shard_map/gather_rows/ppermute | solution.py:272
  39.7 10.0 %collective-permute-start.6 = (bf16[32,2688]{1,0:T(8,128)(2,1)S(1)}, bf16[32,2688]{1,0:T(8,128)(2,1)S(1)}, u32[]{:S(2)}, u32[]{:S(2)}) collective-permute-start(bf16[32,2688]{1,0:T(8,128)(2,1)S(1)} %get-tuple-element.86), channel_id=1, source_target_pairs={{0,4},{4,0},{8,12},{12,8},{1,5},{5,1},{9,13},{13,9},{2,6},{6,2},{1... | collective-permute-start | bytes 516104 | tf_op jit(solution)/shard_map/gather_rows/ppermute | solution.py:272
  40.1 9.7 %collective-permute-start.5 = (bf16[4,32,512]{2,1,0:T(8,128)(2,1)S(1)}, bf16[4,32,512]{2,1,0:T(8,128)(2,1)S(1)}, u32[]{:S(2)}, u32[]{:S(2)}) collective-permute-start(bf16[4,32,512]{2,1,0:T(8,128)(2,1)S(1)} %fusion.5), channel_id=1, source_target_pairs={{0,2},{1,3},{2,0},{3,1},{4,6},{5,7},{6,4},{7,5},{8,10},{9,11},{10,... | collective-permute-start | bytes 393224 | tf_op jit(solution)/shard_map/sum_heads/ppermute | solution.py:276
  50.5 15.4 %collective-permute-start.16 = (bf16[3,32,2176]{2,1,0:T(8,128)(2,1)S(1)}, bf16[3,32,2176]{2,1,0:T(8,128)(2,1)}, u32[]{:S(2)}, u32[]{:S(2)}) collective-permute-start(bf16[3,32,2176]{2,1,0:T(8,128)(2,1)S(1)} %pad_maximum_fusion.refs_0_), channel_id=1, source_target_pairs={{0,2},{1,3},{2,0},{3,1},{4,6},{5,7},{6,4},{7,5},{8,10},{9,11},{10,... | collective-permute-start | bytes 1253384 | tf_op jit(solution)/shard_map/gather_rows/ppermute | solution.py:276
  52.5 8.3 %collective-permute-start.9 = (bf16[4,32,512]{2,1,0:T(8,128)(2,1)S(1)}, bf16[4,32,512]{2,1,0:T(8,128)(2,1)}, u32[]{:S(2)}, u32[]{:S(2)}) collective-permute-start(bf16[4,32,512]{2,1,0:T(8,128)(2,1)S(1)} %hidden_rows.1.refs_0_), channel_id=1, source_target_pairs={{0,8},{4,12},{8,0},{12,4},{1,9},{5,13},{9,1},{13,5},{2,10},{6,14},... | collective-permute-start | bytes 393224 | tf_op jit(solution)/shard_map/gather_hidden/ppermute | solution.py:272
  53.7 10.7 %collective-permute-start.11 = (bf16[4,32,512]{2,1,0:T(8,128)(2,1)S(1)}, bf16[4,32,512]{2,1,0:T(8,128)(2,1)}, u32[]{:S(2)}, u32[]{:S(2)}) collective-permute-start(bf16[4,32,512]{2,1,0:T(8,128)(2,1)S(1)} %hidden_rows.1.refs_0_), channel_id=1, source_target_pairs={{0,2},{1,3},{2,0},{3,1},{4,6},{5,7},{6,4},{7,5},{8,10},{9,11},{10,... | collective-permute-start | bytes 393224 | tf_op jit(solution)/shard_map/gather_hidden/ppermute | solution.py:276
  60.8 17.4 %collective-permute-start.18 = (bf16[3,32,2176]{2,1,0:T(8,128)(2,1)S(1)}, bf16[3,32,2176]{2,1,0:T(8,128)(2,1)S(1)}, u32[]{:S(2)}, u32[]{:S(2)}) collective-permute-start(bf16[3,32,2176]{2,1,0:T(8,128)(2,1)S(1)} %pad_maximum_fusion.refs_0_), channel_id=1, source_target_pairs={{0,1},{1,0},{2,3},{3,2},{4,5},{5,4},{6,7},{7,6},{8,9},{9,8},{10,11... | collective-permute-start | bytes 1253384 | tf_op jit(solution)/shard_map/gather_rows/ppermute | solution.py:276
  65.9 12.9 %collective-permute-start.20 = (bf16[3,32,2176]{2,1,0:T(8,128)(2,1)}, bf16[3,32,2176]{2,1,0:T(8,128)(2,1)S(1)}, u32[]{:S(2)}, u32[]{:S(2)}) collective-permute-start(bf16[3,32,2176]{2,1,0:T(8,128)(2,1)} %collective-permute-done.16.refs_2_), channel_id=1, source_target_pairs={{0,1},{1,0},{2,3},{3,2},{4,5},{5,4},{6,7},{7,6},{8,9},{9,8},{10,11... | collective-permute-start | bytes 1253384 | tf_op jit(solution)/shard_map/gather_rows/ppermute | solution.py:276
  67.3 15.4 %collective-permute-start.22 = (bf16[512,512]{1,0:T(8,128)(2,1)S(1)}, bf16[512,512]{1,0:T(8,128)(2,1)S(1)}, u32[]{:S(2)}, u32[]{:S(2)}) collective-permute-start(bf16[512,512]{1,0:T(8,128)(2,1)S(1)} %constant_dynamic-slice_fusion), channel_id=1, source_target_pairs={{0,4},{4,0},{8,12},{12,8},{1,5},{5,1},{9,13},{13,9},{2,6},{6,2},{1... | collective-permute-start | bytes 1572872 | tf_op jit(solution)/shard_map/gather_proj/ppermute | solution.py:272
  84.3 14.0 %collective-permute-start.35 = (bf16[512,512]{1,0:T(8,128)(2,1)S(1)}, bf16[512,512]{1,0:T(8,128)(2,1)S(1)}, u32[]{:S(2)}, u32[]{:S(2)}) collective-permute-start(bf16[512,512]{1,0:T(8,128)(2,1)S(1)} %collective-permute-done.22.refs_5_), channel_id=1, source_target_pairs={{0,16},{16,0},{1,17},{17,1},{2,18},{18,2},{3,19},{19,3},{4,20},{20... | collective-permute-start | bytes 1572872 | tf_op jit(solution)/shard_map/gather_proj/ppermute | solution.py:837
  92.9 17.5 %collective-permute-start.32 = (bf16[4,32,1536]{2,1,0:T(8,128)(2,1)S(1)}, bf16[4,32,1536]{2,1,0:T(8,128)(2,1)S(1)}, u32[]{:S(2)}, u32[]{:S(2)}) collective-permute-start(bf16[4,32,1536]{2,1,0:T(8,128)(2,1)S(1)} %get-tuple-element.105), channel_id=1, source_target_pairs={{0,1},{1,0},{2,3},{3,2},{4,5},{5,4},{6,7},{7,6},{8,9},{9,8},{10,11... | collective-permute-start | bytes 1179656 | tf_op jit(solution)/shard_map/sum_row_grads/ppermute | solution.py:276
  95.0 15.6 %collective-permute-start.31 = (bf16[2,4,32,2048]{3,2,1,0:T(8,128)(2,1)S(1)}, bf16[2,4,32,2048]{3,2,1,0:T(8,128)(2,1)S(1)}, u32[]{:S(2)}, u32[]{:S(2)}) collective-permute-start(bf16[2,4,32,2048]{3,2,1,0:T(8,128)(2,1)S(1)} %get-tuple-element.103), channel_id=1, source_target_pairs={{0,1},{1,0},{2,3},{3,2},{4,5},{5,4},{6,7},{7,6},{8,9},{9,8},{10,11... | collective-permute-start | bytes 3145736 | tf_op jit(solution)/shard_map/sum_outputs/ppermute | solution.py:276
  98.4 12.0 %collective-permute-start.36 = (bf16[4,32,1536]{2,1,0:T(8,128)(2,1)S(1)}, bf16[4,32,1536]{2,1,0:T(8,128)(2,1)S(1)}, u32[]{:S(2)}, u32[]{:S(2)}) collective-permute-start(bf16[4,32,1536]{2,1,0:T(8,128)(2,1)S(1)} %add_convert_fusion.1), channel_id=1, source_target_pairs={{0,2},{1,3},{2,0},{3,1},{4,6},{5,7},{6,4},{7,5},{8,10},{9,11},{10,... | collective-permute-start | bytes 1179656 | tf_op jit(solution)/shard_map/sum_row_grads/ppermute | solution.py:276
  110.7 11.1 %collective-permute-start.40 = (bf16[4,32,2048]{2,1,0:T(8,128)(2,1)S(1)}, bf16[4,32,2048]{2,1,0:T(8,128)(2,1)S(1)}, u32[]{:S(2)}, u32[]{:S(2)}) collective-permute-start(bf16[4,32,2048]{2,1,0:T(8,128)(2,1)S(1)} %fusion), channel_id=1, source_target_pairs={{0,2},{1,3},{2,0},{3,1},{4,6},{5,7},{6,4},{7,5},{8,10},{9,11},{10,... | collective-permute-start | bytes 1572872 | tf_op jit(solution)/shard_map/sum_outputs/ppermute | solution.py:276
  111.6 10.6 %collective-permute-start.44 = (bf16[32,512]{1,0:T(8,128)(2,1)S(1)}, bf16[32,512]{1,0:T(8,128)(2,1)S(1)}, u32[]{:S(2)}, u32[]{:S(2)}) collective-permute-start(bf16[32,512]{1,0:T(8,128)(2,1)S(1)} %get-tuple-element.161), channel_id=1, source_target_pairs={{0,2},{1,3},{2,0},{3,1},{4,6},{5,7},{6,4},{7,5},{8,10},{9,11},{10,... | collective-permute-start | bytes 98312 | tf_op jit(solution)/shard_map/sum_row_grads/ppermute | solution.py:276
  112.8 9.4 %collective-permute-start.43 = (bf16[32,1536]{1,0:T(8,128)(2,1)S(1)}, bf16[32,1536]{1,0:T(8,128)(2,1)S(1)}, u32[]{:S(2)}, u32[]{:S(2)}) collective-permute-start(bf16[32,1536]{1,0:T(8,128)(2,1)S(1)} %get-tuple-element.116), channel_id=1, source_target_pairs={{0,12},{4,8},{8,4},{12,0},{1,13},{5,9},{9,5},{13,1},{2,14},{6,10},... | collective-permute-start | bytes 294920 | tf_op jit(solution)/shard_map/sum_row_grads/ppermute | solution.py:272
  132.6 15.5 %collective-permute-start.46 = (bf16[32,2048]{1,0:T(8,128)(2,1)S(1)}, bf16[32,2048]{1,0:T(8,128)(2,1)S(1)}, u32[]{:S(2)}, u32[]{:S(2)}) collective-permute-start(bf16[32,2048]{1,0:T(8,128)(2,1)S(1)} %get-tuple-element.124), channel_id=1, source_target_pairs={{0,4},{4,0},{8,12},{12,8},{1,5},{5,1},{9,13},{13,9},{2,6},{6,2},{1... | collective-permute-start | bytes 393224 | tf_op jit(solution)/shard_map/sum_outputs/ppermute | solution.py:272
  136.4 11.8 %collective-permute-start.48 = (bf16[32,2048]{1,0:T(8,128)(2,1)S(1)}, bf16[32,2048]{1,0:T(8,128)(2,1)S(1)}, u32[]{:S(2)}, u32[]{:S(2)}) collective-permute-start(bf16[32,2048]{1,0:T(8,128)(2,1)S(1)} %add_convert_fusion.2), channel_id=1, source_target_pairs={{0,8},{4,12},{8,0},{12,4},{1,9},{5,13},{9,1},{13,5},{2,10},{6,14},... | collective-permute-start | bytes 393224 | tf_op jit(solution)/shard_map/sum_outputs/ppermute | solution.py:272
  139.0 26.7 %collective-permute-start.56 = (bf16[256,512]{1,0:T(8,128)(2,1)S(1)}, bf16[256,512]{1,0:T(8,128)(2,1)S(1)}, u32[]{:S(2)}, u32[]{:S(2)}) collective-permute-start(bf16[256,512]{1,0:T(8,128)(2,1)S(1)} %get-tuple-element.148), channel_id=1, source_target_pairs={{0,4},{4,0},{8,12},{12,8},{1,5},{5,1},{9,13},{13,9},{2,6},{6,2},{1... | collective-permute-start | bytes 786440 | tf_op jit(solution)/shard_map/gather_cuts/ppermute | solution.py:272
  141.5 15.3 %collective-permute-start.52 = (bf16[128,1024]{1,0:T(8,128)(2,1)S(1)}, bf16[128,1024]{1,0:T(8,128)(2,1)S(1)}, u32[]{:S(2)}, u32[]{:S(2)}) collective-permute-start(bf16[128,1024]{1,0:T(8,128)(2,1)S(1)} %get-tuple-element.133), channel_id=1, source_target_pairs={{0,8},{4,12},{8,0},{12,4},{1,9},{5,13},{9,1},{13,5},{2,10},{6,14},... | collective-permute-start | bytes 786440 | tf_op jit(solution)/shard_map/sum_mix_grad/ppermute | solution.py:272
  160.1 8.7 %collective-permute-start.54 = (bf16[144,256]{1,0:T(8,128)(2,1)S(1)}, bf16[144,256]{1,0:T(8,128)(2,1)S(1)}, u32[]{:S(2)}, u32[]{:S(2)}) collective-permute-start(bf16[144,256]{1,0:T(8,128)(2,1)S(1)} %get-tuple-element.142), channel_id=1, source_target_pairs={{0,8},{4,12},{8,0},{12,4},{1,9},{5,13},{9,1},{13,5},{2,10},{6,14},... | collective-permute-start | bytes 221192 | tf_op jit(solution)/shard_map/sum_pairs/ppermute | solution.py:272
  (50 other events, 433.2 us)
